TPU v7x, 512 devices: a whole 4x4x16 slice. The times are simulated.
512 devices in a mesh: outer: 32 (over z_lo, x), inner: 16 (over y, z_hi, core).
Axes of the slice: x: 4, y: 4, z: 16 (z_hi: 2, z_lo: 8; z = z_hi * 8 + z_lo), core: 2. Of those that a mesh axis runs over, the one named last changes fastest.
Arguments:
- queries: bfloat16 [131072, 768], P(('outer', 'inner')), may hold values from -18 to 18
- keys: bfloat16 [131072, 768], P(('outer', 'inner')), may hold values from -6 to 6
- values: bfloat16 [131072, 768], P(('outer', 'inner')), may hold values from -6 to 6
Outputs:
- attended: bfloat16 [131072, 768], P(('outer', 'inner'))
All inputs are finite; a program needn't handle non-finite values.
Results may differ from a plain program's by a relative error of at most 0.0065.
Values may be sent and summed in bfloat16 or wider, within the bound.
No kernel may reach another device: no remote copies, remote signals or barrier semaphores. Data moves between devices by JAX's collectives and lax.ppermute only.
A program may use at most 128 MiB of HBM per device.

v0:
```python
import jax
import jax.numpy as jnp
import numpy as np
from jax import lax
from jax.sharding import PartitionSpec as P

HEADS = 12
HEAD_DIM = 64
R3 = 128


def select(rows, dilation):
    count = rows.shape[0]
    shaped = rows.reshape(count // dilation, dilation, HEADS, HEAD_DIM)
    return shaped[:, np.arange(HEADS) % dilation, np.arange(HEADS), :]


def attend_one(operands):
    query_rows, key_rows, value_rows = operands
    scores = jnp.einsum(
        "nd,md->nm", query_rows, key_rows, preferred_element_type=jnp.float32
    ) * HEAD_DIM ** (-0.5)
    peak = jnp.max(scores, axis=-1)
    expos = jnp.exp(scores - peak[:, None])
    total = jnp.sum(expos, axis=-1)
    weight = expos.astype(jnp.bfloat16)
    partial_value = jnp.einsum("nm,md->nd", weight, value_rows, preferred_element_type=jnp.float32)
    return jnp.concatenate([partial_value, peak[:, None], total[:, None]], axis=-1)


def heads_first(flat_rows):
    return flat_rows.reshape(-1, HEADS, HEAD_DIM).transpose(1, 0, 2)


def combine(first, second):
    peak = jnp.maximum(first[0], second[0])
    scale_one = jnp.exp(first[0] - peak)
    scale_two = jnp.exp(second[0] - peak)
    return (
        peak,
        first[1] * scale_one + second[1] * scale_two,
        first[2] * scale_one[..., None] + second[2] * scale_two[..., None],
    )


def unpack(packed):
    return (packed[..., HEAD_DIM], packed[..., HEAD_DIM + 1], packed[..., :HEAD_DIM])


def combine_packed(first, second):
    peak, total, partial_value = combine(unpack(first), unpack(second))
    return jnp.concatenate([partial_value, peak[..., None], total[..., None]], axis=-1)


def empty_packed(head_count, row_count):
    blank = jnp.zeros((head_count, row_count, HEAD_DIM + 2), jnp.float32)
    return blank.at[..., HEAD_DIM].set(-1e30)


def merge_into(state, level, dilation):
    peak, total, partial_value = state
    count = peak.shape[1]
    heads = np.arange(HEADS)
    offsets = heads % dilation
    peak_view = peak.reshape(HEADS, count // dilation, dilation)
    total_view = total.reshape(HEADS, count // dilation, dilation)
    sum_view = partial_value.reshape(HEADS, count // dilation, dilation, HEAD_DIM)
    merged = combine(
        (peak_view[heads, :, offsets], total_view[heads, :, offsets], sum_view[heads, :, offsets]),
        level,
    )
    peak_view = peak_view.at[heads, :, offsets].set(merged[0])
    total_view = total_view.at[heads, :, offsets].set(merged[1])
    sum_view = sum_view.at[heads, :, offsets].set(merged[2])
    return (
        peak_view.reshape(HEADS, count),
        total_view.reshape(HEADS, count),
        sum_view.reshape(HEADS, count, HEAD_DIM),
    )


def body(queries, keys, values):
    rows = queries.shape[0]
    width = queries.shape[1]
    query_heads = queries.reshape(rows, HEADS, HEAD_DIM)
    key_heads = keys.reshape(rows, HEADS, HEAD_DIM)
    value_heads = values.reshape(rows, HEADS, HEAD_DIM)
    query_split = query_heads.transpose(1, 0, 2)
    joined = jnp.concatenate([keys, values], axis=1)
    piece = lax.all_gather(joined, "inner", axis=0, tiled=True)
    level = lax.map(
        attend_one, (query_split, heads_first(piece[:, :width]), heads_first(piece[:, width:]))
    )
    packed_state = combine_packed(empty_packed(HEADS, rows), level)
    state = unpack(packed_state)
    far_queries = select(query_heads, R3)
    far_count = far_queries.shape[0]
    far_split = far_queries.transpose(1, 0, 2)
    far_keys = select(key_heads, R3)
    far_values = select(value_heads, R3)
    far_joined = jnp.concatenate(
        [far_keys.reshape(-1, width), far_values.reshape(-1, width)], axis=1
    )
    piece = lax.all_gather(far_joined, ("outer", "inner"), axis=0, tiled=True)
    level = lax.map(
        attend_one, (far_split, heads_first(piece[:, :width]), heads_first(piece[:, width:]))
    )
    far_level = unpack(combine_packed(empty_packed(HEADS, far_count), level))
    state = merge_into(state, far_level, R3)
    result = state[2] / state[1][..., None]
    return result.transpose(1, 0, 2).reshape(rows, width).astype(jnp.bfloat16)


def solution(mesh):
    placed = (P(("outer", "inner"), None), P(("outer", "inner"), None), P(("outer", "inner"), None))
    return jax.shard_map(
        body, mesh=mesh, in_specs=placed, out_specs=P(("outer", "inner"), None), check_vma=False
    )
```

profile of v0, /device:TPU:1, one launch (start us, length us, event | category | flops | bytes accessed | tf_op | source)
XLA Modules:
  0.0 1144.2 jit_solution(16980712259637243460)
XLA Ops:
  6.5 1.2 copy.191
  7.8 1.2 copy.192
  15.5 802.6 %all-gather.6.cloned.1.call-done = bf16[512,2,1536]{2,1,0:T(2,128)(2,1)} async-done(((bf16[1,2,1536]{2,1,0:T(2,128)(2,1)}), bf16[512,2,1536]{2,1,0:T(2,128)(2,1)}) %all-gather.6.cloned.1.call-update) | async-done | bytes 3145744 | tf_op jit(solution)/shard_map/all_gather | solution.py:104
  818.2 6.3 reshape.153
  824.5 1.8 fusion.55
  826.3 1.8 copy.207
  828.2 1.6 copy.208
  829.9 28.8 %while.23 = (s32[]{:T(128)}, f32[12,2,66]{2,1,0:T(2,128)}, bf16[12,2,64]{2,1,0:T(2,128)(2,1)S(1)}, bf16[12,1024,64]{1,2,0:T(8,128)(2,1)S(1)}, bf16[12,1024,64]{1,2,0:T(8,128)(2,1)}, /*index=5*/s32[]{:T(128)}) while((s32[]{:T(128)}, f32[12,2,66]{2,1,0:T(2,128)}, bf16[12,2,64]{2,1,0:T(2,128)(2,1)S(1)}, bf16[12,1024,64]{1,2,0:T(8,128)(2,1)S(1)}, ...), condition=%wide.region_7.8_spmd, body=%wide.region_4.7_spmd.sunk | while | flops 536838 | bytes 291477 | solution.py:105
  830.1 1.1 fusion.78
  832.5 1.1 fusion.78
  834.9 1.1 fusion.78
  837.3 1.1 fusion.78
  839.7 1.1 fusion.78
  842.1 1.1 fusion.78
  844.5 1.1 fusion.78
  846.9 1.1 fusion.78
  849.3 1.1 fusion.78
  851.7 1.1 fusion.78
  854.1 1.1 fusion.78
  856.5 1.1 fusion.78
  860.3 202.9 %all-gather.4.cloned.1.call-done = bf16[4096,1536]{0,1:T(8,128)(2,1)} async-done(((bf16[256,1536]{0,1:T(8,128)(2,1)}), bf16[4096,1536]{0,1:T(8,128)(2,1)}) %all-gather.4.cloned.1.call-update) | async-done | bytes 12582928 | tf_op jit(solution)/shard_map/all_gather | solution.py:90
  1063.2 10.4 fusion.54
  1073.6 53.9 %while.22 = (s32[]{:T(128)}, f32[12,256,66]{1,2,0:T(8,128)S(1)}, bf16[12,256,64]{1,2,0:T(8,128)(2,1)S(1)}, bf16[12,4096,64]{1,2,0:T(8,128)(2,1)}, bf16[12,4096,64]{1,2,0:T(8,128)(2,1)}, /*index=5*/s32[]{:T(128)}) while((s32[]{:T(128)}, f32[12,256,66]{1,2,0:T(8,128)S(1)}, bf16[12,256,64]{1,2,0:T(8,128)(2,1)S(1)}, ...), condition=%wide.region_3.4_spmd, body=%wide.region_0.3_spmd.sunk | while | flops 274760192 | bytes 13876809 | solution.py:91
  1073.6 1.9 fusion.70
  1075.5 1.9 fusion.72
  1078.1 1.9 fusion.70
  1080.0 1.9 fusion.72
  1082.6 1.9 fusion.70
  1084.5 1.9 fusion.72
  1087.1 1.9 fusion.70
  1089.0 1.9 fusion.72
  1091.6 1.9 fusion.70
  1093.5 1.9 fusion.72
  1096.1 1.9 fusion.70
  1098.0 1.9 fusion.72
  1100.6 1.9 fusion.70
  1102.5 1.9 fusion.72
  1105.1 1.9 fusion.70
  1107.0 1.9 fusion.72
  1109.6 1.9 fusion.70
  1111.5 1.9 fusion.72
  1114.1 1.9 fusion.70
  1116.0 1.9 fusion.72
  1118.6 1.9 fusion.70
  1120.5 1.9 fusion.72
  1123.1 1.9 fusion.70
  1125.0 1.9 fusion.72
  1129.9 1.1 scatter_fusion.1
  (149 shorter events, 40.9 us)
Async XLA Ops:
  6.5 7.3 copy-start.2
  6.5 811.6 %all-gather.6.cloned.1.call-start = ((), (), s32[]{:S(2)}) async-start(), calls=%async_computation.1 | async-start | bytes 3151872 | tf_op jit(solution)/shard_map/all_gather | solution.py:104
  12.8 1050.5 %all-gather.4.cloned.1.call-start = ((), (), s32[]{:S(2)}) async-start(), calls=%async_computation | async-start | bytes 13369344 | tf_op jit(solution)/shard_map/all_gather | solution.py:90
  826.3 1.9 copy-start
  860.3 213.3 %copy-start.1 = (f32[12,256,66]{1,2,0:T(8,128)S(1)}, f32[12,256,66]{1,2,0:T(8,128)}, u32[]{:S(2)}) copy-start(f32[12,256,66]{1,2,0:T(8,128)} %custom-call.16) | copy-start | bytes 2433028
  1127.7 6.1 copy-start.3
Sparse Core Ops, SparseCore 0:
  12.9 805.2 all-gather.5
  821.3 241.8 all-gather.3
where the time goes:
time: 1150 us; the launch traced here: 1140 us
  waiting for transfers between devices  1010 us (88%)
  matrix products  61.2 us (5%)
  local copies, waits for them, and re-layouts  42.5 us (4%)
  other arithmetic  20.9 us (2%)
  between operations  13.7 us (1%)
    all_gather x1, waiting for transfers between devices, body(): piece = lax.all_gather(far_joined, ('outer', 'inner'), axis=0, tiled=True)  803 us
    all_gather x1, waiting for transfers between devices, body(): piece = lax.all_gather(joined, 'inner', axis=0, tiled=True)  203 us
    dot_general x24, matrix products, attend_one(): jnp.einsum('nm,md->nd', weight, value_rows, preferred_element_type=jnp.fl...  35.9 us
    dot_general x24, matrix products, attend_one(): jnp.einsum('nd,md->nm', query_rows, key_rows, preferred_element_type=jnp....  25.3 us
  transfers between devices with their start and end apart: 2, of which 2 were waited for; matrix products, arithmetic and copies ran while one was open for 4% of the time, Pallas kernels for 0%

commit v1 on v0

v1 whole, which is shorter than its diff:
```python
import functools

import jax
import jax.numpy as jnp
from jax import lax
from jax.experimental import pallas as pl
from jax.experimental.pallas import tpu as pltpu
from jax.sharding import Mesh
from jax.sharding import PartitionSpec as P

HEADS = 12
HEAD_DIM = 64
R3 = 128
OWN = 3
SPAN = OWN * HEAD_DIM
AXES = ("zl", "x", "y", "zh", "core")
SIZES = (8, 4, 4, 2, 2)
FACTOR = HEAD_DIM ** (-0.5) * 1.4426950408889634
BLANK = -1e30
F32 = jnp.float32
BF16 = jnp.bfloat16

KV = 768
QROWS = 384
PIECE = 1168


def route(dx=0, dy=0, dz=0, flip=0, by_core=False):
    pairs = []
    for src in range(512):
        rest, core = divmod(src, 2)
        rest, zh = divmod(rest, 2)
        rest, y = divmod(rest, 4)
        zl, x = divmod(rest, 4)
        sign = -1 if by_core and core else 1
        z = (zh * 8 + zl + sign * dz) % 16
        dst = ((((z % 8) * 4 + (x + dx) % 4) * 4 + (y + dy) % 4) * 2 + z // 8) * 2 + (core ^ flip)
        pairs.append((src, dst))
    return pairs


def move(array, **step):
    return lax.ppermute(array, AXES, route(**step))


def hop(array):
    return move(array, dz=4, by_core=True)


SMEM = pl.BlockSpec(memory_space=pltpu.SMEM)


def shape(*dims, dtype=BF16):
    return jax.ShapeDtypeStruct(dims, dtype)


def whole(*dims):
    return pl.BlockSpec(dims, lambda i: (0,) * len(dims))


def params():
    return pltpu.CompilerParams(vmem_limit_bytes=48 * 2**20)


def prep_kernel(
    y_ref, q_hbm, k_hbm, v_hbm, own_kv, staged, q_ref, k_ref, v_ref, sems
):
    copies = [
        pltpu.make_async_copy(source, target, sems.at[i])
        for i, (source, target) in enumerate(((k_hbm, k_ref), (v_hbm, v_ref), (q_hbm, q_ref)))
    ]
    for copy in copies:
        copy.start()
    y = y_ref[0]
    for copy in copies:
        copy.wait()
    keys = k_ref[...]
    keys32 = keys.astype(F32)
    values = v_ref[...].astype(F32)
    values_t = values.T.astype(BF16)
    queries_t = q_ref[...].astype(F32).T.astype(BF16)
    row = lax.broadcasted_iota(jnp.int32, (16, 768), 0)
    chosen = row == lax.broadcasted_iota(jnp.int32, (16, 768), 1) // HEAD_DIM
    picked = [
        jnp.sum(jnp.where(chosen, source[j * R3 : j * R3 + 16], 0.0), axis=0, keepdims=True)
        for source in (keys32, values)
        for j in range(2)
    ]
    for group in range(4):
        lo = group * SPAN
        part = keys32[:, lo : lo + SPAN]
        staged[group, 0:256, :] = part[:, 0:128].astype(BF16)
        staged[group, 256:384, :] = jnp.concatenate(
            [part[0:128, 128:192], part[128:256, 128:192]], axis=1
        ).astype(BF16)
        staged[group, 384:576, :] = values_t[lo : lo + SPAN, 0:128]
        staged[group, 576:768, :] = values_t[lo : lo + SPAN, 128:256]
        staged[group, 768:960, :] = queries_t[lo : lo + SPAN, 0:128]
        staged[group, 960:1152, :] = queries_t[lo : lo + SPAN, 128:256]
        far_rows = []
        for first, second in (picked[0:2], picked[2:4]):
            first, second = first[:, lo : lo + SPAN], second[:, lo : lo + SPAN]
            far_rows += [
                first[:, 0:128],
                second[:, 0:128],
                jnp.concatenate([first[:, 128:192], second[:, 128:192]], axis=1),
            ]
        far_rows.append(jnp.zeros((10, 128), F32))
        staged[group, 1152:1168, :] = jnp.concatenate(far_rows, axis=0).astype(BF16)
    own_kv[...] = staged[y, 0:KV, :]


def prep(y, queries, keys, values):
    return pl.pallas_call(
        prep_kernel,
        grid=(1,),
        out_shape=[shape(KV, 128), shape(4, PIECE, 128)],
        in_specs=[SMEM] + [pl.BlockSpec(memory_space=pltpu.HBM)] * 3,
        out_specs=[whole(KV, 128), whole(4, PIECE, 128)],
        scratch_shapes=[pltpu.VMEM((256, 768), BF16)] * 3 + [pltpu.SemaphoreType.DMA((3,))],
        compiler_params=params(),
        name="prep",
    )(y, queries, keys, values)


def sort_kernel(y_ref, got, all_kv, away_kv, q_out, far_out):
    y = y_ref[0]
    far_rows = []
    for i in range(4):
        all_kv[i * KV : (i + 1) * KV, :] = got[i, 0:KV, :]
        if i:
            away_kv[(i - 1) * KV : i * KV, :] = got[lax.rem(y + i, 4), 0:KV, :]
        q_out[i] = jnp.concatenate(
            [got[i, KV : KV + SPAN, :], got[i, KV + SPAN : KV + QROWS, :]], axis=1
        )
        far_rows.append(got[i, KV + QROWS : PIECE, :].astype(F32))
    blank = jnp.zeros((4, 128), F32)
    packed = []
    for base in (0, 3):
        packed += [rows[base : base + 2] for rows in far_rows]
        packed += [rows[base + 2 : base + 3] for rows in far_rows]
        packed.append(blank)
    packed = jnp.concatenate(packed, axis=0).astype(BF16)
    for i in range(16):
        far_out[i] = packed


def sort(y, got):
    shapes = [(4 * KV, 128), (3 * KV, 128), (4, SPAN, 256), (16, 32, 128)]
    return pl.pallas_call(
        sort_kernel,
        grid=(1,),
        out_shape=[shape(*dims) for dims in shapes],
        in_specs=[SMEM, whole(4, PIECE, 128)],
        out_specs=[whole(*dims) for dims in shapes],
        compiler_params=params(),
        name="sort",
    )(y, got)


def attend(blocks, queries, head, scores, first_peak):
    mine = queries[head * HEAD_DIM : (head + 1) * HEAD_DIM]
    blank = jnp.zeros_like(mine)
    low = jnp.concatenate([mine, blank], axis=0)
    high = jnp.concatenate([blank, mine], axis=0)
    top = None
    for i, (ref, base) in enumerate(blocks):
        if head < 2:
            parts = [(ref[base : base + 256, :], high if head else low)]
        else:
            third = ref[base + 256 : base + 384, :]
            parts = [(third, low), (third, high)]
        at = i * 256
        for rows, side in parts:
            s = jnp.dot(rows, side, preferred_element_type=F32)
            count = s.shape[0]
            scores[at : at + count, :] = s
            at += count
            here = jnp.max(s.reshape(count // 8, 8, 512), axis=0)
            top = here if top is None else jnp.maximum(top, here)
    peak = jnp.max(top, axis=0, keepdims=True)
    if first_peak is not None:
        peak = jnp.maximum(peak, first_peak)
    total = jnp.zeros((8, 512), F32)
    partial_value = jnp.zeros((HEAD_DIM, 512), F32)
    lo = head * HEAD_DIM
    for i, (ref, base) in enumerate(blocks):
        expos = jnp.exp2((scores[i * 256 : (i + 1) * 256, :] - peak) * FACTOR)
        total = total + jnp.sum(expos.reshape(32, 8, 512), axis=0)
        values = jnp.concatenate(
            [
                ref[base + 384 + lo : base + 384 + lo + HEAD_DIM, :],
                ref[base + 576 + lo : base + 576 + lo + HEAD_DIM, :],
            ],
            axis=1,
        )
        partial_value = partial_value + jnp.dot(
            values, expos.astype(BF16), preferred_element_type=F32
        )
    return peak, jnp.sum(total, axis=0, keepdims=True), partial_value


def near_kernel(counts, has_state, is_last, q_ref, *refs):
    refs = list(refs)
    blocks = []
    for count in counts:
        ref = refs.pop(0)
        blocks += [(ref, i * KV) for i in range(count)]
    if has_state:
        old_sum, old_stat = refs.pop(0), refs.pop(0)
    if is_last:
        far_sum, far_stat = refs.pop(0), refs.pop(0)
        out, scores = refs
    else:
        sum_out, stat_out, scores = refs
    queries = jnp.concatenate([q_ref[0], q_ref[1]], axis=1)
    peaks, totals = [], []
    for head in range(OWN):
        rows = slice(head * HEAD_DIM, (head + 1) * HEAD_DIM)
        first_peak = None
        if has_state:
            old_peak = old_stat[head : head + 1, :]
            old_total = old_stat[4 + head : 5 + head, :]
            first_peak = old_peak
        if is_last:
            far_peak = far_stat[head : head + 1, :]
            far_total = far_stat[8 + head : 9 + head, :]
            first_peak = jnp.maximum(old_peak, far_peak)
        peak, total, partial_value = attend(blocks, queries, head, scores.at[head], first_peak)
        if has_state:
            scale = jnp.exp2((old_peak - peak) * FACTOR)
            total = total + old_total * scale
            partial_value = partial_value + old_sum[rows, :] * scale
        if is_last:
            scale = jnp.exp2((far_peak - peak) * FACTOR)
            total = total + far_total * scale
            partial_value = partial_value + far_sum[rows, :] * scale
            result = (partial_value / total).astype(BF16)
            out[0, rows, :] = result[:, 0:256]
            out[1, rows, :] = result[:, 256:512]
        else:
            sum_out[rows, :] = partial_value
            peaks.append(peak)
            totals.append(total)
    if not is_last:
        blank = [jnp.zeros((1, 512), F32)]
        stat_out[...] = jnp.concatenate(peaks + blank + totals + blank, axis=0)


def near(queries, arrays, state=None, far_state=None):
    def along(rows):
        return pl.BlockSpec((rows, 512), lambda i: (0, i))

    counts = tuple(a.shape[0] // KV for a in arrays)
    is_last = far_state is not None
    two = pl.BlockSpec((2, SPAN, 256), lambda i: (i, 0, 0))
    operands = [queries, *arrays]
    in_specs = [two] + [whole(*a.shape) for a in arrays]
    if state is not None:
        operands += state
        in_specs += [along(SPAN), along(8)]
    if is_last:
        operands += far_state
        in_specs += [along(SPAN), along(16)]
        out_shape, out_specs = shape(4, SPAN, 256), two
    else:
        out_shape = [shape(SPAN, 1024, dtype=F32), shape(8, 1024, dtype=F32)]
        out_specs = [along(SPAN), along(8)]
    return pl.pallas_call(
        functools.partial(near_kernel, counts, state is not None, is_last),
        grid=(2,),
        out_shape=out_shape,
        in_specs=in_specs,
        out_specs=out_specs,
        scratch_shapes=[pltpu.VMEM((OWN, sum(counts) * 256, 512), F32)],
        compiler_params=params(),
        name="last" if is_last else "near",
    )(*operands)


def far_kernel(y_ref, q_ref, rows_ref, sum_out, stat_out):
    y = y_ref[0]
    place_r = lax.broadcasted_iota(jnp.int32, (1024, 128), 1)
    place = ((place_r // 2) % 4) * 256 + (place_r % 2) * 128 + y * OWN + place_r // 8
    lane = lax.broadcasted_iota(jnp.int32, (1024, 128), 0)
    pick = jnp.where((place_r < 24) & (lane == place), 1.0, 0.0)
    chosen = jnp.zeros((SPAN, 128), F32)
    for t in range(4):
        chosen = chosen + jnp.dot(
            q_ref[t], pick[t * 256 : (t + 1) * 256].astype(BF16), preferred_element_type=F32
        )
    row_head = lax.broadcasted_iota(jnp.int32, (SPAN, 128), 0) // HEAD_DIM
    r_head = lax.broadcasted_iota(jnp.int32, (SPAN, 128), 1) // 8
    mine = row_head == r_head
    chosen = jnp.where(mine, chosen, 0.0).astype(BF16)
    third = chosen[128:192]
    blank = jnp.zeros_like(third)

    gathered = rows_ref[...].astype(F32).reshape(128, 4, 8, 128)

    def section(i):
        return gathered[:, i].reshape(1024, 128)

    keys_a, keys_b = section(0).astype(BF16), section(1).astype(BF16)
    values_a = section(2).T.astype(BF16)
    values_b = section(3).T.astype(BF16)
    r = lax.broadcasted_iota(jnp.int32, (1024, 128), 1)
    key_row = lax.broadcasted_iota(jnp.int32, (1024, 128), 0)
    there_a = r < 16
    there_b = (r >= 16) & (key_row % 8 < 4)
    scores = [
        jnp.where(there, jnp.dot(rows, side, preferred_element_type=F32), BLANK)
        for rows, side, there in (
            (keys_a, chosen[0:128], there_a),
            (keys_b, jnp.concatenate([third, blank], axis=0), there_b),
            (keys_b, jnp.concatenate([blank, third], axis=0), there_b),
        )
    ]
    peak = functools.reduce(
        jnp.maximum, [jnp.max(s, axis=0, keepdims=True) for s in scores]
    )
    total = jnp.zeros((1, 128), F32)
    sums = []
    for s, values, there in zip(
        scores,
        (values_a, values_b[0:64], values_b[64:128]),
        (there_a, there_b, there_b),
    ):
        expos = jnp.where(there, jnp.exp2((s - peak) * FACTOR), 0.0)
        total = total + jnp.sum(expos, axis=0, keepdims=True)
        sums.append(jnp.dot(values, expos.astype(BF16), preferred_element_type=F32))
    partial_value = jnp.concatenate([sums[0], sums[1] + sums[2]], axis=0)
    partial_value = jnp.where(mine, partial_value, 0.0)
    head = lax.broadcasted_iota(jnp.int32, (8, 128), 0)
    r8 = lax.broadcasted_iota(jnp.int32, (8, 128), 1)
    same = (r8 // 8 == head) & (r8 < 24)
    wide = jnp.concatenate(
        [
            partial_value,
            jnp.where(same, peak, 0.0),
            jnp.where(same, total, 0.0),
            jnp.where(same, 1.0, 0.0),
        ],
        axis=0,
    )
    dense = lax.dot_general(
        wide,
        pick,
        (((1,), (1,)), ((), ())),
        precision=lax.Precision.HIGHEST,
        preferred_element_type=F32,
    )
    sum_out[...] = dense[0:SPAN]
    there = dense[SPAN + 16 : SPAN + 24] > 0.5
    stat_out[0:8, :] = jnp.where(there, dense[SPAN : SPAN + 8], BLANK)
    stat_out[8:16, :] = dense[SPAN + 8 : SPAN + 16]


def far(y, queries, rows):
    return pl.pallas_call(
        far_kernel,
        grid=(1,),
        out_shape=[shape(SPAN, 1024, dtype=F32), shape(16, 1024, dtype=F32)],
        in_specs=[SMEM, whole(4, SPAN, 256), whole(4096, 128)],
        out_specs=[whole(SPAN, 1024), whole(16, 1024)],
        compiler_params=params(),
        name="far",
    )(y, queries, rows)


def turn_kernel(in_ref, out_ref):
    out_ref[...] = in_ref[...].astype(F32).T.astype(BF16)


def turn(array):
    return pl.pallas_call(
        turn_kernel,
        grid=(1,),
        out_shape=shape(256, 768),
        in_specs=[whole(768, 256)],
        out_specs=whole(256, 768),
        compiler_params=params(),
        name="turn",
    )(array)


def body(queries, keys, values):
    y = lax.axis_index("y").astype(jnp.int32).reshape(1)
    own_kv, staged = prep(y, queries, keys, values)

    crossed_own = move(own_kv, dz=8)
    got = lax.all_to_all(staged, "y", 0, 0, tiled=True)
    crossed_own, got = lax.optimization_barrier((crossed_own, got))
    all_kv, away_kv, q, far_rows = sort(y, got)
    crossed_away = move(away_kv, dz=8)
    partner_kv = move(all_kv, flip=1)
    partner_own = move(crossed_own, flip=1)
    state = near(q, [all_kv])
    far_rows = lax.all_to_all(far_rows, ("zl", "zh"), 0, 0, tiled=True).reshape(512, 128)
    state, far_rows, partner_kv, partner_own = lax.optimization_barrier((state, far_rows, partner_kv, partner_own))
    state = near(q, [partner_kv], state)
    far_rows, *state = lax.optimization_barrier((far_rows, *state))
    far_rows = lax.all_to_all(
        jnp.broadcast_to(far_rows, (8, 512, 128)), ("x", "core"), 0, 0, tiled=True
    ).reshape(4096, 128)
    state, far_rows = lax.optimization_barrier((state, far_rows))
    state = near(q, [crossed_own, partner_own], state)
    far_state = far(y, q, far_rows)
    crossed_away, state, far_state = lax.optimization_barrier((crossed_away, state, far_state))
    partner_away = move(crossed_away, flip=1)
    state = near(q, [crossed_away], state)
    result = near(q, [partner_away], state, far_state)
    back = lax.all_to_all(result, "y", 0, 0, tiled=True)
    return turn(back.reshape(HEADS * HEAD_DIM, 256))


def solution(mesh):
    fine = Mesh(mesh.devices.reshape(SIZES), AXES)
    placed = P(AXES, None)
    return jax.shard_map(
        body, mesh=fine, in_specs=(placed,) * 3, out_specs=placed, check_vma=False
    )
```

time: 1150 us -> 165 us (0.14)
  the two profiles are of different devices: /device:TPU:1 before, /device:TPU:162 now
where the time goes in v1:
time: 165 us; the launch traced here: 164 us
  waiting for transfers between devices  68.5 us (42%)
  starting transfers between devices  49.9 us (30%)
  Pallas kernels  28.4 us (17%)
  blocking collectives  13 us (8%)
  local copies, waits for them, and re-layouts  4.13 us (3%)
    ppermute x5, waiting for transfers between devices, move(): return lax.ppermute(array, AXES, route(**step))  58.7 us
    ppermute x5, starting transfers between devices, move(): return lax.ppermute(array, AXES, route(**step))  24.4 us
    pallas_call x5, Pallas kernels, near(): pl.pallas_call(functools.partial(near_kernel, counts, state is not None,...  22.3 us
    all_to_all x1, starting transfers between devices, body(): lax.all_to_all(far_rows, ('zl', 'zh'), 0, 0, tiled=True).reshape(512, 128)  16.3 us
    all_to_all x1, blocking collectives, body(): back = lax.all_to_all(result, 'y', 0, 0, tiled=True)  13 us
    all_to_all x1, waiting for transfers between devices, body(): lax.all_to_all(jnp.broadcast_to(far_rows, (8, 512, 128)), ('x', 'core'),...  6.04 us
    all_to_all x1, starting transfers between devices, body(): lax.all_to_all(jnp.broadcast_to(far_rows, (8, 512, 128)), ('x', 'core'),...  4.83 us
    all_to_all x1, starting transfers between devices, body(): got = lax.all_to_all(staged, 'y', 0, 0, tiled=True)  4.48 us
  transfers between devices with their start and end apart: 8, of which 4 were waited for; matrix products, arithmetic and copies ran while one was open for 0% of the time, Pallas kernels for 9%

profile of v1, /device:TPU:162, one launch (start us, length us, event | category | flops | bytes accessed | tf_op | source)
XLA Modules:
  0.0 164.2 jit_solution(5126505612113072765)
XLA Ops:
  0.0 0.0 copy-start
  0.0 1.0 copy-done
  1.0 0.0 copy-start.1
  1.0 1.0 copy-done.1
  2.0 0.0 copy-start.2
  2.0 1.0 copy-done.2
  3.0 2.1 %prep.1 = (bf16[768,128]{1,0:T(8,128)(2,1)S(1)}, bf16[4,1168,128]{2,1,0:T(8,128)(2,1)}) custom-call(s32[1]{0:T(128)} %bitcast.y_ref, bf16[256,768]{1,0:T(8,128)(2,1)S(1)} %copy-done, bf16[256,768]{1,0:T(8,128)(2,1)S(1)} %copy-done.1, bf16[256,768]{1,0:T(8,128)(2,1)S(1)} %copy-done.2), custom_call_target="tpu_custom_call" | custom-call | tf_op jit(solution)/shard_map/prep/pallas_call | solution.py:114
  5.1 4.5 %all-to-all-start = ((bf16[4,1168,128]{2,1,0:T(8,128)(2,1)}), bf16[4,1168,128]{2,1,0:T(8,128)(2,1)S(1)}, u32[]{:S(2)}, u32[]{:S(2)}) async-start(bf16[4,1168,128]{2,1,0:T(8,128)(2,1)} %get-tuple-element.40), calls=%async_computation | async-start | bytes 2392064 | tf_op jit(solution)/shard_map/all_to_all | solution.py:392
  9.6 10.0 %collective-permute-start = (bf16[768,128]{1,0:T(8,128)(2,1)S(1)}, bf16[768,128]{1,0:T(8,128)(2,1)S(1)}, u32[]{:S(2)}, u32[]{:S(2)}) collective-permute-start(bf16[768,128]{1,0:T(8,128)(2,1)S(1)} %get-tuple-element.39), channel_id=1, source_target_pairs={{0,2},{1,3},{2,0},{3,1},{4,6},{5,7},{6,4},{7,5},{8,10},{9,11},{10,... | collective-permute-start | bytes 589832 | tf_op jit(solution)/shard_map/ppermute | solution.py:43
  19.6 14.5 %collective-permute-done.refs_0_ = bf16[768,128]{1,0:T(8,128)(2,1)S(1)} collective-permute-done((bf16[768,128]{1,0:T(8,128)(2,1)S(1)}, bf16[768,128]{1,0:T(8,128)(2,1)S(1)}, u32[]{:S(2)}, u32[]{:S(2)}) %collective-permute-start) | collective-permute-done | bytes 196640 | tf_op jit(solution)/shard_map/ppermute | solution.py:43
  34.1 0.0 all-to-all-done.got
  34.1 0.8 sort.1
  34.9 0.0 copy-start.5
  34.9 1.9 %collective-permute-start.2 = (bf16[3072,128]{1,0:T(8,128)(2,1)S(1)}, bf16[3072,128]{1,0:T(8,128)(2,1)S(1)}, u32[]{:S(2)}, u32[]{:S(2)}) collective-permute-start(bf16[3072,128]{1,0:T(8,128)(2,1)S(1)} %get-tuple-element.45.refs_0_), channel_id=1, source_target_pairs={{0,1},{1,0},{2,3},{3,2},{4,5},{5,4},{6,7},{7,6},{8,9},{9,8},{10,11... | collective-permute-start | bytes 2359304 | tf_op jit(solution)/shard_map/ppermute | solution.py:43
  36.9 16.3 %all-to-all-start.1 = ((bf16[16,32,128]{2,1,0:T(8,128)(2,1)}), bf16[16,32,128]{2,1,0:T(8,128)(2,1)S(1)}, u32[]{:S(2)}, u32[]{:S(2)}) async-start(bf16[16,32,128]{2,1,0:T(8,128)(2,1)} %get-tuple-element.48), calls=%async_computation.1 | async-start | bytes 262144 | tf_op jit(solution)/shard_map/all_to_all | solution.py:399
  53.1 1.9 %collective-permute-start.3 = (bf16[768,128]{1,0:T(8,128)(2,1)S(1)}, bf16[768,128]{1,0:T(8,128)(2,1)S(1)}, u32[]{:S(2)}, u32[]{:S(2)}) collective-permute-start(bf16[768,128]{1,0:T(8,128)(2,1)S(1)} %collective-permute-done.refs_0_), channel_id=1, source_target_pairs={{0,1},{1,0},{2,3},{3,2},{4,5},{5,4},{6,7},{7,6},{8,9},{9,8},{10,11... | collective-permute-start | bytes 589832 | tf_op jit(solution)/shard_map/ppermute | solution.py:43
  55.0 0.0 copy-done.5
  55.1 5.2 %near.4 = (f32[192,1024]{1,0:T(8,128)S(1)}, f32[8,1024]{1,0:T(8,128)S(1)}) custom-call(bf16[4,192,256]{2,1,0:T(8,128)(2,1)S(1)} %get-tuple-element.42.q_ref, bf16[3072,128]{1,0:T(8,128)(2,1)S(1)} %get-tuple-element.45.refs_0_), custom_call_target="tpu_custom_call" | custom-call | tf_op jit(solution)/shard_map/near/pallas_call | solution.py:269
  60.2 0.0 collective-permute-done.3.refs_1_
  60.2 3.7 %all-to-all-done.1 = bf16[16,32,128]{2,1,0:T(8,128)(2,1)S(1)} async-done(((bf16[16,32,128]{2,1,0:T(8,128)(2,1)}), bf16[16,32,128]{2,1,0:T(8,128)(2,1)S(1)}, u32[]{:S(2)}, u32[]{:S(2)}) %all-to-all-start.1) | async-done | bytes 131104 | tf_op jit(solution)/shard_map/all_to_all | solution.py:399
  64.0 0.0 collective-permute-done.2.refs_0_
  64.0 5.3 %near.5 = (f32[192,1024]{1,0:T(8,128)S(1)}, f32[8,1024]{1,0:T(8,128)S(1)}) custom-call(bf16[4,192,256]{2,1,0:T(8,128)(2,1)S(1)} %get-tuple-element.42.q_ref, bf16[3072,128]{1,0:T(8,128)(2,1)S(1)} %collective-permute-done.2.refs_0_, f32[192,1024]{1,0:T(8,128)S(1)} %get-tuple-element.52.refs_1_, f32[8,1024]{1,0:T(8,128)S(1)} %get-tuple-element.53.refs_2_), custom_call_target="tpu_custom_call" | custom-call | tf_op jit(solution)/shard_map/near/pallas_call | solution.py:269
  69.3 0.0 copy-start.3
  69.3 1.1 broadcast_in_dim.3
  70.4 0.0 copy-done.3
  70.4 4.8 %all-to-all-start.2 = ((bf16[8,512,128]{2,1,0:T(8,128)(2,1)}), bf16[8,512,128]{2,1,0:T(8,128)(2,1)S(1)}, u32[]{:S(2)}, u32[]{:S(2)}) async-start(bf16[8,512,128]{2,1,0:T(8,128)(2,1)} %broadcast_in_dim.3), calls=%async_computation.2 | async-start | bytes 2097152 | tf_op jit(solution)/shard_map/all_to_all | solution.py:403
  75.2 0.0 copy-start.4
  75.2 8.5 %collective-permute-start.1 = (bf16[2304,128]{1,0:T(8,128)(2,1)}, bf16[2304,128]{1,0:T(8,128)(2,1)S(1)}, u32[]{:S(2)}, u32[]{:S(2)}) collective-permute-start(bf16[2304,128]{1,0:T(8,128)(2,1)} %copy-done.5), channel_id=1, source_target_pairs={{0,2},{1,3},{2,0},{3,1},{4,6},{5,7},{6,4},{7,5},{8,10},{9,11},{10,... | collective-permute-start | bytes 1769480 | tf_op jit(solution)/shard_map/ppermute | solution.py:43
  83.7 6.0 %all-to-all-done.2 = bf16[8,512,128]{2,1,0:T(8,128)(2,1)S(1)} async-done(((bf16[8,512,128]{2,1,0:T(8,128)(2,1)}), bf16[8,512,128]{2,1,0:T(8,128)(2,1)S(1)}, u32[]{:S(2)}, u32[]{:S(2)}) %all-to-all-start.2) | async-done | bytes 1048608 | tf_op jit(solution)/shard_map/all_to_all | solution.py:403
  89.8 2.2 %far.1 = (f32[192,1024]{1,0:T(8,128)S(1)}, f32[16,1024]{1,0:T(8,128)S(1)}) custom-call(s32[1]{0:T(128)} %bitcast.y_ref, bf16[4,192,256]{2,1,0:T(8,128)(2,1)S(1)} %get-tuple-element.42.q_ref, bf16[4096,128]{1,0:T(8,128)(2,1)S(1)} %bitcast.4), custom_call_target="tpu_custom_call" | custom-call | tf_op jit(solution)/shard_map/far/pallas_call | solution.py:360
  92.0 0.0 copy-done.4
  92.0 3.3 %near.6 = (f32[192,1024]{1,0:T(8,128)S(1)}, f32[8,1024]{1,0:T(8,128)S(1)}) custom-call(bf16[4,192,256]{2,1,0:T(8,128)(2,1)S(1)} %get-tuple-element.42.q_ref, bf16[768,128]{1,0:T(8,128)(2,1)S(1)} %collective-permute-done.refs_0_, bf16[768,128]{1,0:T(8,128)(2,1)S(1)} %collective-permute-done.3.refs_1_, f32[192,1024]{1,0:T(8,128)S(1)} %get-tuple-element.59.refs_2_, ...), custom_call_target="tpu_custom_call" | custom-call | tf_op jit(solution)/shard_map/near/pallas_call | solution.py:269
  95.3 44.2 %collective-permute-done.1.refs_0_ = bf16[2304,128]{1,0:T(8,128)(2,1)S(1)} collective-permute-done((bf16[2304,128]{1,0:T(8,128)(2,1)}, bf16[2304,128]{1,0:T(8,128)(2,1)S(1)}, u32[]{:S(2)}, u32[]{:S(2)}) %collective-permute-start.1) | collective-permute-done | bytes 589856 | tf_op jit(solution)/shard_map/ppermute | solution.py:43
  139.5 2.1 %collective-permute-start.4 = (bf16[2304,128]{1,0:T(8,128)(2,1)S(1)}, bf16[2304,128]{1,0:T(8,128)(2,1)S(1)}, u32[]{:S(2)}, u32[]{:S(2)}) collective-permute-start(bf16[2304,128]{1,0:T(8,128)(2,1)S(1)} %collective-permute-done.1.refs_0_), channel_id=1, source_target_pairs={{0,1},{1,0},{2,3},{3,2},{4,5},{5,4},{6,7},{7,6},{8,9},{9,8},{10,11... | collective-permute-start | bytes 1769480 | tf_op jit(solution)/shard_map/ppermute | solution.py:43
  141.6 4.4 %near.7 = (f32[192,1024]{1,0:T(8,128)S(1)}, f32[8,1024]{1,0:T(8,128)S(1)}) custom-call(bf16[4,192,256]{2,1,0:T(8,128)(2,1)S(1)} %get-tuple-element.42.q_ref, bf16[2304,128]{1,0:T(8,128)(2,1)S(1)} %collective-permute-done.1.refs_0_, f32[192,1024]{1,0:T(8,128)S(1)} %get-tuple-element.67.refs_1_, f32[8,1024]{1,0:T(8,128)S(1)} %get-tuple-element.68.refs_2_), custom_call_target="tpu_custom_call" | custom-call | tf_op jit(solution)/shard_map/near/pallas_call | solution.py:269
  146.0 0.0 collective-permute-done.4.refs_0_
  146.0 4.2 %last.1 = bf16[4,192,256]{2,1,0:T(8,128)(2,1)S(1)} custom-call(bf16[4,192,256]{2,1,0:T(8,128)(2,1)S(1)} %get-tuple-element.42.q_ref, bf16[2304,128]{1,0:T(8,128)(2,1)S(1)} %collective-permute-done.4.refs_0_, f32[192,1024]{1,0:T(8,128)S(1)} %get-tuple-element.69.refs_1_, f32[8,1024]{1,0:T(8,128)S(1)} %get-tuple-element.70.refs_2_, ...), custom_call_target="tpu_custom_call" | custom-call | tf_op jit(solution)/shard_map/last/pallas_call | solution.py:269
  150.2 13.0 %all_to_all.20 = bf16[4,192,256]{2,1,0:T(8,128)(2,1)S(1)} all-to-all(bf16[4,192,256]{2,1,0:T(8,128)(2,1)S(1)} %last.1), channel_id=1, replica_groups=mesh['zl'=8,'x'=4,'y'=4,'zh'=2,'core'=2] {'y'}, dimensions={0} | all-to-all | bytes 786432 | tf_op jit(solution)/shard_map/all_to_all | solution.py:413
  163.2 0.9 turn.1
Async XLA Ops:
  0.0 1.0 copy-start
  1.0 1.0 copy-start.1
  2.0 1.0 copy-start.2
  5.1 29.0 %all-to-all-start = ((bf16[4,1168,128]{2,1,0:T(8,128)(2,1)}), bf16[4,1168,128]{2,1,0:T(8,128)(2,1)S(1)}, u32[]{:S(2)}, u32[]{:S(2)}) async-start(bf16[4,1168,128]{2,1,0:T(8,128)(2,1)} %get-tuple-element.40), calls=%async_computation | async-start | bytes 2392064 | tf_op jit(solution)/shard_map/all_to_all | solution.py:392
  9.6 24.5 %collective-permute-start = (bf16[768,128]{1,0:T(8,128)(2,1)S(1)}, bf16[768,128]{1,0:T(8,128)(2,1)S(1)}, u32[]{:S(2)}, u32[]{:S(2)}) collective-permute-start(bf16[768,128]{1,0:T(8,128)(2,1)S(1)} %get-tuple-element.39), channel_id=1, source_target_pairs={{0,2},{1,3},{2,0},{3,1},{4,6},{5,7},{6,4},{7,5},{8,10},{9,11},{10,... | collective-permute-start | bytes 589832 | tf_op jit(solution)/shard_map/ppermute | solution.py:43
  34.9 20.1 %copy-start.5 = (bf16[2304,128]{1,0:T(8,128)(2,1)}, bf16[2304,128]{1,0:T(8,128)(2,1)S(1)}, u32[]{:S(2)}) copy-start(bf16[2304,128]{1,0:T(8,128)(2,1)S(1)} %get-tuple-element.43) | copy-start | bytes 1769476
  34.9 29.0 %collective-permute-start.2 = (bf16[3072,128]{1,0:T(8,128)(2,1)S(1)}, bf16[3072,128]{1,0:T(8,128)(2,1)S(1)}, u32[]{:S(2)}, u32[]{:S(2)}) collective-permute-start(bf16[3072,128]{1,0:T(8,128)(2,1)S(1)} %get-tuple-element.45.refs_0_), channel_id=1, source_target_pairs={{0,1},{1,0},{2,3},{3,2},{4,5},{5,4},{6,7},{7,6},{8,9},{9,8},{10,11... | collective-permute-start | bytes 2359304 | tf_op jit(solution)/shard_map/ppermute | solution.py:43
  36.9 27.1 %all-to-all-start.1 = ((bf16[16,32,128]{2,1,0:T(8,128)(2,1)}), bf16[16,32,128]{2,1,0:T(8,128)(2,1)S(1)}, u32[]{:S(2)}, u32[]{:S(2)}) async-start(bf16[16,32,128]{2,1,0:T(8,128)(2,1)} %get-tuple-element.48), calls=%async_computation.1 | async-start | bytes 262144 | tf_op jit(solution)/shard_map/all_to_all | solution.py:399
  53.1 7.1 %collective-permute-start.3 = (bf16[768,128]{1,0:T(8,128)(2,1)S(1)}, bf16[768,128]{1,0:T(8,128)(2,1)S(1)}, u32[]{:S(2)}, u32[]{:S(2)}) collective-permute-start(bf16[768,128]{1,0:T(8,128)(2,1)S(1)} %collective-permute-done.refs_0_), channel_id=1, source_target_pairs={{0,1},{1,0},{2,3},{3,2},{4,5},{5,4},{6,7},{7,6},{8,9},{9,8},{10,11... | collective-permute-start | bytes 589832 | tf_op jit(solution)/shard_map/ppermute | solution.py:43
  69.3 1.1 copy-start.3
  70.4 19.3 %all-to-all-start.2 = ((bf16[8,512,128]{2,1,0:T(8,128)(2,1)}), bf16[8,512,128]{2,1,0:T(8,128)(2,1)S(1)}, u32[]{:S(2)}, u32[]{:S(2)}) async-start(bf16[8,512,128]{2,1,0:T(8,128)(2,1)} %broadcast_in_dim.3), calls=%async_computation.2 | async-start | bytes 2097152 | tf_op jit(solution)/shard_map/all_to_all | solution.py:403
  75.2 16.7 %copy-start.4 = (f32[8,1024]{1,0:T(8,128)S(1)}, f32[8,1024]{1,0:T(8,128)}, u32[]{:S(2)}) copy-start(f32[8,1024]{1,0:T(8,128)} %copy-done.3) | copy-start | bytes 98308
  75.2 64.3 %collective-permute-start.1 = (bf16[2304,128]{1,0:T(8,128)(2,1)}, bf16[2304,128]{1,0:T(8,128)(2,1)S(1)}, u32[]{:S(2)}, u32[]{:S(2)}) collective-permute-start(bf16[2304,128]{1,0:T(8,128)(2,1)} %copy-done.5), channel_id=1, source_target_pairs={{0,2},{1,3},{2,0},{3,1},{4,6},{5,7},{6,4},{7,5},{8,10},{9,11},{10,... | collective-permute-start | bytes 1769480 | tf_op jit(solution)/shard_map/ppermute | solution.py:43
  139.5 6.5 %collective-permute-start.4 = (bf16[2304,128]{1,0:T(8,128)(2,1)S(1)}, bf16[2304,128]{1,0:T(8,128)(2,1)S(1)}, u32[]{:S(2)}, u32[]{:S(2)}) collective-permute-start(bf16[2304,128]{1,0:T(8,128)(2,1)S(1)} %collective-permute-done.1.refs_0_), channel_id=1, source_target_pairs={{0,1},{1,0},{2,3},{3,2},{4,5},{5,4},{6,7},{7,6},{8,9},{9,8},{10,11... | collective-permute-start | bytes 1769480 | tf_op jit(solution)/shard_map/ppermute | solution.py:43

commit v2 on v1

--- a/solution.py
+++ b/solution.py
@@ -22,7 +22,7 @@
 
 KV = 768
 QROWS = 384
-PIECE = 1168
+PIECE = 1152
 
 
 def route(dx=0, dy=0, dz=0, flip=0, by_core=False):
@@ -58,12 +58,15 @@
     return pl.BlockSpec(dims, lambda i: (0,) * len(dims))
 
 
+FREE = pl.CostEstimate(flops=1, transcendentals=0, bytes_accessed=1)
+
+
 def params():
     return pltpu.CompilerParams(vmem_limit_bytes=48 * 2**20)
 
 
 def prep_kernel(
-    y_ref, q_hbm, k_hbm, v_hbm, own_kv, staged, q_ref, k_ref, v_ref, sems
+    q_hbm, k_hbm, v_hbm, staged, far_out, q_ref, k_ref, v_ref, sems
 ):
     copies = [
         pltpu.make_async_copy(source, target, sems.at[i])
@@ -71,7 +74,6 @@
     ]
     for copy in copies:
         copy.start()
-    y = y_ref[0]
     for copy in copies:
         copy.wait()
     keys = k_ref[...]
@@ -86,6 +88,7 @@
         for source in (keys32, values)
         for j in range(2)
     ]
+    packed = []
     for group in range(4):
         lo = group * SPAN
         part = keys32[:, lo : lo + SPAN]
@@ -105,57 +108,72 @@
                 second[:, 0:128],
                 jnp.concatenate([first[:, 128:192], second[:, 128:192]], axis=1),
             ]
-        far_rows.append(jnp.zeros((10, 128), F32))
-        staged[group, 1152:1168, :] = jnp.concatenate(far_rows, axis=0).astype(BF16)
-    own_kv[...] = staged[y, 0:KV, :]
-
-
-def prep(y, queries, keys, values):
-    return pl.pallas_call(
-        prep_kernel,
-        grid=(1,),
-        out_shape=[shape(KV, 128), shape(4, PIECE, 128)],
-        in_specs=[SMEM] + [pl.BlockSpec(memory_space=pltpu.HBM)] * 3,
-        out_specs=[whole(KV, 128), whole(4, PIECE, 128)],
-        scratch_shapes=[pltpu.VMEM((256, 768), BF16)] * 3 + [pltpu.SemaphoreType.DMA((3,))],
-        compiler_params=params(),
-        name="prep",
-    )(y, queries, keys, values)
-
-
-def sort_kernel(y_ref, got, all_kv, away_kv, q_out, far_out):
-    y = y_ref[0]
-    far_rows = []
-    for i in range(4):
-        all_kv[i * KV : (i + 1) * KV, :] = got[i, 0:KV, :]
-        if i:
-            away_kv[(i - 1) * KV : i * KV, :] = got[lax.rem(y + i, 4), 0:KV, :]
-        q_out[i] = jnp.concatenate(
-            [got[i, KV : KV + SPAN, :], got[i, KV + SPAN : KV + QROWS, :]], axis=1
-        )
-        far_rows.append(got[i, KV + QROWS : PIECE, :].astype(F32))
-    blank = jnp.zeros((4, 128), F32)
-    packed = []
-    for base in (0, 3):
-        packed += [rows[base : base + 2] for rows in far_rows]
-        packed += [rows[base + 2 : base + 3] for rows in far_rows]
-        packed.append(blank)
+        packed += far_rows + [jnp.zeros((2, 128), F32)]
     packed = jnp.concatenate(packed, axis=0).astype(BF16)
     for i in range(16):
         far_out[i] = packed
 
 
-def sort(y, got):
-    shapes = [(4 * KV, 128), (3 * KV, 128), (4, SPAN, 256), (16, 32, 128)]
+def prep(queries, keys, values):
+    return pl.pallas_call(
+        prep_kernel,
+        grid=(1,),
+        out_shape=[shape(4, PIECE, 128), shape(16, 32, 128)],
+        in_specs=[pl.BlockSpec(memory_space=pltpu.HBM)] * 3,
+        out_specs=[whole(4, PIECE, 128), whole(16, 32, 128)],
+        scratch_shapes=[pltpu.VMEM((256, 768), BF16)] * 3 + [pltpu.SemaphoreType.DMA((3,))],
+        compiler_params=params(),
+        name="prep",
+    )(queries, keys, values)
+
+
+def sort_kernel(got, all_kv, q_out):
+    for i in range(4):
+        all_kv[i * KV : (i + 1) * KV, :] = got[i, 0:KV, :]
+        q_out[i] = jnp.concatenate(
+            [got[i, KV : KV + SPAN, :], got[i, KV + SPAN : PIECE, :]], axis=1
+        )
+
+
+def sort(got):
+    shapes = [(4 * KV, 128), (4, SPAN, 256)]
     return pl.pallas_call(
         sort_kernel,
         grid=(1,),
         out_shape=[shape(*dims) for dims in shapes],
-        in_specs=[SMEM, whole(4, PIECE, 128)],
+        in_specs=[whole(4, PIECE, 128)],
         out_specs=[whole(*dims) for dims in shapes],
         compiler_params=params(),
+        cost_estimate=FREE,
         name="sort",
-    )(y, got)
+    )(got)
+
+
+def spread_kernel(rows_ref, out):
+    rows = rows_ref[...].astype(F32).reshape(16, 4, 8, 128)
+    for group in range(4):
+        part = rows[:, group]
+        kinds = []
+        for base in (0, 3):
+            kinds += [part[i, base : base + 2] for i in range(16)]
+            kinds += [part[i, base + 2 : base + 3] for i in range(16)]
+        packed = jnp.concatenate(kinds, axis=0).astype(BF16)
+        for x in range(4):
+            for core in range(2):
+                out[(x * 4 + group) * 2 + core] = packed
+
+
+def spread(rows):
+    return pl.pallas_call(
+        spread_kernel,
+        grid=(1,),
+        out_shape=shape(32, 96, 128),
+        in_specs=[whole(16, 32, 128)],
+        out_specs=whole(32, 96, 128),
+        compiler_params=params(),
+        cost_estimate=FREE,
+        name="spread",
+    )(rows)
 
 
 def attend(blocks, queries, head, scores, first_peak):
@@ -296,18 +314,14 @@
     third = chosen[128:192]
     blank = jnp.zeros_like(third)
 
-    gathered = rows_ref[...].astype(F32).reshape(128, 4, 8, 128)
-
-    def section(i):
-        return gathered[:, i].reshape(1024, 128)
-
-    keys_a, keys_b = section(0).astype(BF16), section(1).astype(BF16)
-    values_a = section(2).T.astype(BF16)
-    values_b = section(3).T.astype(BF16)
-    r = lax.broadcasted_iota(jnp.int32, (1024, 128), 1)
-    key_row = lax.broadcasted_iota(jnp.int32, (1024, 128), 0)
-    there_a = r < 16
-    there_b = (r >= 16) & (key_row % 8 < 4)
+    def section(low, high):
+        return rows_ref[:, low:high, :].reshape(32 * (high - low), 128)
+
+    keys_a, keys_b = section(0, 32), section(32, 48)
+    values_a = section(48, 80).astype(F32).T.astype(BF16)
+    values_b = section(80, 96).astype(F32).T.astype(BF16)
+    r = lax.broadcasted_iota(jnp.int32, (1, 128), 1)
+    there_a, there_b = r < 16, r >= 16
     scores = [
         jnp.where(there, jnp.dot(rows, side, preferred_element_type=F32), BLANK)
         for rows, side, there in (
@@ -361,7 +375,7 @@
         far_kernel,
         grid=(1,),
         out_shape=[shape(SPAN, 1024, dtype=F32), shape(16, 1024, dtype=F32)],
-        in_specs=[SMEM, whole(4, SPAN, 256), whole(4096, 128)],
+        in_specs=[SMEM, whole(4, SPAN, 256), whole(32, 96, 128)],
         out_specs=[whole(SPAN, 1024), whole(16, 1024)],
         compiler_params=params(),
         name="far",
@@ -386,30 +400,20 @@
 
 def body(queries, keys, values):
     y = lax.axis_index("y").astype(jnp.int32).reshape(1)
-    own_kv, staged = prep(y, queries, keys, values)
-
-    crossed_own = move(own_kv, dz=8)
+    staged, far_rows = prep(queries, keys, values)
     got = lax.all_to_all(staged, "y", 0, 0, tiled=True)
-    crossed_own, got = lax.optimization_barrier((crossed_own, got))
-    all_kv, away_kv, q, far_rows = sort(y, got)
-    crossed_away = move(away_kv, dz=8)
+    far_rows = spread(lax.all_to_all(far_rows, ("zl", "zh"), 0, 0, tiled=True))
+    far_rows = lax.all_to_all(far_rows, ("x", "y", "core"), 0, 0, tiled=True)
+    all_kv, q = sort(got)
+    crossed = move(all_kv, dz=8)
     partner_kv = move(all_kv, flip=1)
-    partner_own = move(crossed_own, flip=1)
-    state = near(q, [all_kv])
-    far_rows = lax.all_to_all(far_rows, ("zl", "zh"), 0, 0, tiled=True).reshape(512, 128)
-    state, far_rows, partner_kv, partner_own = lax.optimization_barrier((state, far_rows, partner_kv, partner_own))
-    state = near(q, [partner_kv], state)
-    far_rows, *state = lax.optimization_barrier((far_rows, *state))
-    far_rows = lax.all_to_all(
-        jnp.broadcast_to(far_rows, (8, 512, 128)), ("x", "core"), 0, 0, tiled=True
-    ).reshape(4096, 128)
-    state, far_rows = lax.optimization_barrier((state, far_rows))
-    state = near(q, [crossed_own, partner_own], state)
+    all_kv, partner_kv, far_rows = lax.optimization_barrier((all_kv, partner_kv, far_rows))
     far_state = far(y, q, far_rows)
-    crossed_away, state, far_state = lax.optimization_barrier((crossed_away, state, far_state))
-    partner_away = move(crossed_away, flip=1)
-    state = near(q, [crossed_away], state)
-    result = near(q, [partner_away], state, far_state)
+    state = near(q, [all_kv, partner_kv])
+    crossed, state, far_state = lax.optimization_barrier((crossed, state, far_state))
+    partner_crossed = move(crossed, flip=1)
+    state = near(q, [crossed], state)
+    result = near(q, [partner_crossed], state, far_state)
     back = lax.all_to_all(result, "y", 0, 0, tiled=True)
     return turn(back.reshape(HEADS * HEAD_DIM, 256))
 

time: 165 us -> 149 us (0.903)
  the two profiles are of different devices: /device:TPU:162 before, /device:TPU:1 now
where the time goes in v2:
time: 149 us
  starting transfers between devices  56.4 us (38%)
  waiting for transfers between devices  35.9 us (24%)
  blocking collectives  27.2 us (18%)
  Pallas kernels  26.1 us (18%)
  local copies, waits for them, and re-layouts  2.99 us (2%)
    ppermute x3, starting transfers between devices, move(): return lax.ppermute(array, AXES, route(**step))  32.5 us
    ppermute x3, waiting for transfers between devices, move(): return lax.ppermute(array, AXES, route(**step))  21.4 us
    pallas_call x3, Pallas kernels, near(): pl.pallas_call(functools.partial(near_kernel, counts, state is not None,...  19.7 us
    all_to_all x1, starting transfers between devices, body(): far_rows = spread(lax.all_to_all(far_rows, ('zl', 'zh'), 0, 0, tiled=True))  18.5 us
    all_to_all x1, blocking collectives, body(): got = lax.all_to_all(staged, 'y', 0, 0, tiled=True)  16.9 us
    all_to_all x1, waiting for transfers between devices, body(): far_rows = lax.all_to_all(far_rows, ('x', 'y', 'core'), 0, 0, tiled=True)  14.5 us
    all_to_all x1, blocking collectives, body(): back = lax.all_to_all(result, 'y', 0, 0, tiled=True)  10.3 us
    all_to_all x1, starting transfers between devices, body(): far_rows = lax.all_to_all(far_rows, ('x', 'y', 'core'), 0, 0, tiled=True)  5.43 us
  transfers between devices with their start and end apart: 5, of which 2 were waited for; matrix products, arithmetic and copies ran while one was open for 0% of the time, Pallas kernels for 12%

profile of v2, /device:TPU:1, one launch (start us, length us, event | category | flops | bytes accessed | tf_op | source)
XLA Modules:
  0.0 148.6 jit_solution(16200842405180098735)
XLA Ops:
  0.0 0.0 copy-start
  0.0 1.0 copy-done
  1.0 0.0 copy-start.1
  1.0 1.0 copy-done.1
  2.0 0.0 copy-start.2
  2.0 1.0 copy-done.2
  3.0 1.6 %prep.1 = (bf16[4,1152,128]{2,1,0:T(8,128)(2,1)S(1)}, bf16[16,32,128]{2,1,0:T(8,128)(2,1)}) custom-call(bf16[256,768]{1,0:T(8,128)(2,1)S(1)} %copy-done, bf16[256,768]{1,0:T(8,128)(2,1)S(1)} %copy-done.1, bf16[256,768]{1,0:T(8,128)(2,1)S(1)} %copy-done.2), custom_call_target="tpu_custom_call" | custom-call | tf_op jit(solution)/shard_map/prep/pallas_call | solution.py:118
  4.6 16.9 %all_to_all.20.got = bf16[4,1152,128]{2,1,0:T(8,128)(2,1)S(1)} all-to-all(bf16[4,1152,128]{2,1,0:T(8,128)(2,1)S(1)} %get-tuple-element.23), channel_id=1, replica_groups=mesh['zl'=8,'x'=4,'y'=4,'zh'=2,'core'=2] {'y'}, dimensions={0} | all-to-all | bytes 2359296 | tf_op jit(solution)/shard_map/all_to_all | solution.py:404
  21.5 18.5 %all-to-all-start.1 = ((bf16[16,32,128]{2,1,0:T(8,128)(2,1)}), bf16[16,32,128]{2,1,0:T(8,128)(2,1)}, u32[]{:S(2)}, u32[]{:S(2)}) async-start(bf16[16,32,128]{2,1,0:T(8,128)(2,1)} %get-tuple-element.26), calls=%async_computation.1 | async-start | bytes 262144 | tf_op jit(solution)/shard_map/all_to_all | solution.py:405
  40.0 0.1 sort.1
  40.1 4.1 %collective-permute-start.1 = (bf16[3072,128]{1,0:T(8,128)(2,1)S(1)}, bf16[3072,128]{1,0:T(8,128)(2,1)S(1)}, u32[]{:S(2)}, u32[]{:S(2)}) collective-permute-start(bf16[3072,128]{1,0:T(8,128)(2,1)S(1)} %get-tuple-element.27.refs_0_), channel_id=1, source_target_pairs={{0,1},{1,0},{2,3},{3,2},{4,5},{5,4},{6,7},{7,6},{8,9},{9,8},{10,11... | collective-permute-start | bytes 2359304 | tf_op jit(solution)/shard_map/ppermute | solution.py:43
  44.2 12.2 %collective-permute-start = (bf16[3072,128]{1,0:T(8,128)(2,1)S(1)}, bf16[3072,128]{1,0:T(8,128)(2,1)S(1)}, u32[]{:S(2)}, u32[]{:S(2)}) collective-permute-start(bf16[3072,128]{1,0:T(8,128)(2,1)S(1)} %get-tuple-element.27.refs_0_), channel_id=1, source_target_pairs={{0,2},{1,3},{2,0},{3,1},{4,6},{5,7},{6,4},{7,5},{8,10},{9,11},{10,... | collective-permute-start | bytes 2359304 | tf_op jit(solution)/shard_map/ppermute | solution.py:43
  56.4 0.0 all-to-all-done.1.rows_ref
  56.4 1.9 %spread.1 = bf16[32,96,128]{2,1,0:T(8,128)(2,1)} custom-call(bf16[16,32,128]{2,1,0:T(8,128)(2,1)} %all-to-all-done.1.rows_ref), custom_call_target="tpu_custom_call" | custom-call | flops 1 | bytes 1 | tf_op jit(solution)/shard_map/spread/pallas_call | solution.py:167
  58.3 5.4 %all-to-all-start.2 = ((bf16[32,96,128]{2,1,0:T(8,128)(2,1)}), bf16[32,96,128]{2,1,0:T(8,128)(2,1)S(1)}, u32[]{:S(2)}, u32[]{:S(2)}) async-start(bf16[32,96,128]{2,1,0:T(8,128)(2,1)} %spread.1), calls=%async_computation.2 | async-start | bytes 1572864 | tf_op jit(solution)/shard_map/all_to_all | solution.py:406
  63.7 14.5 %all-to-all-done.2.rows_ref = bf16[32,96,128]{2,1,0:T(8,128)(2,1)S(1)} async-done(((bf16[32,96,128]{2,1,0:T(8,128)(2,1)}), bf16[32,96,128]{2,1,0:T(8,128)(2,1)S(1)}, u32[]{:S(2)}, u32[]{:S(2)}) %all-to-all-start.2) | async-done | bytes 786464 | tf_op jit(solution)/shard_map/all_to_all | solution.py:406
  78.2 0.0 collective-permute-done.1.refs_1_
  78.2 9.3 %near.2 = (f32[192,1024]{1,0:T(8,128)S(1)}, f32[8,1024]{1,0:T(8,128)S(1)}) custom-call(bf16[4,192,256]{2,1,0:T(8,128)(2,1)S(1)} %get-tuple-element.24.q_ref, bf16[3072,128]{1,0:T(8,128)(2,1)S(1)} %get-tuple-element.27.refs_0_, bf16[3072,128]{1,0:T(8,128)(2,1)S(1)} %collective-permute-done.1.refs_1_), custom_call_target="tpu_custom_call" | custom-call | tf_op jit(solution)/shard_map/near/pallas_call | solution.py:287
  87.6 1.8 %far.1 = (f32[192,1024]{1,0:T(8,128)S(1)}, f32[16,1024]{1,0:T(8,128)S(1)}) custom-call(s32[1]{0:T(128)} %bitcast.y_ref, bf16[4,192,256]{2,1,0:T(8,128)(2,1)S(1)} %get-tuple-element.24.q_ref, bf16[32,96,128]{2,1,0:T(8,128)(2,1)S(1)} %all-to-all-done.2.rows_ref), custom_call_target="tpu_custom_call" | custom-call | tf_op jit(solution)/shard_map/far/pallas_call | solution.py:374
  89.4 21.4 %collective-permute-done.refs_0_ = bf16[3072,128]{1,0:T(8,128)(2,1)S(1)} collective-permute-done((bf16[3072,128]{1,0:T(8,128)(2,1)S(1)}, bf16[3072,128]{1,0:T(8,128)(2,1)S(1)}, u32[]{:S(2)}, u32[]{:S(2)}) %collective-permute-start) | collective-permute-done | bytes 786464 | tf_op jit(solution)/shard_map/ppermute | solution.py:43
  110.8 16.2 %collective-permute-start.2 = (bf16[3072,128]{1,0:T(8,128)(2,1)S(1)}, bf16[3072,128]{1,0:T(8,128)(2,1)S(1)}, u32[]{:S(2)}, u32[]{:S(2)}) collective-permute-start(bf16[3072,128]{1,0:T(8,128)(2,1)S(1)} %collective-permute-done.refs_0_), channel_id=1, source_target_pairs={{0,1},{1,0},{2,3},{3,2},{4,5},{5,4},{6,7},{7,6},{8,9},{9,8},{10,11... | collective-permute-start | bytes 2359304 | tf_op jit(solution)/shard_map/ppermute | solution.py:43
  127.0 5.3 %near.3 = (f32[192,1024]{1,0:T(8,128)S(1)}, f32[8,1024]{1,0:T(8,128)S(1)}) custom-call(bf16[4,192,256]{2,1,0:T(8,128)(2,1)S(1)} %get-tuple-element.24.q_ref, bf16[3072,128]{1,0:T(8,128)(2,1)S(1)} %collective-permute-done.refs_0_, f32[192,1024]{1,0:T(8,128)S(1)} %get-tuple-element.35.refs_1_, f32[8,1024]{1,0:T(8,128)S(1)} %get-tuple-element.36.refs_2_), custom_call_target="tpu_custom_call" | custom-call | tf_op jit(solution)/shard_map/near/pallas_call | solution.py:287
  132.3 0.0 collective-permute-done.2.refs_0_
  132.3 5.1 %last.1 = bf16[4,192,256]{2,1,0:T(8,128)(2,1)S(1)} custom-call(bf16[4,192,256]{2,1,0:T(8,128)(2,1)S(1)} %get-tuple-element.24.q_ref, bf16[3072,128]{1,0:T(8,128)(2,1)S(1)} %collective-permute-done.2.refs_0_, f32[192,1024]{1,0:T(8,128)S(1)} %get-tuple-element.37.refs_1_, f32[8,1024]{1,0:T(8,128)S(1)} %get-tuple-element.38.refs_2_, ...), custom_call_target="tpu_custom_call" | custom-call | tf_op jit(solution)/shard_map/last/pallas_call | solution.py:287
  137.4 10.3 %all_to_all.21 = bf16[4,192,256]{2,1,0:T(8,128)(2,1)S(1)} all-to-all(bf16[4,192,256]{2,1,0:T(8,128)(2,1)S(1)} %last.1), channel_id=1, replica_groups=mesh['zl'=8,'x'=4,'y'=4,'zh'=2,'core'=2] {'y'}, dimensions={0} | all-to-all | bytes 786432 | tf_op jit(solution)/shard_map/all_to_all | solution.py:417
  147.7 0.9 turn.1
Async XLA Ops:
  0.0 1.0 copy-start
  1.0 1.0 copy-start.1
  2.0 1.0 copy-start.2
  21.5 34.9 %all-to-all-start.1 = ((bf16[16,32,128]{2,1,0:T(8,128)(2,1)}), bf16[16,32,128]{2,1,0:T(8,128)(2,1)}, u32[]{:S(2)}, u32[]{:S(2)}) async-start(bf16[16,32,128]{2,1,0:T(8,128)(2,1)} %get-tuple-element.26), calls=%async_computation.1 | async-start | bytes 262144 | tf_op jit(solution)/shard_map/all_to_all | solution.py:405
  40.1 38.1 %collective-permute-start.1 = (bf16[3072,128]{1,0:T(8,128)(2,1)S(1)}, bf16[3072,128]{1,0:T(8,128)(2,1)S(1)}, u32[]{:S(2)}, u32[]{:S(2)}) collective-permute-start(bf16[3072,128]{1,0:T(8,128)(2,1)S(1)} %get-tuple-element.27.refs_0_), channel_id=1, source_target_pairs={{0,1},{1,0},{2,3},{3,2},{4,5},{5,4},{6,7},{7,6},{8,9},{9,8},{10,11... | collective-permute-start | bytes 2359304 | tf_op jit(solution)/shard_map/ppermute | solution.py:43
  44.2 66.6 %collective-permute-start = (bf16[3072,128]{1,0:T(8,128)(2,1)S(1)}, bf16[3072,128]{1,0:T(8,128)(2,1)S(1)}, u32[]{:S(2)}, u32[]{:S(2)}) collective-permute-start(bf16[3072,128]{1,0:T(8,128)(2,1)S(1)} %get-tuple-element.27.refs_0_), channel_id=1, source_target_pairs={{0,2},{1,3},{2,0},{3,1},{4,6},{5,7},{6,4},{7,5},{8,10},{9,11},{10,... | collective-permute-start | bytes 2359304 | tf_op jit(solution)/shard_map/ppermute | solution.py:43
  58.3 19.9 %all-to-all-start.2 = ((bf16[32,96,128]{2,1,0:T(8,128)(2,1)}), bf16[32,96,128]{2,1,0:T(8,128)(2,1)S(1)}, u32[]{:S(2)}, u32[]{:S(2)}) async-start(bf16[32,96,128]{2,1,0:T(8,128)(2,1)} %spread.1), calls=%async_computation.2 | async-start | bytes 1572864 | tf_op jit(solution)/shard_map/all_to_all | solution.py:406
  110.8 21.5 %collective-permute-start.2 = (bf16[3072,128]{1,0:T(8,128)(2,1)S(1)}, bf16[3072,128]{1,0:T(8,128)(2,1)S(1)}, u32[]{:S(2)}, u32[]{:S(2)}) collective-permute-start(bf16[3072,128]{1,0:T(8,128)(2,1)S(1)} %collective-permute-done.refs_0_), channel_id=1, source_target_pairs={{0,1},{1,0},{2,3},{3,2},{4,5},{5,4},{6,7},{7,6},{8,9},{9,8},{10,11... | collective-permute-start | bytes 2359304 | tf_op jit(solution)/shard_map/ppermute | solution.py:43

commit v3 on v2

--- a/solution.py
+++ b/solution.py
@@ -66,7 +66,8 @@
 
 
 def prep_kernel(
-    q_hbm, k_hbm, v_hbm, staged, far_out, q_ref, k_ref, v_ref, sems
+    y_ref, q_hbm, k_hbm, v_hbm, staged, far_out, cross_0, cross_1, cross_2, cross_3,
+    q_ref, k_ref, v_ref, sems,
 ):
     copies = [
         pltpu.make_async_copy(source, target, sems.at[i])
@@ -112,19 +113,21 @@
     packed = jnp.concatenate(packed, axis=0).astype(BF16)
     for i in range(16):
         far_out[i] = packed
-
-
-def prep(queries, keys, values):
+    for i, out in enumerate((cross_0, cross_1, cross_2, cross_3)):
+        out[...] = staged[lax.rem(y_ref[0] + i, 4), 0:KV, :]
+
+
+def prep(y, queries, keys, values):
     return pl.pallas_call(
         prep_kernel,
         grid=(1,),
-        out_shape=[shape(4, PIECE, 128), shape(16, 32, 128)],
-        in_specs=[pl.BlockSpec(memory_space=pltpu.HBM)] * 3,
-        out_specs=[whole(4, PIECE, 128), whole(16, 32, 128)],
+        out_shape=[shape(4, PIECE, 128), shape(16, 32, 128)] + [shape(KV, 128)] * 4,
+        in_specs=[SMEM] + [pl.BlockSpec(memory_space=pltpu.HBM)] * 3,
+        out_specs=[whole(4, PIECE, 128), whole(16, 32, 128)] + [whole(KV, 128)] * 4,
         scratch_shapes=[pltpu.VMEM((256, 768), BF16)] * 3 + [pltpu.SemaphoreType.DMA((3,))],
         compiler_params=params(),
         name="prep",
-    )(queries, keys, values)
+    )(y, queries, keys, values)
 
 
 def sort_kernel(got, all_kv, q_out):
@@ -398,19 +401,27 @@
     )(array)
 
 
-def body(queries, keys, values):
-    y = lax.axis_index("y").astype(jnp.int32).reshape(1)
-    staged, far_rows = prep(queries, keys, values)
+def own_half(y, staged, far_rows):
     got = lax.all_to_all(staged, "y", 0, 0, tiled=True)
     far_rows = spread(lax.all_to_all(far_rows, ("zl", "zh"), 0, 0, tiled=True))
     far_rows = lax.all_to_all(far_rows, ("x", "y", "core"), 0, 0, tiled=True)
     all_kv, q = sort(got)
-    crossed = move(all_kv, dz=8)
     partner_kv = move(all_kv, flip=1)
-    all_kv, partner_kv, far_rows = lax.optimization_barrier((all_kv, partner_kv, far_rows))
-    far_state = far(y, q, far_rows)
     state = near(q, [all_kv, partner_kv])
+    return q, tuple(state), tuple(far(y, q, far_rows))
+
+
+def body(queries, keys, values):
+    y = lax.axis_index("y").astype(jnp.int32).reshape(1)
+    staged, far_rows, *cross = prep(y, queries, keys, values)
+    crossed = [move(a, dy=i, dz=8) for i, a in enumerate(cross)]
+
+    def blank(*args):
+        return jax.tree.map(lambda a: jnp.zeros(a.shape, a.dtype), jax.eval_shape(own_half, *args))
+
+    q, state, far_state = lax.cond(y[0] < 4, own_half, blank, y, staged, far_rows)
     crossed, state, far_state = lax.optimization_barrier((crossed, state, far_state))
+    crossed = jnp.concatenate(crossed, axis=0)
     partner_crossed = move(crossed, flip=1)
     state = near(q, [crossed], state)
     result = near(q, [partner_crossed], state, far_state)

time: 149 us -> 164 us (1.10)
  blocking collectives: 27.2 us -> 55.5 us
  waiting for transfers between devices: 35.9 us -> 17.1 us
  Pallas kernels: 26.1 us -> 31 us
    all_to_all x1 -> x2, blocking collectives: 16.9 us -> 45.2 us  [the longest x1 23 us: own_half(): got = lax.all_to_all(staged, 'y', 0, 0, tiled=True)]
    ppermute x3 -> x6, waiting for transfers between devices: 21.4 us -> 0.02 us  [move(): return lax.ppermute(array, AXES, route(**step))]
    all_to_all x2 -> x1, starting transfers between devices: 23.9 us -> 12 us  [own_half(): far_rows = spread(lax.all_to_all(far_rows, ('zl', 'zh'), 0, 0, tiled=True))]
    ppermute x3 -> x6, starting transfers between devices: 32.5 us -> 43.2 us  [move(): return lax.ppermute(array, AXES, route(**step))]
    pallas_call x3, Pallas kernels: 19.7 us -> 23.3 us  [near(): pl.pallas_call(functools.partial(near_kernel, counts, state is not None,...]
    all_to_all x2 -> x1, waiting for transfers between devices: 14.5 us -> 17.1 us  [own_half(): far_rows = spread(lax.all_to_all(far_rows, ('zl', 'zh'), 0, 0, tiled=True))]
    pallas_call x1, Pallas kernels: 1.82 us -> 3.68 us  [far(): pl.pallas_call(far_kernel, grid=(1,), out_shape=[shape(SPAN, 1024, dtype=...]
    pallas_call x1, Pallas kernels: 1.89 us -> 0.07 us  [spread(): pl.pallas_call(spread_kernel, grid=(1,), out_shape=shape(32, 96, 128), in...]
  transfers between devices with their start and end apart: 5 -> 7, of which waited for: 2 -> 1; matrix products, arithmetic and copies ran while one was open for 0% -> 0% of each run, Pallas kernels for 12% -> 13%
where the time goes in v3:
time: 164 us; the launch traced here: 163 us
  blocking collectives  55.5 us (34%)
  starting transfers between devices  55.2 us (34%)
  Pallas kernels  31 us (19%)
  waiting for transfers between devices  17.1 us (10%)
  local copies, waits for them, and re-layouts  4.01 us (2%)
    ppermute x6, starting transfers between devices, move(): return lax.ppermute(array, AXES, route(**step))  43.2 us
    pallas_call x3, Pallas kernels, near(): pl.pallas_call(functools.partial(near_kernel, counts, state is not None,...  23.3 us
    all_to_all x1, blocking collectives, own_half(): got = lax.all_to_all(staged, 'y', 0, 0, tiled=True)  23 us
    all_to_all x1, blocking collectives, own_half(): far_rows = lax.all_to_all(far_rows, ('x', 'y', 'core'), 0, 0, tiled=True)  22.2 us
    all_to_all x1, waiting for transfers between devices, own_half(): far_rows = spread(lax.all_to_all(far_rows, ('zl', 'zh'), 0, 0, tiled=True))  17.1 us
    all_to_all x1, starting transfers between devices, own_half(): far_rows = spread(lax.all_to_all(far_rows, ('zl', 'zh'), 0, 0, tiled=True))  12 us
    all_to_all x1, blocking collectives, body(): back = lax.all_to_all(result, 'y', 0, 0, tiled=True)  10.3 us
    pallas_call x1, Pallas kernels, far(): pl.pallas_call(far_kernel, grid=(1,), out_shape=[shape(SPAN, 1024, dtype=...  3.68 us
  transfers between devices with their start and end apart: 7, of which 1 were waited for; matrix products, arithmetic and copies ran while one was open for 0% of the time, Pallas kernels for 13%

profile of v3, /device:TPU:1, one launch (start us, length us, event | category | flops | bytes accessed | tf_op | source)
XLA Modules:
  0.0 163.0 jit_solution(4222099818605363053)
XLA Ops:
  0.0 0.0 copy-start
  0.0 1.0 copy-done
  1.0 0.0 copy-start.1
  1.0 1.0 copy-done.1
  2.0 0.0 copy-start.2
  2.0 1.0 copy-done.2
  3.0 2.2 %prep.1 = (bf16[4,1152,128]{2,1,0:T(8,128)(2,1)}, bf16[16,32,128]{2,1,0:T(8,128)(2,1)}, bf16[768,128]{1,0:T(8,128)(2,1)S(1)}, bf16[768,128]{1,0:T(8,128)(2,1)S(1...) custom-call(s32[1]{0:T(128)} %bitcast.y_ref, bf16[256,768]{1,0:T(8,128)(2,1)S(1)} %copy-done, ...), custom_call_target="tpu_custom_call" | custom-call | tf_op jit(solution)/shard_map/prep/pallas_call | solution.py:121
  5.2 16.3 %collective-permute-start.1 = (bf16[768,128]{1,0:T(8,128)(2,1)S(1)}, bf16[768,128]{1,0:T(8,128)(2,1)S(1)}, u32[]{:S(2)}, u32[]{:S(2)}) collective-permute-start(bf16[768,128]{1,0:T(8,128)(2,1)S(1)} %get-tuple-element.44), channel_id=1, source_target_pairs={{0,2},{1,3},{2,0},{3,1},{4,6},{5,7},{6,4},{7,5},{8,10},{9,11},{10,... | collective-permute-start | bytes 589832 | tf_op jit(solution)/shard_map/ppermute | solution.py:43
  21.5 2.9 %collective-permute-start.2 = (bf16[768,128]{1,0:T(8,128)(2,1)S(1)}, bf16[768,128]{1,0:T(8,128)(2,1)S(1)}, u32[]{:S(2)}, u32[]{:S(2)}) collective-permute-start(bf16[768,128]{1,0:T(8,128)(2,1)S(1)} %get-tuple-element.45), channel_id=1, source_target_pairs={{0,6},{1,7},{2,4},{3,5},{4,10},{5,11},{6,8},{7,9},{8,14},{9,15},{1... | collective-permute-start | bytes 589832 | tf_op jit(solution)/shard_map/ppermute | solution.py:43
  24.4 14.4 %collective-permute-start.3 = (bf16[768,128]{1,0:T(8,128)(2,1)S(1)}, bf16[768,128]{1,0:T(8,128)(2,1)S(1)}, u32[]{:S(2)}, u32[]{:S(2)}) collective-permute-start(bf16[768,128]{1,0:T(8,128)(2,1)S(1)} %get-tuple-element.46), channel_id=1, source_target_pairs={{0,10},{1,11},{2,8},{3,9},{4,14},{5,15},{6,12},{7,13},{8,2},{9,3},... | collective-permute-start | bytes 589832 | tf_op jit(solution)/shard_map/ppermute | solution.py:43
  38.9 2.7 %collective-permute-start.4 = (bf16[768,128]{1,0:T(8,128)(2,1)S(1)}, bf16[768,128]{1,0:T(8,128)(2,1)}, u32[]{:S(2)}, u32[]{:S(2)}) collective-permute-start(bf16[768,128]{1,0:T(8,128)(2,1)S(1)} %get-tuple-element.47), channel_id=1, source_target_pairs={{0,14},{1,15},{2,12},{3,13},{4,2},{5,3},{6,0},{7,1},{8,6},{9,7},{1... | collective-permute-start | bytes 589832 | tf_op jit(solution)/shard_map/ppermute | solution.py:43
  41.6 94.6 %conditional.1 = (bf16[4,192,256]{2,1,0:T(8,128)(2,1)}, f32[192,1024]{1,0:T(8,128)}, f32[8,1024]{1,0:T(8,128)}, f32[192,1024]{1,0:T(8,128)}, f32[16,1024]{1,0:T(8,128)S(1)}) conditional(s32[]{:T(128)} %convert_element_type.3, () %tuple.14, (bf16[4,1152,128]{2,1,0:T(8,128)(2,1)}, bf16[16,32,128]{2,1,0:T(8,128)(2,1)}, s32[1]{0:T(128)}) %tuple.15), branch_computations={%region_0.0_spmd, %region_1.0_spmd} | conditional | flops 2 | bytes 7471218 | solution.py:422
  41.6 23.0 %all_to_all.17.got = bf16[4,1152,128]{2,1,0:T(8,128)(2,1)S(1)} all-to-all(bf16[4,1152,128]{2,1,0:T(8,128)(2,1)} %get-tuple-element.11), channel_id=1, replica_groups=mesh['zl'=8,'x'=4,'y'=4,'zh'=2,'core'=2] {'y'}, dimensions={0} | all-to-all | bytes 2359296 | tf_op jit(solution)/shard_map/cond/branch_1_fun/all_to_all | solution.py:405
  64.6 12.0 %all-to-all-start.1 = ((bf16[16,32,128]{2,1,0:T(8,128)(2,1)}), bf16[16,32,128]{2,1,0:T(8,128)(2,1)S(1)}, u32[]{:S(2)}, u32[]{:S(2)}) async-start(bf16[16,32,128]{2,1,0:T(8,128)(2,1)} %get-tuple-element.17), calls=%async_computation.1 | async-start | bytes 262144 | tf_op jit(solution)/shard_map/cond/branch_1_fun/all_to_all | solution.py:406
  76.6 0.8 sort.1
  77.4 4.7 %collective-permute-start = (bf16[3072,128]{1,0:T(8,128)(2,1)S(1)}, bf16[3072,128]{1,0:T(8,128)(2,1)S(1)}, u32[]{:S(2)}, u32[]{:S(2)}) collective-permute-start(bf16[3072,128]{1,0:T(8,128)(2,1)S(1)} %get-tuple-element.13.refs_0_), channel_id=1, source_target_pairs={{0,1},{1,0},{2,3},{3,2},{4,5},{5,4},{6,7},{7,6},{8,9},{9,8},{10,11... | collective-permute-start | bytes 2359304 | tf_op jit(solution)/shard_map/cond/branch_1_fun/ppermute | solution.py:43
  82.2 17.1 %all-to-all-done.1.rows_ref = bf16[16,32,128]{2,1,0:T(8,128)(2,1)S(1)} async-done(((bf16[16,32,128]{2,1,0:T(8,128)(2,1)}), bf16[16,32,128]{2,1,0:T(8,128)(2,1)S(1)}, u32[]{:S(2)}, u32[]{:S(2)}) %all-to-all-start.1) | async-done | bytes 131104 | tf_op jit(solution)/shard_map/cond/branch_1_fun/all_to_all | solution.py:406
  99.2 0.1 spread.1
  99.3 22.2 %all_to_all.18.rows_ref = bf16[32,96,128]{2,1,0:T(8,128)(2,1)S(1)} all-to-all(bf16[32,96,128]{2,1,0:T(8,128)(2,1)S(1)} %spread.1), channel_id=1, replica_groups=mesh['zl'=8,'x'=4,'y'=4,'zh'=2,'core'=2] {'x','y','core'}, dimensions={0} | all-to-all | bytes 1572864 | tf_op jit(solution)/shard_map/cond/branch_1_fun/all_to_all | solution.py:407
  121.5 3.7 %far.1 = (f32[192,1024]{1,0:T(8,128)}, f32[16,1024]{1,0:T(8,128)S(1)}) custom-call(s32[1]{0:T(128)} %get-tuple-element.16.y_ref, bf16[4,192,256]{2,1,0:T(8,128)(2,1)} %get-tuple-element.67.q_ref, bf16[32,96,128]{2,1,0:T(8,128)(2,1)S(1)} %all_to_all.18.rows_ref), custom_call_target="tpu_custom_call" | custom-call | tf_op jit(solution)/shard_map/cond/branch_1_fun/far/pallas_call | solution.py:377
  125.2 0.0 collective-permute-done.refs_1_
  125.2 11.0 %near.2 = (f32[192,1024]{1,0:T(8,128)}, f32[8,1024]{1,0:T(8,128)}) custom-call(bf16[4,192,256]{2,1,0:T(8,128)(2,1)} %get-tuple-element.67.q_ref, bf16[3072,128]{1,0:T(8,128)(2,1)S(1)} %get-tuple-element.13.refs_0_, bf16[3072,128]{1,0:T(8,128)(2,1)S(1)} %collective-permute-done.refs_1_), custom_call_target="tpu_custom_call" | custom-call | tf_op jit(solution)/shard_map/cond/branch_1_fun/near/pallas_call | solution.py:290
  136.1 0.0 collective-permute-done.1
  136.1 0.0 collective-permute-done.2
  136.1 0.0 collective-permute-done.3
  136.2 0.0 collective-permute-done.4
  136.3 1.0 constant_dynamic-update-slice_fusion.refs_0_
  137.2 2.1 %collective-permute-start.5 = (bf16[3072,128]{1,0:T(8,128)(2,1)S(1)}, bf16[3072,128]{1,0:T(8,128)(2,1)S(1)}, u32[]{:S(2)}, u32[]{:S(2)}) collective-permute-start(bf16[3072,128]{1,0:T(8,128)(2,1)S(1)} %constant_dynamic-update-slice_fusion.refs_0_), channel_id=1, source_target_pairs={{0,1},{1,0},{2,3},{3,2},{4,5},{5,4},{6,7},{7,6},{8,9},{9,8},{10,11... | collective-permute-start | bytes 2359304 | tf_op jit(solution)/shard_map/ppermute | solution.py:43
  139.3 6.3 %near.3 = (f32[192,1024]{1,0:T(8,128)S(1)}, f32[8,1024]{1,0:T(8,128)S(1)}) custom-call(bf16[4,192,256]{2,1,0:T(8,128)(2,1)} %get-tuple-element.43.q_ref, bf16[3072,128]{1,0:T(8,128)(2,1)S(1)} %constant_dynamic-update-slice_fusion.refs_0_, f32[192,1024]{1,0:T(8,128)} %get-tuple-element.56.refs_1_, f32[8,1024]{1,0:T(8,128)} %get-tuple-element.57.refs_2_), custom_call_target="tpu_custom_call" | custom-call | tf_op jit(solution)/shard_map/near/pallas_call | solution.py:290
  145.6 0.0 collective-permute-done.5.refs_0_
  145.6 6.1 %last.1 = bf16[4,192,256]{2,1,0:T(8,128)(2,1)S(1)} custom-call(bf16[4,192,256]{2,1,0:T(8,128)(2,1)} %get-tuple-element.43.q_ref, bf16[3072,128]{1,0:T(8,128)(2,1)S(1)} %collective-permute-done.5.refs_0_, f32[192,1024]{1,0:T(8,128)S(1)} %get-tuple-element.58.refs_1_, f32[8,1024]{1,0:T(8,128)S(1)} %get-tuple-element.59.refs_2_, ...), custom_call_target="tpu_custom_call" | custom-call | tf_op jit(solution)/shard_map/last/pallas_call | solution.py:290
  151.7 10.3 %all_to_all.19 = bf16[4,192,256]{2,1,0:T(8,128)(2,1)S(1)} all-to-all(bf16[4,192,256]{2,1,0:T(8,128)(2,1)S(1)} %last.1), channel_id=1, replica_groups=mesh['zl'=8,'x'=4,'y'=4,'zh'=2,'core'=2] {'y'}, dimensions={0} | all-to-all | bytes 786432 | tf_op jit(solution)/shard_map/all_to_all | solution.py:428
  162.0 0.9 turn.1
  (3 shorter events, 0.1 us)
Async XLA Ops:
  0.0 1.0 copy-start
  1.0 1.0 copy-start.1
  2.0 1.0 copy-start.2
  5.2 130.9 %collective-permute-start.1 = (bf16[768,128]{1,0:T(8,128)(2,1)S(1)}, bf16[768,128]{1,0:T(8,128)(2,1)S(1)}, u32[]{:S(2)}, u32[]{:S(2)}) collective-permute-start(bf16[768,128]{1,0:T(8,128)(2,1)S(1)} %get-tuple-element.44), channel_id=1, source_target_pairs={{0,2},{1,3},{2,0},{3,1},{4,6},{5,7},{6,4},{7,5},{8,10},{9,11},{10,... | collective-permute-start | bytes 589832 | tf_op jit(solution)/shard_map/ppermute | solution.py:43
  21.5 114.6 %collective-permute-start.2 = (bf16[768,128]{1,0:T(8,128)(2,1)S(1)}, bf16[768,128]{1,0:T(8,128)(2,1)S(1)}, u32[]{:S(2)}, u32[]{:S(2)}) collective-permute-start(bf16[768,128]{1,0:T(8,128)(2,1)S(1)} %get-tuple-element.45), channel_id=1, source_target_pairs={{0,6},{1,7},{2,4},{3,5},{4,10},{5,11},{6,8},{7,9},{8,14},{9,15},{1... | collective-permute-start | bytes 589832 | tf_op jit(solution)/shard_map/ppermute | solution.py:43
  24.4 111.7 %collective-permute-start.3 = (bf16[768,128]{1,0:T(8,128)(2,1)S(1)}, bf16[768,128]{1,0:T(8,128)(2,1)S(1)}, u32[]{:S(2)}, u32[]{:S(2)}) collective-permute-start(bf16[768,128]{1,0:T(8,128)(2,1)S(1)} %get-tuple-element.46), channel_id=1, source_target_pairs={{0,10},{1,11},{2,8},{3,9},{4,14},{5,15},{6,12},{7,13},{8,2},{9,3},... | collective-permute-start | bytes 589832 | tf_op jit(solution)/shard_map/ppermute | solution.py:43
  38.9 97.3 %collective-permute-start.4 = (bf16[768,128]{1,0:T(8,128)(2,1)S(1)}, bf16[768,128]{1,0:T(8,128)(2,1)}, u32[]{:S(2)}, u32[]{:S(2)}) collective-permute-start(bf16[768,128]{1,0:T(8,128)(2,1)S(1)} %get-tuple-element.47), channel_id=1, source_target_pairs={{0,14},{1,15},{2,12},{3,13},{4,2},{5,3},{6,0},{7,1},{8,6},{9,7},{1... | collective-permute-start | bytes 589832 | tf_op jit(solution)/shard_map/ppermute | solution.py:43
  64.6 34.7 %all-to-all-start.1 = ((bf16[16,32,128]{2,1,0:T(8,128)(2,1)}), bf16[16,32,128]{2,1,0:T(8,128)(2,1)S(1)}, u32[]{:S(2)}, u32[]{:S(2)}) async-start(bf16[16,32,128]{2,1,0:T(8,128)(2,1)} %get-tuple-element.17), calls=%async_computation.1 | async-start | bytes 262144 | tf_op jit(solution)/shard_map/cond/branch_1_fun/all_to_all | solution.py:406
  77.4 47.7 %collective-permute-start = (bf16[3072,128]{1,0:T(8,128)(2,1)S(1)}, bf16[3072,128]{1,0:T(8,128)(2,1)S(1)}, u32[]{:S(2)}, u32[]{:S(2)}) collective-permute-start(bf16[3072,128]{1,0:T(8,128)(2,1)S(1)} %get-tuple-element.13.refs_0_), channel_id=1, source_target_pairs={{0,1},{1,0},{2,3},{3,2},{4,5},{5,4},{6,7},{7,6},{8,9},{9,8},{10,11... | collective-permute-start | bytes 2359304 | tf_op jit(solution)/shard_map/cond/branch_1_fun/ppermute | solution.py:43
  137.2 8.4 %collective-permute-start.5 = (bf16[3072,128]{1,0:T(8,128)(2,1)S(1)}, bf16[3072,128]{1,0:T(8,128)(2,1)S(1)}, u32[]{:S(2)}, u32[]{:S(2)}) collective-permute-start(bf16[3072,128]{1,0:T(8,128)(2,1)S(1)} %constant_dynamic-update-slice_fusion.refs_0_), channel_id=1, source_target_pairs={{0,1},{1,0},{2,3},{3,2},{4,5},{5,4},{6,7},{7,6},{8,9},{9,8},{10,11... | collective-permute-start | bytes 2359304 | tf_op jit(solution)/shard_map/ppermute | solution.py:43

commit v4 on v3

--- a/solution.py
+++ b/solution.py
@@ -21,8 +21,6 @@
 BF16 = jnp.bfloat16
 
 KV = 768
-QROWS = 384
-PIECE = 1152
 
 
 def route(dx=0, dy=0, dz=0, flip=0, by_core=False):
@@ -66,8 +64,7 @@
 
 
 def prep_kernel(
-    y_ref, q_hbm, k_hbm, v_hbm, staged, far_out, cross_0, cross_1, cross_2, cross_3,
-    q_ref, k_ref, v_ref, sems,
+    y_ref, q_hbm, k_hbm, v_hbm, far_out, own_kv, staged, q_out, q_ref, k_ref, v_ref, sems
 ):
     copies = [
         pltpu.make_async_copy(source, target, sems.at[i])
@@ -99,8 +96,7 @@
         ).astype(BF16)
         staged[group, 384:576, :] = values_t[lo : lo + SPAN, 0:128]
         staged[group, 576:768, :] = values_t[lo : lo + SPAN, 128:256]
-        staged[group, 768:960, :] = queries_t[lo : lo + SPAN, 0:128]
-        staged[group, 960:1152, :] = queries_t[lo : lo + SPAN, 128:256]
+        q_out[group] = queries_t[lo : lo + SPAN, :]
         far_rows = []
         for first, second in (picked[0:2], picked[2:4]):
             first, second = first[:, lo : lo + SPAN], second[:, lo : lo + SPAN]
@@ -113,43 +109,39 @@
     packed = jnp.concatenate(packed, axis=0).astype(BF16)
     for i in range(16):
         far_out[i] = packed
-    for i, out in enumerate((cross_0, cross_1, cross_2, cross_3)):
-        out[...] = staged[lax.rem(y_ref[0] + i, 4), 0:KV, :]
+    own_kv[...] = staged[y_ref[0]]
 
 
 def prep(y, queries, keys, values):
+    shapes = [(16, 32, 128), (KV, 128), (4, KV, 128), (4, SPAN, 256)]
     return pl.pallas_call(
         prep_kernel,
         grid=(1,),
-        out_shape=[shape(4, PIECE, 128), shape(16, 32, 128)] + [shape(KV, 128)] * 4,
+        out_shape=[shape(*dims) for dims in shapes],
         in_specs=[SMEM] + [pl.BlockSpec(memory_space=pltpu.HBM)] * 3,
-        out_specs=[whole(4, PIECE, 128), whole(16, 32, 128)] + [whole(KV, 128)] * 4,
+        out_specs=[whole(*dims) for dims in shapes],
         scratch_shapes=[pltpu.VMEM((256, 768), BF16)] * 3 + [pltpu.SemaphoreType.DMA((3,))],
         compiler_params=params(),
         name="prep",
     )(y, queries, keys, values)
 
 
-def sort_kernel(got, all_kv, q_out):
-    for i in range(4):
-        all_kv[i * KV : (i + 1) * KV, :] = got[i, 0:KV, :]
-        q_out[i] = jnp.concatenate(
-            [got[i, KV : KV + SPAN, :], got[i, KV + SPAN : PIECE, :]], axis=1
-        )
-
-
-def sort(got):
-    shapes = [(4 * KV, 128), (4, SPAN, 256)]
+def sort_kernel(y_ref, got, away):
+    for i in range(3):
+        away[i * KV : (i + 1) * KV, :] = got[lax.rem(y_ref[0] + 1 + i, 4)]
+
+
+def sort(y, got):
     return pl.pallas_call(
         sort_kernel,
         grid=(1,),
-        out_shape=[shape(*dims) for dims in shapes],
-        in_specs=[whole(4, PIECE, 128)],
-        out_specs=[whole(*dims) for dims in shapes],
+        out_shape=shape(3 * KV, 128),
+        in_specs=[SMEM, whole(4, KV, 128)],
+        out_specs=whole(3 * KV, 128),
         compiler_params=params(),
         cost_estimate=FREE,
         name="sort",
-    )(got)
+    )(y, got)
 
 
 def spread_kernel(rows_ref, out):
@@ -401,27 +393,38 @@
     )(array)
 
 
-def own_half(y, staged, far_rows):
+def exchange(y, staged, far_rows):
+    far_rows = lax.all_to_all(far_rows, ("zl", "zh"), 0, 0, tiled=True)
     got = lax.all_to_all(staged, "y", 0, 0, tiled=True)
-    far_rows = spread(lax.all_to_all(far_rows, ("zl", "zh"), 0, 0, tiled=True))
-    far_rows = lax.all_to_all(far_rows, ("x", "y", "core"), 0, 0, tiled=True)
-    all_kv, q = sort(got)
+    return got.reshape(4 * KV, 128), sort(y, got), far_rows
+
+
+def beside(y, q, all_kv, crossed_own, far_rows):
+    far_rows = lax.all_to_all(spread(far_rows), ("x", "y", "core"), 0, 0, tiled=True)
+    q = lax.all_to_all(q, "y", 0, 0, tiled=True)
     partner_kv = move(all_kv, flip=1)
-    state = near(q, [all_kv, partner_kv])
+    partner_own = move(crossed_own, flip=1)
+    state = near(q, [all_kv, partner_kv, crossed_own, partner_own])
+    far_rows, *state = lax.optimization_barrier((far_rows, *state))
     return q, tuple(state), tuple(far(y, q, far_rows))
+
+
+def branch(y, work, *args):
+    def blank(*args):
+        return jax.tree.map(lambda a: jnp.zeros(a.shape, a.dtype), jax.eval_shape(work, *args))
+
+    return lax.cond(y[0] < 4, work, blank, *args)
 
 
 def body(queries, keys, values):
     y = lax.axis_index("y").astype(jnp.int32).reshape(1)
-    staged, far_rows, *cross = prep(y, queries, keys, values)
-    crossed = [move(a, dy=i, dz=8) for i, a in enumerate(cross)]
-
-    def blank(*args):
-        return jax.tree.map(lambda a: jnp.zeros(a.shape, a.dtype), jax.eval_shape(own_half, *args))
-
-    q, state, far_state = lax.cond(y[0] < 4, own_half, blank, y, staged, far_rows)
+    far_rows, own_kv, staged, q = prep(y, queries, keys, values)
+    crossed_own = move(own_kv, dz=8)
+    all_kv, away, far_rows = branch(y, exchange, y, staged, far_rows)
+    away, crossed_own = lax.optimization_barrier((away, crossed_own))
+    crossed = move(away, dz=8)
+    q, state, far_state = branch(y, beside, y, q, all_kv, crossed_own, far_rows)
     crossed, state, far_state = lax.optimization_barrier((crossed, state, far_state))
-    crossed = jnp.concatenate(crossed, axis=0)
     partner_crossed = move(crossed, flip=1)
     state = near(q, [crossed], state)
     result = near(q, [partner_crossed], state, far_state)

time: 164 us -> 136 us (0.83)
  the two profiles are of different devices: /device:TPU:1 before, /device:TPU:38 now
where the time goes in v4:
time: 136 us; the launch traced here: 135 us
  starting transfers between devices  39.5 us (29%)
  Pallas kernels  33.3 us (24%)
  waiting for transfers between devices  30.4 us (22%)
  blocking collectives  27.8 us (20%)
  local copies, waits for them, and re-layouts  3.65 us (3%)
    pallas_call x3, Pallas kernels, near(): pl.pallas_call(functools.partial(near_kernel, counts, state is not None,...  23.9 us
    ppermute x5, starting transfers between devices, move(): return lax.ppermute(array, AXES, route(**step))  23.8 us
    all_to_all x1, blocking collectives, exchange(): got = lax.all_to_all(staged, 'y', 0, 0, tiled=True)  16.4 us
    ppermute x5, waiting for transfers between devices, move(): return lax.ppermute(array, AXES, route(**step))  13.9 us
    all_to_all x1, waiting for transfers between devices, exchange(): far_rows = lax.all_to_all(far_rows, ('zl', 'zh'), 0, 0, tiled=True)  12.8 us
    all_to_all x1, blocking collectives, body(): back = lax.all_to_all(result, 'y', 0, 0, tiled=True)  11.4 us
    all_to_all x1, starting transfers between devices, exchange(): far_rows = lax.all_to_all(far_rows, ('zl', 'zh'), 0, 0, tiled=True)  6.04 us
    all_to_all x1, starting transfers between devices, beside(): lax.all_to_all(spread(far_rows), ('x', 'y', 'core'), 0, 0, tiled=True)  5.58 us
  transfers between devices with their start and end apart: 8, of which 4 were waited for; matrix products, arithmetic and copies ran while one was open for 0% of the time, Pallas kernels for 19%

profile of v4, /device:TPU:38, one launch (start us, length us, event | category | flops | bytes accessed | tf_op | source)
XLA Modules:
  0.0 134.7 jit_solution(8145121303712782155)
XLA Ops:
  0.0 0.0 copy-start
  0.0 1.0 copy-done
  1.0 0.0 copy-start.1
  1.0 1.0 copy-done.1
  2.0 0.0 copy-start.2
  2.0 1.0 copy-done.2
  3.0 1.7 %prep.1 = (bf16[16,32,128]{2,1,0:T(8,128)(2,1)}, bf16[768,128]{1,0:T(8,128)(2,1)S(1)}, bf16[4,768,128]{2,1,0:T(8,128)(2,1)S(1)}, bf16[4,192,256]{2,1,0:T(8,128)(2,1)}) custom-call(s32[1]{0:T(128)} %bitcast.1.y_ref, bf16[256,768]{1,0:T(8,128)(2,1)S(1)} %copy-done, bf16[256,768]{1,0:T(8,128)(2,1)S(1)} %copy-done.1, bf16[256,768]{1,0:T(8,128)(2,1)S(1)} %copy-done.2), custom_call_target="tpu_custom_call" | custom-call | tf_op jit(solution)/shard_map/prep/pallas_call | solution.py:117
  4.7 14.8 %collective-permute-start.2 = (bf16[768,128]{1,0:T(8,128)(2,1)S(1)}, bf16[768,128]{1,0:T(8,128)(2,1)S(1)}, u32[]{:S(2)}, u32[]{:S(2)}) collective-permute-start(bf16[768,128]{1,0:T(8,128)(2,1)S(1)} %get-tuple-element.63), channel_id=1, source_target_pairs={{0,2},{1,3},{2,0},{3,1},{4,6},{5,7},{6,4},{7,5},{8,10},{9,11},{10,... | collective-permute-start | bytes 589832 | tf_op jit(solution)/shard_map/ppermute | solution.py:41
  19.5 36.4 %conditional.2 = (bf16[3072,128]{1,0:T(8,128)(2,1)}, bf16[2304,128]{1,0:T(8,128)(2,1)S(1)}, bf16[16,32,128]{2,1,0:T(8,128)(2,1)}) conditional(s32[]{:T(128)} %convert_element_type.4, () %tuple.25, (bf16[4,768,128]{2,1,0:T(8,128)(2,1)S(1)}, s32[1]{0:T(128)}, bf16[16,32,128]{2,1,0:T(8,128)(2,1)}) %tuple.26), branch_computations={%region_0.0_spmd, %region_1.0_spmd} | conditional | flops 1 | bytes 1966137 | solution.py:416
  19.5 16.4 %all_to_all.21.got = bf16[4,768,128]{2,1,0:T(8,128)(2,1)} all-to-all(bf16[4,768,128]{2,1,0:T(8,128)(2,1)S(1)} %get-tuple-element.21), channel_id=1, replica_groups=mesh['zl'=8,'x'=4,'y'=4,'zh'=2,'core'=2] {'y'}, dimensions={0} | all-to-all | bytes 1572864 | tf_op jit(solution)/shard_map/cond/branch_1_fun/all_to_all | solution.py:398
  35.9 6.0 %all-to-all-start.1 = ((bf16[16,32,128]{2,1,0:T(8,128)(2,1)}), bf16[16,32,128]{2,1,0:T(8,128)(2,1)}, u32[]{:S(2)}, u32[]{:S(2)}) async-start(bf16[16,32,128]{2,1,0:T(8,128)(2,1)} %get-tuple-element.23), calls=%async_computation.1 | async-start | bytes 262144 | tf_op jit(solution)/shard_map/cond/branch_1_fun/all_to_all | solution.py:397
  41.9 1.2 sort.1
  43.1 12.8 %all-to-all-done.1 = bf16[16,32,128]{2,1,0:T(8,128)(2,1)} async-done(((bf16[16,32,128]{2,1,0:T(8,128)(2,1)}), bf16[16,32,128]{2,1,0:T(8,128)(2,1)}, u32[]{:S(2)}, u32[]{:S(2)}) %all-to-all-start.1) | async-done | bytes 131104 | tf_op jit(solution)/shard_map/cond/branch_1_fun/all_to_all | solution.py:397
  55.9 0.0 collective-permute-done.2
  55.9 2.9 %collective-permute-start.3 = (bf16[2304,128]{1,0:T(8,128)(2,1)S(1)}, bf16[2304,128]{1,0:T(8,128)(2,1)S(1)}, u32[]{:S(2)}, u32[]{:S(2)}) collective-permute-start(bf16[2304,128]{1,0:T(8,128)(2,1)S(1)} %get-tuple-element.66), channel_id=1, source_target_pairs={{0,2},{1,3},{2,0},{3,1},{4,6},{5,7},{6,4},{7,5},{8,10},{9,11},{10,... | collective-permute-start | bytes 1769480 | tf_op jit(solution)/shard_map/ppermute | solution.py:41
  58.8 38.5 %conditional.3 = (bf16[4,192,256]{2,1,0:T(8,128)(2,1)}, f32[192,1024]{1,0:T(8,128)S(1)}, f32[8,1024]{1,0:T(8,128)}, f32[192,1024]{1,0:T(8,128)}, f32[16,1024]{1,0:T(8,128)}) conditional(s32[]{:T(128)} %convert_element_type.4, () %tuple.24, (bf16[4,192,256]{2,1,0:T(8,128)(2,1)}, bf16[16,32,128]{2,1,0:T(8,128)(2,1)}, bf16[3072,128]{1,0:T(8,128)(2,1)}, ...), branch_computations={%region_2.0_spmd, %region_3.0_spmd} | conditional | flops 1 | bytes 9044209 | solution.py:416
  58.8 0.0 copy-start.3
  58.8 0.7 copy-done.3
  59.4 4.1 %all-to-all-start.2 = ((bf16[4,192,256]{2,1,0:T(8,128)(2,1)}), bf16[4,192,256]{2,1,0:T(8,128)(2,1)}, u32[]{:S(2)}, u32[]{:S(2)}) async-start(bf16[4,192,256]{2,1,0:T(8,128)(2,1)} %get-tuple-element.24), calls=%async_computation.2 | async-start | bytes 786432 | tf_op jit(solution)/shard_map/cond/branch_1_fun/all_to_all | solution.py:404
  63.6 1.9 %collective-permute-start = (bf16[3072,128]{1,0:T(8,128)(2,1)}, bf16[3072,128]{1,0:T(8,128)(2,1)S(1)}, u32[]{:S(2)}, u32[]{:S(2)}) collective-permute-start(bf16[3072,128]{1,0:T(8,128)(2,1)} %get-tuple-element.26.refs_0_), channel_id=1, source_target_pairs={{0,1},{1,0},{2,3},{3,2},{4,5},{5,4},{6,7},{7,6},{8,9},{9,8},{10,11... | collective-permute-start | bytes 2359304 | tf_op jit(solution)/shard_map/cond/branch_1_fun/ppermute | solution.py:41
  65.5 1.9 %spread.1 = bf16[32,96,128]{2,1,0:T(8,128)(2,1)} custom-call(bf16[16,32,128]{2,1,0:T(8,128)(2,1)} %get-tuple-element.25.rows_ref), custom_call_target="tpu_custom_call" | custom-call | flops 1 | bytes 1 | tf_op jit(solution)/shard_map/cond/branch_1_fun/spread/pallas_call | solution.py:162
  67.4 0.0 copy-start.4
  67.4 3.6 %all-to-all-done.2.q_ref = bf16[4,192,256]{2,1,0:T(8,128)(2,1)} async-done(((bf16[4,192,256]{2,1,0:T(8,128)(2,1)}), bf16[4,192,256]{2,1,0:T(8,128)(2,1)}, u32[]{:S(2)}, u32[]{:S(2)}) %all-to-all-start.2) | async-done | bytes 393248 | tf_op jit(solution)/shard_map/cond/branch_1_fun/all_to_all | solution.py:404
  71.0 5.6 %all-to-all-start.3 = ((bf16[32,96,128]{2,1,0:T(8,128)(2,1)}), bf16[32,96,128]{2,1,0:T(8,128)(2,1)S(1)}, u32[]{:S(2)}, u32[]{:S(2)}) async-start(bf16[32,96,128]{2,1,0:T(8,128)(2,1)} %spread.1), calls=%async_computation.3 | async-start | bytes 1572864 | tf_op jit(solution)/shard_map/cond/branch_1_fun/all_to_all | solution.py:403
  76.6 0.0 copy-done.4
  76.6 2.1 %collective-permute-start.1 = (bf16[768,128]{1,0:T(8,128)(2,1)S(1)}, bf16[768,128]{1,0:T(8,128)(2,1)S(1)}, u32[]{:S(2)}, u32[]{:S(2)}) collective-permute-start(bf16[768,128]{1,0:T(8,128)(2,1)S(1)} %copy-done.4), channel_id=1, source_target_pairs={{0,1},{1,0},{2,3},{3,2},{4,5},{5,4},{6,7},{7,6},{8,9},{9,8},{10,11... | collective-permute-start | bytes 589832 | tf_op jit(solution)/shard_map/cond/branch_1_fun/ppermute | solution.py:41
  78.7 1.3 collective-permute-done.1.refs_3_
  79.9 0.0 collective-permute-done.refs_1_
  79.9 13.6 %near.2 = (f32[192,1024]{1,0:T(8,128)S(1)}, f32[8,1024]{1,0:T(8,128)}) custom-call(bf16[4,192,256]{2,1,0:T(8,128)(2,1)} %all-to-all-done.2.q_ref, bf16[3072,128]{1,0:T(8,128)(2,1)} %get-tuple-element.26.refs_0_, bf16[3072,128]{1,0:T(8,128)(2,1)S(1)} %collective-permute-done.refs_1_, bf16[768,128]{1,0:T(8,128)(2,1)} %copy-done.3, ...), custom_call_target="tpu_custom_call" | custom-call | tf_op jit(solution)/shard_map/cond/branch_1_fun/near/pallas_call | solution.py:282
  93.6 0.0 all-to-all-done.3.rows_ref
  93.6 3.7 %far.1 = (f32[192,1024]{1,0:T(8,128)}, f32[16,1024]{1,0:T(8,128)}) custom-call(s32[1]{0:T(128)} %get-tuple-element.32.y_ref, bf16[4,192,256]{2,1,0:T(8,128)(2,1)} %all-to-all-done.2.q_ref, bf16[32,96,128]{2,1,0:T(8,128)(2,1)S(1)} %all-to-all-done.3.rows_ref), custom_call_target="tpu_custom_call" | custom-call | tf_op jit(solution)/shard_map/cond/branch_1_fun/far/pallas_call | solution.py:369
  97.3 12.7 %collective-permute-done.3.refs_0_ = bf16[2304,128]{1,0:T(8,128)(2,1)S(1)} collective-permute-done((bf16[2304,128]{1,0:T(8,128)(2,1)S(1)}, bf16[2304,128]{1,0:T(8,128)(2,1)S(1)}, u32[]{:S(2)}, u32[]{:S(2)}) %collective-permute-start.3) | collective-permute-done | bytes 589856 | tf_op jit(solution)/shard_map/ppermute | solution.py:41
  110.0 2.1 %collective-permute-start.4 = (bf16[2304,128]{1,0:T(8,128)(2,1)S(1)}, bf16[2304,128]{1,0:T(8,128)(2,1)S(1)}, u32[]{:S(2)}, u32[]{:S(2)}) collective-permute-start(bf16[2304,128]{1,0:T(8,128)(2,1)S(1)} %collective-permute-done.3.refs_0_), channel_id=1, source_target_pairs={{0,1},{1,0},{2,3},{3,2},{4,5},{5,4},{6,7},{7,6},{8,9},{9,8},{10,11... | collective-permute-start | bytes 1769480 | tf_op jit(solution)/shard_map/ppermute | solution.py:41
  112.0 5.2 %near.3 = (f32[192,1024]{1,0:T(8,128)S(1)}, f32[8,1024]{1,0:T(8,128)S(1)}) custom-call(bf16[4,192,256]{2,1,0:T(8,128)(2,1)} %get-tuple-element.65.q_ref, bf16[2304,128]{1,0:T(8,128)(2,1)S(1)} %collective-permute-done.3.refs_0_, f32[192,1024]{1,0:T(8,128)S(1)} %get-tuple-element.72.refs_1_, f32[8,1024]{1,0:T(8,128)} %get-tuple-element.73.refs_2_), custom_call_target="tpu_custom_call" | custom-call | tf_op jit(solution)/shard_map/near/pallas_call | solution.py:282
  117.3 0.0 collective-permute-done.4.refs_0_
  117.3 5.1 %last.1 = bf16[4,192,256]{2,1,0:T(8,128)(2,1)S(1)} custom-call(bf16[4,192,256]{2,1,0:T(8,128)(2,1)} %get-tuple-element.65.q_ref, bf16[2304,128]{1,0:T(8,128)(2,1)S(1)} %collective-permute-done.4.refs_0_, f32[192,1024]{1,0:T(8,128)S(1)} %get-tuple-element.74.refs_1_, f32[8,1024]{1,0:T(8,128)S(1)} %get-tuple-element.75.refs_2_, ...), custom_call_target="tpu_custom_call" | custom-call | tf_op jit(solution)/shard_map/last/pallas_call | solution.py:282
  122.4 11.4 %all_to_all.22 = bf16[4,192,256]{2,1,0:T(8,128)(2,1)S(1)} all-to-all(bf16[4,192,256]{2,1,0:T(8,128)(2,1)S(1)} %last.1), channel_id=1, replica_groups=mesh['zl'=8,'x'=4,'y'=4,'zh'=2,'core'=2] {'y'}, dimensions={0} | all-to-all | bytes 786432 | tf_op jit(solution)/shard_map/all_to_all | solution.py:431
  133.8 0.9 turn.1
Async XLA Ops:
  0.0 1.0 copy-start
  1.0 1.0 copy-start.1
  2.0 1.0 copy-start.2
  4.7 51.2 %collective-permute-start.2 = (bf16[768,128]{1,0:T(8,128)(2,1)S(1)}, bf16[768,128]{1,0:T(8,128)(2,1)S(1)}, u32[]{:S(2)}, u32[]{:S(2)}) collective-permute-start(bf16[768,128]{1,0:T(8,128)(2,1)S(1)} %get-tuple-element.63), channel_id=1, source_target_pairs={{0,2},{1,3},{2,0},{3,1},{4,6},{5,7},{6,4},{7,5},{8,10},{9,11},{10,... | collective-permute-start | bytes 589832 | tf_op jit(solution)/shard_map/ppermute | solution.py:41
  35.9 20.0 %all-to-all-start.1 = ((bf16[16,32,128]{2,1,0:T(8,128)(2,1)}), bf16[16,32,128]{2,1,0:T(8,128)(2,1)}, u32[]{:S(2)}, u32[]{:S(2)}) async-start(bf16[16,32,128]{2,1,0:T(8,128)(2,1)} %get-tuple-element.23), calls=%async_computation.1 | async-start | bytes 262144 | tf_op jit(solution)/shard_map/cond/branch_1_fun/all_to_all | solution.py:397
  55.9 54.1 %collective-permute-start.3 = (bf16[2304,128]{1,0:T(8,128)(2,1)S(1)}, bf16[2304,128]{1,0:T(8,128)(2,1)S(1)}, u32[]{:S(2)}, u32[]{:S(2)}) collective-permute-start(bf16[2304,128]{1,0:T(8,128)(2,1)S(1)} %get-tuple-element.66), channel_id=1, source_target_pairs={{0,2},{1,3},{2,0},{3,1},{4,6},{5,7},{6,4},{7,5},{8,10},{9,11},{10,... | collective-permute-start | bytes 1769480 | tf_op jit(solution)/shard_map/ppermute | solution.py:41
  58.8 0.7 copy-start.3
  59.4 11.6 %all-to-all-start.2 = ((bf16[4,192,256]{2,1,0:T(8,128)(2,1)}), bf16[4,192,256]{2,1,0:T(8,128)(2,1)}, u32[]{:S(2)}, u32[]{:S(2)}) async-start(bf16[4,192,256]{2,1,0:T(8,128)(2,1)} %get-tuple-element.24), calls=%async_computation.2 | async-start | bytes 786432 | tf_op jit(solution)/shard_map/cond/branch_1_fun/all_to_all | solution.py:404
  63.6 16.4 %collective-permute-start = (bf16[3072,128]{1,0:T(8,128)(2,1)}, bf16[3072,128]{1,0:T(8,128)(2,1)S(1)}, u32[]{:S(2)}, u32[]{:S(2)}) collective-permute-start(bf16[3072,128]{1,0:T(8,128)(2,1)} %get-tuple-element.26.refs_0_), channel_id=1, source_target_pairs={{0,1},{1,0},{2,3},{3,2},{4,5},{5,4},{6,7},{7,6},{8,9},{9,8},{10,11... | collective-permute-start | bytes 2359304 | tf_op jit(solution)/shard_map/cond/branch_1_fun/ppermute | solution.py:41
  67.4 9.2 %copy-start.4 = (bf16[768,128]{1,0:T(8,128)(2,1)S(1)}, bf16[768,128]{1,0:T(8,128)(2,1)}, u32[]{:S(2)}) copy-start(bf16[768,128]{1,0:T(8,128)(2,1)} %copy-done.3) | copy-start | bytes 589828 | tf_op jit(solution)/shard_map/cond
  71.0 22.5 %all-to-all-start.3 = ((bf16[32,96,128]{2,1,0:T(8,128)(2,1)}), bf16[32,96,128]{2,1,0:T(8,128)(2,1)S(1)}, u32[]{:S(2)}, u32[]{:S(2)}) async-start(bf16[32,96,128]{2,1,0:T(8,128)(2,1)} %spread.1), calls=%async_computation.3 | async-start | bytes 1572864 | tf_op jit(solution)/shard_map/cond/branch_1_fun/all_to_all | solution.py:403
  76.6 3.3 %collective-permute-start.1 = (bf16[768,128]{1,0:T(8,128)(2,1)S(1)}, bf16[768,128]{1,0:T(8,128)(2,1)S(1)}, u32[]{:S(2)}, u32[]{:S(2)}) collective-permute-start(bf16[768,128]{1,0:T(8,128)(2,1)S(1)} %copy-done.4), channel_id=1, source_target_pairs={{0,1},{1,0},{2,3},{3,2},{4,5},{5,4},{6,7},{7,6},{8,9},{9,8},{10,11... | collective-permute-start | bytes 589832 | tf_op jit(solution)/shard_map/cond/branch_1_fun/ppermute | solution.py:41
  110.0 7.3 %collective-permute-start.4 = (bf16[2304,128]{1,0:T(8,128)(2,1)S(1)}, bf16[2304,128]{1,0:T(8,128)(2,1)S(1)}, u32[]{:S(2)}, u32[]{:S(2)}) collective-permute-start(bf16[2304,128]{1,0:T(8,128)(2,1)S(1)} %collective-permute-done.3.refs_0_), channel_id=1, source_target_pairs={{0,1},{1,0},{2,3},{3,2},{4,5},{5,4},{6,7},{7,6},{8,9},{9,8},{10,11... | collective-permute-start | bytes 1769480 | tf_op jit(solution)/shard_map/ppermute | solution.py:41

commit v5 on v4

--- a/solution.py
+++ b/solution.py
@@ -394,13 +394,13 @@
 
 
 def exchange(y, staged, far_rows):
-    far_rows = lax.all_to_all(far_rows, ("zl", "zh"), 0, 0, tiled=True)
+    far_rows = spread(far_rows)
     got = lax.all_to_all(staged, "y", 0, 0, tiled=True)
     return got.reshape(4 * KV, 128), sort(y, got), far_rows
 
 
 def beside(y, q, all_kv, crossed_own, far_rows):
-    far_rows = lax.all_to_all(spread(far_rows), ("x", "y", "core"), 0, 0, tiled=True)
+    far_rows = lax.all_to_all(far_rows, ("x", "y", "core"), 0, 0, tiled=True)
     q = lax.all_to_all(q, "y", 0, 0, tiled=True)
     partner_kv = move(all_kv, flip=1)
     partner_own = move(crossed_own, flip=1)
@@ -418,7 +418,11 @@
 
 def body(queries, keys, values):
     y = lax.axis_index("y").astype(jnp.int32).reshape(1)
+    queries, keys, values = (
+        pltpu.with_memory_space_constraint(a, pltpu.HBM) for a in (queries, keys, values)
+    )
     far_rows, own_kv, staged, q = prep(y, queries, keys, values)
+    far_rows = lax.all_to_all(far_rows, ("zl", "zh"), 0, 0, tiled=True)
     crossed_own = move(own_kv, dz=8)
     all_kv, away, far_rows = branch(y, exchange, y, staged, far_rows)
     away, crossed_own = lax.optimization_barrier((away, crossed_own))

time: 136 us -> 137 us (level)
  the two profiles are of different devices: /device:TPU:38 before, /device:TPU:1 now
where the time goes in v5:
time: 137 us; the launch traced here: 135 us
  starting transfers between devices  60.3 us (44%)
  Pallas kernels  32.5 us (24%)
  waiting for transfers between devices  30.8 us (22%)
  blocking collectives  10.4 us (8%)
    ppermute x5, starting transfers between devices, move(): return lax.ppermute(array, AXES, route(**step))  28.4 us
    pallas_call x3, Pallas kernels, near(): pl.pallas_call(functools.partial(near_kernel, counts, state is not None,...  23.9 us
    ppermute x5, waiting for transfers between devices, move(): return lax.ppermute(array, AXES, route(**step))  17.8 us
    all_to_all x1, starting transfers between devices, body(): far_rows = lax.all_to_all(far_rows, ('zl', 'zh'), 0, 0, tiled=True)  15.8 us
    all_to_all x1, blocking collectives, body(): back = lax.all_to_all(result, 'y', 0, 0, tiled=True)  10.4 us
    all_to_all x1, waiting for transfers between devices, exchange(): got = lax.all_to_all(staged, 'y', 0, 0, tiled=True)  8.35 us
    all_to_all x1, starting transfers between devices, beside(): far_rows = lax.all_to_all(far_rows, ('x', 'y', 'core'), 0, 0, tiled=True)  7.81 us
    all_to_all x1, starting transfers between devices, beside(): q = lax.all_to_all(q, 'y', 0, 0, tiled=True)  4.2 us
  transfers between devices with their start and end apart: 9, of which 6 were waited for; matrix products, arithmetic and copies ran while one was open for 0% of the time, Pallas kernels for 18%

profile of v5, /device:TPU:1, one launch (start us, length us, event | category | flops | bytes accessed | tf_op | source)
XLA Modules:
  0.0 134.7 jit_solution(12939950656798393224)
XLA Ops:
  0.0 2.7 %prep.1 = (bf16[16,32,128]{2,1,0:T(8,128)(2,1)}, bf16[768,128]{1,0:T(8,128)(2,1)S(1)}, bf16[4,768,128]{2,1,0:T(8,128)(2,1)}, bf16[4,192,256]{2,1,0:T(8,128)(2,1)}) custom-call(s32[1]{0:T(128)} %bitcast.1.y_ref, bf16[256,768]{1,0:T(8,128)(2,1)} %q_hbm.1, bf16[256,768]{1,0:T(8,128)(2,1)} %k_hbm.1, bf16[256,768]{1,0:T(8,128)(2,1)} %v_hbm.1), custom_call_target="tpu_custom_call" | custom-call | tf_op jit(solution)/shard_map/prep/pallas_call | solution.py:117
  2.7 15.8 %all-to-all-start.3 = ((bf16[16,32,128]{2,1,0:T(8,128)(2,1)}), bf16[16,32,128]{2,1,0:T(8,128)(2,1)S(1)}, u32[]{:S(2)}, u32[]{:S(2)}) async-start(bf16[16,32,128]{2,1,0:T(8,128)(2,1)} %get-tuple-element.59), calls=%async_computation.3 | async-start | bytes 262144 | tf_op jit(solution)/shard_map/all_to_all | solution.py:425
  18.5 12.0 %collective-permute-start.2 = (bf16[768,128]{1,0:T(8,128)(2,1)S(1)}, bf16[768,128]{1,0:T(8,128)(2,1)S(1)}, u32[]{:S(2)}, u32[]{:S(2)}) collective-permute-start(bf16[768,128]{1,0:T(8,128)(2,1)S(1)} %get-tuple-element.63), channel_id=1, source_target_pairs={{0,2},{1,3},{2,0},{3,1},{4,6},{5,7},{6,4},{7,5},{8,10},{9,11},{10,... | collective-permute-start | bytes 589832 | tf_op jit(solution)/shard_map/ppermute | solution.py:41
  30.5 1.4 %all-to-all-done.3 = bf16[16,32,128]{2,1,0:T(8,128)(2,1)S(1)} async-done(((bf16[16,32,128]{2,1,0:T(8,128)(2,1)}), bf16[16,32,128]{2,1,0:T(8,128)(2,1)S(1)}, u32[]{:S(2)}, u32[]{:S(2)}) %all-to-all-start.3) | async-done | bytes 131104 | tf_op jit(solution)/shard_map/all_to_all | solution.py:425
  31.9 13.8 %conditional.2 = (bf16[3072,128]{1,0:T(8,128)(2,1)}, bf16[2304,128]{1,0:T(8,128)(2,1)S(1)}, bf16[32,96,128]{2,1,0:T(8,128)(2,1)S(1)}) conditional(s32[]{:T(128)} %convert_element_type.4, () %tuple.25, (bf16[4,768,128]{2,1,0:T(8,128)(2,1)}, s32[1]{0:T(128)}, bf16[16,32,128]{2,1,0:T(8,128)(2,1)S(1)}) %tuple.26), branch_computations={%region_0.0_spmd, %region_1.0_spmd} | conditional | flops 2 | bytes 2359354 | solution.py:416
  31.9 4.2 %all-to-all-start = ((bf16[4,768,128]{2,1,0:T(8,128)(2,1)}), bf16[4,768,128]{2,1,0:T(8,128)(2,1)}, u32[]{:S(2)}, u32[]{:S(2)}) async-start(bf16[4,768,128]{2,1,0:T(8,128)(2,1)} %get-tuple-element.21), calls=%async_computation | async-start | bytes 1572864 | tf_op jit(solution)/shard_map/cond/branch_1_fun/all_to_all | solution.py:398
  36.1 0.1 spread.1
  36.1 8.4 %all-to-all-done.got = bf16[4,768,128]{2,1,0:T(8,128)(2,1)} async-done(((bf16[4,768,128]{2,1,0:T(8,128)(2,1)}), bf16[4,768,128]{2,1,0:T(8,128)(2,1)}, u32[]{:S(2)}, u32[]{:S(2)}) %all-to-all-start) | async-done | bytes 786464 | tf_op jit(solution)/shard_map/cond/branch_1_fun/all_to_all | solution.py:398
  44.5 1.2 sort.1
  45.7 6.3 %collective-permute-done.2 = bf16[768,128]{1,0:T(8,128)(2,1)S(1)} collective-permute-done((bf16[768,128]{1,0:T(8,128)(2,1)S(1)}, bf16[768,128]{1,0:T(8,128)(2,1)S(1)}, u32[]{:S(2)}, u32[]{:S(2)}) %collective-permute-start.2) | collective-permute-done | bytes 196640 | tf_op jit(solution)/shard_map/ppermute | solution.py:41
  52.0 0.0 copy-start.1
  52.0 0.7 copy-done.1
  52.6 8.3 %collective-permute-start.3 = (bf16[2304,128]{1,0:T(8,128)(2,1)S(1)}, bf16[2304,128]{1,0:T(8,128)(2,1)S(1)}, u32[]{:S(2)}, u32[]{:S(2)}) collective-permute-start(bf16[2304,128]{1,0:T(8,128)(2,1)S(1)} %get-tuple-element.66), channel_id=1, source_target_pairs={{0,2},{1,3},{2,0},{3,1},{4,6},{5,7},{6,4},{7,5},{8,10},{9,11},{10,... | collective-permute-start | bytes 1769480 | tf_op jit(solution)/shard_map/ppermute | solution.py:41
  60.9 39.2 %conditional.3 = (bf16[4,192,256]{2,1,0:T(8,128)(2,1)}, f32[192,1024]{1,0:T(8,128)S(1)}, f32[8,1024]{1,0:T(8,128)}, f32[192,1024]{1,0:T(8,128)}, f32[16,1024]{1,0:T(8,128)}) conditional(s32[]{:T(128)} %convert_element_type.4, () %tuple.24, (bf16[4,192,256]{2,1,0:T(8,128)(2,1)}, bf16[32,96,128]{2,1,0:T(8,128)(2,1)S(1)}, bf16[3072,128]{1,0:T(8,128)(2,1)}, ...), branch_computations={%region_2.0_spmd, %region_3.0_spmd} | conditional | bytes 11403504 | solution.py:416
  60.9 0.0 copy-start
  60.9 4.2 %all-to-all-start.1 = ((bf16[4,192,256]{2,1,0:T(8,128)(2,1)}), bf16[4,192,256]{2,1,0:T(8,128)(2,1)}, u32[]{:S(2)}, u32[]{:S(2)}) async-start(bf16[4,192,256]{2,1,0:T(8,128)(2,1)} %get-tuple-element.24), calls=%async_computation.1 | async-start | bytes 786432 | tf_op jit(solution)/shard_map/cond/branch_1_fun/all_to_all | solution.py:404
  65.1 3.3 %collective-permute-start = (bf16[3072,128]{1,0:T(8,128)(2,1)}, bf16[3072,128]{1,0:T(8,128)(2,1)S(1)}, u32[]{:S(2)}, u32[]{:S(2)}) collective-permute-start(bf16[3072,128]{1,0:T(8,128)(2,1)} %get-tuple-element.26.refs_0_), channel_id=1, source_target_pairs={{0,1},{1,0},{2,3},{3,2},{4,5},{5,4},{6,7},{7,6},{8,9},{9,8},{10,11... | collective-permute-start | bytes 2359304 | tf_op jit(solution)/shard_map/cond/branch_1_fun/ppermute | solution.py:41
  68.4 3.2 %all-to-all-done.1.q_ref = bf16[4,192,256]{2,1,0:T(8,128)(2,1)} async-done(((bf16[4,192,256]{2,1,0:T(8,128)(2,1)}), bf16[4,192,256]{2,1,0:T(8,128)(2,1)}, u32[]{:S(2)}, u32[]{:S(2)}) %all-to-all-start.1) | async-done | bytes 393248 | tf_op jit(solution)/shard_map/cond/branch_1_fun/all_to_all | solution.py:404
  71.7 0.0 copy-done
  71.7 0.0 copy-start.2
  71.7 7.8 %all-to-all-start.2 = ((bf16[32,96,128]{2,1,0:T(8,128)(2,1)}), bf16[32,96,128]{2,1,0:T(8,128)(2,1)S(1)}, u32[]{:S(2)}, u32[]{:S(2)}) async-start(bf16[32,96,128]{2,1,0:T(8,128)(2,1)} %copy-done), calls=%async_computation.2 | async-start | bytes 1572864 | tf_op jit(solution)/shard_map/cond/branch_1_fun/all_to_all | solution.py:403
  79.5 0.0 copy-done.2
  79.5 2.1 %collective-permute-start.1 = (bf16[768,128]{1,0:T(8,128)(2,1)S(1)}, bf16[768,128]{1,0:T(8,128)(2,1)S(1)}, u32[]{:S(2)}, u32[]{:S(2)}) collective-permute-start(bf16[768,128]{1,0:T(8,128)(2,1)S(1)} %copy-done.2), channel_id=1, source_target_pairs={{0,1},{1,0},{2,3},{3,2},{4,5},{5,4},{6,7},{7,6},{8,9},{9,8},{10,11... | collective-permute-start | bytes 589832 | tf_op jit(solution)/shard_map/cond/branch_1_fun/ppermute | solution.py:41
  81.6 1.2 collective-permute-done.1.refs_3_
  82.8 0.0 collective-permute-done.refs_1_
  82.8 13.6 %near.2 = (f32[192,1024]{1,0:T(8,128)S(1)}, f32[8,1024]{1,0:T(8,128)}) custom-call(bf16[4,192,256]{2,1,0:T(8,128)(2,1)} %all-to-all-done.1.q_ref, bf16[3072,128]{1,0:T(8,128)(2,1)} %get-tuple-element.26.refs_0_, bf16[3072,128]{1,0:T(8,128)(2,1)S(1)} %collective-permute-done.refs_1_, bf16[768,128]{1,0:T(8,128)(2,1)} %get-tuple-element.27.refs_2_, ...), custom_call_target="tpu_custom_call" | custom-call | tf_op jit(solution)/shard_map/cond/branch_1_fun/near/pallas_call | solution.py:282
  96.4 0.0 all-to-all-done.2.rows_ref
  96.4 3.7 %far.1 = (f32[192,1024]{1,0:T(8,128)}, f32[16,1024]{1,0:T(8,128)}) custom-call(s32[1]{0:T(128)} %get-tuple-element.32.y_ref, bf16[4,192,256]{2,1,0:T(8,128)(2,1)} %all-to-all-done.1.q_ref, bf16[32,96,128]{2,1,0:T(8,128)(2,1)S(1)} %all-to-all-done.2.rows_ref), custom_call_target="tpu_custom_call" | custom-call | tf_op jit(solution)/shard_map/cond/branch_1_fun/far/pallas_call | solution.py:369
  100.1 10.3 %collective-permute-done.3.refs_0_ = bf16[2304,128]{1,0:T(8,128)(2,1)S(1)} collective-permute-done((bf16[2304,128]{1,0:T(8,128)(2,1)S(1)}, bf16[2304,128]{1,0:T(8,128)(2,1)S(1)}, u32[]{:S(2)}, u32[]{:S(2)}) %collective-permute-start.3) | collective-permute-done | bytes 589856 | tf_op jit(solution)/shard_map/ppermute | solution.py:41
  110.4 2.7 %collective-permute-start.4 = (bf16[2304,128]{1,0:T(8,128)(2,1)S(1)}, bf16[2304,128]{1,0:T(8,128)(2,1)S(1)}, u32[]{:S(2)}, u32[]{:S(2)}) collective-permute-start(bf16[2304,128]{1,0:T(8,128)(2,1)S(1)} %collective-permute-done.3.refs_0_), channel_id=1, source_target_pairs={{0,1},{1,0},{2,3},{3,2},{4,5},{5,4},{6,7},{7,6},{8,9},{9,8},{10,11... | collective-permute-start | bytes 1769480 | tf_op jit(solution)/shard_map/ppermute | solution.py:41
  113.1 5.2 %near.3 = (f32[192,1024]{1,0:T(8,128)S(1)}, f32[8,1024]{1,0:T(8,128)S(1)}) custom-call(bf16[4,192,256]{2,1,0:T(8,128)(2,1)} %get-tuple-element.65.q_ref, bf16[2304,128]{1,0:T(8,128)(2,1)S(1)} %collective-permute-done.3.refs_0_, f32[192,1024]{1,0:T(8,128)S(1)} %get-tuple-element.72.refs_1_, f32[8,1024]{1,0:T(8,128)} %get-tuple-element.73.refs_2_), custom_call_target="tpu_custom_call" | custom-call | tf_op jit(solution)/shard_map/near/pallas_call | solution.py:282
  118.3 0.0 collective-permute-done.4.refs_0_
  118.3 5.1 %last.1 = bf16[4,192,256]{2,1,0:T(8,128)(2,1)S(1)} custom-call(bf16[4,192,256]{2,1,0:T(8,128)(2,1)} %get-tuple-element.65.q_ref, bf16[2304,128]{1,0:T(8,128)(2,1)S(1)} %collective-permute-done.4.refs_0_, f32[192,1024]{1,0:T(8,128)S(1)} %get-tuple-element.74.refs_1_, f32[8,1024]{1,0:T(8,128)S(1)} %get-tuple-element.75.refs_2_, ...), custom_call_target="tpu_custom_call" | custom-call | tf_op jit(solution)/shard_map/last/pallas_call | solution.py:282
  123.5 10.4 %all_to_all.22 = bf16[4,192,256]{2,1,0:T(8,128)(2,1)S(1)} all-to-all(bf16[4,192,256]{2,1,0:T(8,128)(2,1)S(1)} %last.1), channel_id=1, replica_groups=mesh['zl'=8,'x'=4,'y'=4,'zh'=2,'core'=2] {'y'}, dimensions={0} | all-to-all | bytes 786432 | tf_op jit(solution)/shard_map/all_to_all | solution.py:435
  133.8 0.9 turn.1
Async XLA Ops:
  2.7 29.2 %all-to-all-start.3 = ((bf16[16,32,128]{2,1,0:T(8,128)(2,1)}), bf16[16,32,128]{2,1,0:T(8,128)(2,1)S(1)}, u32[]{:S(2)}, u32[]{:S(2)}) async-start(bf16[16,32,128]{2,1,0:T(8,128)(2,1)} %get-tuple-element.59), calls=%async_computation.3 | async-start | bytes 262144 | tf_op jit(solution)/shard_map/all_to_all | solution.py:425
  18.5 33.5 %collective-permute-start.2 = (bf16[768,128]{1,0:T(8,128)(2,1)S(1)}, bf16[768,128]{1,0:T(8,128)(2,1)S(1)}, u32[]{:S(2)}, u32[]{:S(2)}) collective-permute-start(bf16[768,128]{1,0:T(8,128)(2,1)S(1)} %get-tuple-element.63), channel_id=1, source_target_pairs={{0,2},{1,3},{2,0},{3,1},{4,6},{5,7},{6,4},{7,5},{8,10},{9,11},{10,... | collective-permute-start | bytes 589832 | tf_op jit(solution)/shard_map/ppermute | solution.py:41
  31.9 12.6 %all-to-all-start = ((bf16[4,768,128]{2,1,0:T(8,128)(2,1)}), bf16[4,768,128]{2,1,0:T(8,128)(2,1)}, u32[]{:S(2)}, u32[]{:S(2)}) async-start(bf16[4,768,128]{2,1,0:T(8,128)(2,1)} %get-tuple-element.21), calls=%async_computation | async-start | bytes 1572864 | tf_op jit(solution)/shard_map/cond/branch_1_fun/all_to_all | solution.py:398
  52.0 0.7 copy-start.1
  52.6 57.8 %collective-permute-start.3 = (bf16[2304,128]{1,0:T(8,128)(2,1)S(1)}, bf16[2304,128]{1,0:T(8,128)(2,1)S(1)}, u32[]{:S(2)}, u32[]{:S(2)}) collective-permute-start(bf16[2304,128]{1,0:T(8,128)(2,1)S(1)} %get-tuple-element.66), channel_id=1, source_target_pairs={{0,2},{1,3},{2,0},{3,1},{4,6},{5,7},{6,4},{7,5},{8,10},{9,11},{10,... | collective-permute-start | bytes 1769480 | tf_op jit(solution)/shard_map/ppermute | solution.py:41
  60.9 10.7 %copy-start = (bf16[32,96,128]{2,1,0:T(8,128)(2,1)}, bf16[32,96,128]{2,1,0:T(8,128)(2,1)S(1)}, u32[]{:S(2)}) copy-start(bf16[32,96,128]{2,1,0:T(8,128)(2,1)S(1)} %get-tuple-element.25) | copy-start | bytes 2359300 | tf_op jit(solution)/shard_map/cond
  60.9 10.7 %all-to-all-start.1 = ((bf16[4,192,256]{2,1,0:T(8,128)(2,1)}), bf16[4,192,256]{2,1,0:T(8,128)(2,1)}, u32[]{:S(2)}, u32[]{:S(2)}) async-start(bf16[4,192,256]{2,1,0:T(8,128)(2,1)} %get-tuple-element.24), calls=%async_computation.1 | async-start | bytes 786432 | tf_op jit(solution)/shard_map/cond/branch_1_fun/all_to_all | solution.py:404
  65.1 17.7 %collective-permute-start = (bf16[3072,128]{1,0:T(8,128)(2,1)}, bf16[3072,128]{1,0:T(8,128)(2,1)S(1)}, u32[]{:S(2)}, u32[]{:S(2)}) collective-permute-start(bf16[3072,128]{1,0:T(8,128)(2,1)} %get-tuple-element.26.refs_0_), channel_id=1, source_target_pairs={{0,1},{1,0},{2,3},{3,2},{4,5},{5,4},{6,7},{7,6},{8,9},{9,8},{10,11... | collective-permute-start | bytes 2359304 | tf_op jit(solution)/shard_map/cond/branch_1_fun/ppermute | solution.py:41
  71.7 7.8 %copy-start.2 = (bf16[768,128]{1,0:T(8,128)(2,1)S(1)}, bf16[768,128]{1,0:T(8,128)(2,1)}, u32[]{:S(2)}) copy-start(bf16[768,128]{1,0:T(8,128)(2,1)} %get-tuple-element.27.refs_2_) | copy-start | bytes 589828 | tf_op jit(solution)/shard_map/cond
  71.7 24.8 %all-to-all-start.2 = ((bf16[32,96,128]{2,1,0:T(8,128)(2,1)}), bf16[32,96,128]{2,1,0:T(8,128)(2,1)S(1)}, u32[]{:S(2)}, u32[]{:S(2)}) async-start(bf16[32,96,128]{2,1,0:T(8,128)(2,1)} %copy-done), calls=%async_computation.2 | async-start | bytes 1572864 | tf_op jit(solution)/shard_map/cond/branch_1_fun/all_to_all | solution.py:403
  79.5 3.3 %collective-permute-start.1 = (bf16[768,128]{1,0:T(8,128)(2,1)S(1)}, bf16[768,128]{1,0:T(8,128)(2,1)S(1)}, u32[]{:S(2)}, u32[]{:S(2)}) collective-permute-start(bf16[768,128]{1,0:T(8,128)(2,1)S(1)} %copy-done.2), channel_id=1, source_target_pairs={{0,1},{1,0},{2,3},{3,2},{4,5},{5,4},{6,7},{7,6},{8,9},{9,8},{10,11... | collective-permute-start | bytes 589832 | tf_op jit(solution)/shard_map/cond/branch_1_fun/ppermute | solution.py:41
  110.4 7.9 %collective-permute-start.4 = (bf16[2304,128]{1,0:T(8,128)(2,1)S(1)}, bf16[2304,128]{1,0:T(8,128)(2,1)S(1)}, u32[]{:S(2)}, u32[]{:S(2)}) collective-permute-start(bf16[2304,128]{1,0:T(8,128)(2,1)S(1)} %collective-permute-done.3.refs_0_), channel_id=1, source_target_pairs={{0,1},{1,0},{2,3},{3,2},{4,5},{5,4},{6,7},{7,6},{8,9},{9,8},{10,11... | collective-permute-start | bytes 1769480 | tf_op jit(solution)/shard_map/ppermute | solution.py:41

commit v6 on v5

--- a/solution.py
+++ b/solution.py
@@ -423,6 +423,7 @@
     )
     far_rows, own_kv, staged, q = prep(y, queries, keys, values)
     far_rows = lax.all_to_all(far_rows, ("zl", "zh"), 0, 0, tiled=True)
+    far_rows, own_kv, staged = lax.optimization_barrier((far_rows, own_kv, staged))
     crossed_own = move(own_kv, dz=8)
     all_kv, away, far_rows = branch(y, exchange, y, staged, far_rows)
     away, crossed_own = lax.optimization_barrier((away, crossed_own))

time: 137 us -> 141 us (1.029)
  the two profiles are of different devices: /device:TPU:1 before, /device:TPU:100 now
where the time goes in v6:
time: 141 us
  blocking collectives  38.8 us (28%)
  waiting for transfers between devices  37.4 us (27%)
  Pallas kernels  32.4 us (23%)
  starting transfers between devices  31.3 us (22%)
    all_to_all x1, blocking collectives, body(): far_rows = lax.all_to_all(far_rows, ('zl', 'zh'), 0, 0, tiled=True)  27.4 us
    pallas_call x3, Pallas kernels, near(): pl.pallas_call(functools.partial(near_kernel, counts, state is not None,...  24 us
    ppermute x5, waiting for transfers between devices, move(): return lax.ppermute(array, AXES, route(**step))  20.3 us
    ppermute x5, starting transfers between devices, move(): return lax.ppermute(array, AXES, route(**step))  16.7 us
    all_to_all x1, waiting for transfers between devices, exchange(): got = lax.all_to_all(staged, 'y', 0, 0, tiled=True)  11.5 us
    all_to_all x1, blocking collectives, body(): back = lax.all_to_all(result, 'y', 0, 0, tiled=True)  11.4 us
    all_to_all x1, starting transfers between devices, beside(): far_rows = lax.all_to_all(far_rows, ('x', 'y', 'core'), 0, 0, tiled=True)  5.7 us
    all_to_all x1, waiting for transfers between devices, beside(): q = lax.all_to_all(q, 'y', 0, 0, tiled=True)  5.57 us
  transfers between devices with their start and end apart: 8, of which 5 were waited for; matrix products, arithmetic and copies ran while one was open for 0% of the time, Pallas kernels for 17%

profile of v6, /device:TPU:100, one launch (start us, length us, event | category | flops | bytes accessed | tf_op | source)
XLA Modules:
  0.0 140.7 jit_solution(12357005921291149012)
XLA Ops:
  0.0 2.5 %prep.1 = (bf16[16,32,128]{2,1,0:T(8,128)(2,1)S(1)}, bf16[768,128]{1,0:T(8,128)(2,1)S(1)}, bf16[4,768,128]{2,1,0:T(8,128)(2,1)}, bf16[4,192,256]{2,1,0:T(8,128)(2,1)}) custom-call(s32[1]{0:T(128)} %bitcast.1.y_ref, bf16[256,768]{1,0:T(8,128)(2,1)} %q_hbm.1, bf16[256,768]{1,0:T(8,128)(2,1)} %k_hbm.1, bf16[256,768]{1,0:T(8,128)(2,1)} %v_hbm.1), custom_call_target="tpu_custom_call" | custom-call | tf_op jit(solution)/shard_map/prep/pallas_call | solution.py:117
  2.5 27.4 %all_to_all.22 = bf16[16,32,128]{2,1,0:T(8,128)(2,1)S(1)} all-to-all(bf16[16,32,128]{2,1,0:T(8,128)(2,1)S(1)} %get-tuple-element.61), channel_id=1, replica_groups=mesh['zl'=8,'x'=4,'y'=4,'zh'=2,'core'=2] {'zl','zh'}, dimensions={0} | all-to-all | bytes 262144 | tf_op jit(solution)/shard_map/all_to_all | solution.py:425
  29.9 5.0 %collective-permute-start.2 = (bf16[768,128]{1,0:T(8,128)(2,1)S(1)}, bf16[768,128]{1,0:T(8,128)(2,1)S(1)}, u32[]{:S(2)}, u32[]{:S(2)}) collective-permute-start(bf16[768,128]{1,0:T(8,128)(2,1)S(1)} %get-tuple-element.69), channel_id=1, source_target_pairs={{0,2},{1,3},{2,0},{3,1},{4,6},{5,7},{6,4},{7,5},{8,10},{9,11},{10,... | collective-permute-start | bytes 589832 | tf_op jit(solution)/shard_map/ppermute | solution.py:41
  34.9 17.3 %conditional.2 = (bf16[3072,128]{1,0:T(8,128)(2,1)}, bf16[2304,128]{1,0:T(8,128)(2,1)S(1)}, bf16[32,96,128]{2,1,0:T(8,128)(2,1)S(1)}) conditional(s32[]{:T(128)} %convert_element_type.4, () %tuple.26, (bf16[4,768,128]{2,1,0:T(8,128)(2,1)}, s32[1]{0:T(128)}, bf16[16,32,128]{2,1,0:T(8,128)(2,1)S(1)}) %tuple.28), branch_computations={%region_0.0_spmd, %region_1.0_spmd} | conditional | flops 2 | bytes 2359354 | solution.py:416
  34.9 4.5 %all-to-all-start = ((bf16[4,768,128]{2,1,0:T(8,128)(2,1)}), bf16[4,768,128]{2,1,0:T(8,128)(2,1)}, u32[]{:S(2)}, u32[]{:S(2)}) async-start(bf16[4,768,128]{2,1,0:T(8,128)(2,1)} %get-tuple-element.21), calls=%async_computation | async-start | bytes 1572864 | tf_op jit(solution)/shard_map/cond/branch_1_fun/all_to_all | solution.py:398
  39.4 0.1 spread.1
  39.5 11.5 %all-to-all-done.got = bf16[4,768,128]{2,1,0:T(8,128)(2,1)} async-done(((bf16[4,768,128]{2,1,0:T(8,128)(2,1)}), bf16[4,768,128]{2,1,0:T(8,128)(2,1)}, u32[]{:S(2)}, u32[]{:S(2)}) %all-to-all-start) | async-done | bytes 786464 | tf_op jit(solution)/shard_map/cond/branch_1_fun/all_to_all | solution.py:398
  51.0 1.2 sort.1
  52.2 6.5 %collective-permute-done.2 = bf16[768,128]{1,0:T(8,128)(2,1)S(1)} collective-permute-done((bf16[768,128]{1,0:T(8,128)(2,1)S(1)}, bf16[768,128]{1,0:T(8,128)(2,1)S(1)}, u32[]{:S(2)}, u32[]{:S(2)}) %collective-permute-start.2) | collective-permute-done | bytes 196640 | tf_op jit(solution)/shard_map/ppermute | solution.py:41
  58.7 0.0 copy-start.1
  58.7 0.7 copy-done.1
  59.4 5.6 %collective-permute-start.3 = (bf16[2304,128]{1,0:T(8,128)(2,1)S(1)}, bf16[2304,128]{1,0:T(8,128)(2,1)S(1)}, u32[]{:S(2)}, u32[]{:S(2)}) collective-permute-start(bf16[2304,128]{1,0:T(8,128)(2,1)S(1)} %get-tuple-element.72), channel_id=1, source_target_pairs={{0,2},{1,3},{2,0},{3,1},{4,6},{5,7},{6,4},{7,5},{8,10},{9,11},{10,... | collective-permute-start | bytes 1769480 | tf_op jit(solution)/shard_map/ppermute | solution.py:41
  65.0 38.4 %conditional.3 = (bf16[4,192,256]{2,1,0:T(8,128)(2,1)}, f32[192,1024]{1,0:T(8,128)S(1)}, f32[8,1024]{1,0:T(8,128)}, f32[192,1024]{1,0:T(8,128)}, f32[16,1024]{1,0:T(8,128)}) conditional(s32[]{:T(128)} %convert_element_type.4, () %tuple.25, (bf16[4,192,256]{2,1,0:T(8,128)(2,1)}, bf16[32,96,128]{2,1,0:T(8,128)(2,1)S(1)}, bf16[3072,128]{1,0:T(8,128)(2,1)}, ...), branch_computations={%region_2.0_spmd, %region_3.0_spmd} | conditional | bytes 11403504 | solution.py:416
  65.0 0.0 copy-start
  65.0 4.5 %all-to-all-start.1 = ((bf16[4,192,256]{2,1,0:T(8,128)(2,1)}), bf16[4,192,256]{2,1,0:T(8,128)(2,1)}, u32[]{:S(2)}, u32[]{:S(2)}) async-start(bf16[4,192,256]{2,1,0:T(8,128)(2,1)} %get-tuple-element.24), calls=%async_computation.1 | async-start | bytes 786432 | tf_op jit(solution)/shard_map/cond/branch_1_fun/all_to_all | solution.py:404
  69.5 1.9 %collective-permute-start = (bf16[3072,128]{1,0:T(8,128)(2,1)}, bf16[3072,128]{1,0:T(8,128)(2,1)S(1)}, u32[]{:S(2)}, u32[]{:S(2)}) collective-permute-start(bf16[3072,128]{1,0:T(8,128)(2,1)} %get-tuple-element.26.refs_0_), channel_id=1, source_target_pairs={{0,1},{1,0},{2,3},{3,2},{4,5},{5,4},{6,7},{7,6},{8,9},{9,8},{10,11... | collective-permute-start | bytes 2359304 | tf_op jit(solution)/shard_map/cond/branch_1_fun/ppermute | solution.py:41
  71.4 5.6 %all-to-all-done.1.q_ref = bf16[4,192,256]{2,1,0:T(8,128)(2,1)} async-done(((bf16[4,192,256]{2,1,0:T(8,128)(2,1)}), bf16[4,192,256]{2,1,0:T(8,128)(2,1)}, u32[]{:S(2)}, u32[]{:S(2)}) %all-to-all-start.1) | async-done | bytes 393248 | tf_op jit(solution)/shard_map/cond/branch_1_fun/all_to_all | solution.py:404
  77.0 0.0 copy-done
  77.0 0.0 copy-start.2
  77.0 5.7 %all-to-all-start.2 = ((bf16[32,96,128]{2,1,0:T(8,128)(2,1)}), bf16[32,96,128]{2,1,0:T(8,128)(2,1)S(1)}, u32[]{:S(2)}, u32[]{:S(2)}) async-start(bf16[32,96,128]{2,1,0:T(8,128)(2,1)} %copy-done), calls=%async_computation.2 | async-start | bytes 1572864 | tf_op jit(solution)/shard_map/cond/branch_1_fun/all_to_all | solution.py:403
  82.7 0.0 copy-done.2
  82.7 2.1 %collective-permute-start.1 = (bf16[768,128]{1,0:T(8,128)(2,1)S(1)}, bf16[768,128]{1,0:T(8,128)(2,1)S(1)}, u32[]{:S(2)}, u32[]{:S(2)}) collective-permute-start(bf16[768,128]{1,0:T(8,128)(2,1)S(1)} %copy-done.2), channel_id=1, source_target_pairs={{0,1},{1,0},{2,3},{3,2},{4,5},{5,4},{6,7},{7,6},{8,9},{9,8},{10,11... | collective-permute-start | bytes 589832 | tf_op jit(solution)/shard_map/cond/branch_1_fun/ppermute | solution.py:41
  84.8 1.3 collective-permute-done.1.refs_3_
  86.1 0.0 collective-permute-done.refs_1_
  86.1 13.6 %near.2 = (f32[192,1024]{1,0:T(8,128)S(1)}, f32[8,1024]{1,0:T(8,128)}) custom-call(bf16[4,192,256]{2,1,0:T(8,128)(2,1)} %all-to-all-done.1.q_ref, bf16[3072,128]{1,0:T(8,128)(2,1)} %get-tuple-element.26.refs_0_, bf16[3072,128]{1,0:T(8,128)(2,1)S(1)} %collective-permute-done.refs_1_, bf16[768,128]{1,0:T(8,128)(2,1)} %get-tuple-element.27.refs_2_, ...), custom_call_target="tpu_custom_call" | custom-call | tf_op jit(solution)/shard_map/cond/branch_1_fun/near/pallas_call | solution.py:282
  99.7 0.0 all-to-all-done.2.rows_ref
  99.7 3.7 %far.1 = (f32[192,1024]{1,0:T(8,128)}, f32[16,1024]{1,0:T(8,128)}) custom-call(s32[1]{0:T(128)} %get-tuple-element.32.y_ref, bf16[4,192,256]{2,1,0:T(8,128)(2,1)} %all-to-all-done.1.q_ref, bf16[32,96,128]{2,1,0:T(8,128)(2,1)S(1)} %all-to-all-done.2.rows_ref), custom_call_target="tpu_custom_call" | custom-call | tf_op jit(solution)/shard_map/cond/branch_1_fun/far/pallas_call | solution.py:369
  103.4 12.5 %collective-permute-done.3.refs_0_ = bf16[2304,128]{1,0:T(8,128)(2,1)S(1)} collective-permute-done((bf16[2304,128]{1,0:T(8,128)(2,1)S(1)}, bf16[2304,128]{1,0:T(8,128)(2,1)S(1)}, u32[]{:S(2)}, u32[]{:S(2)}) %collective-permute-start.3) | collective-permute-done | bytes 589856 | tf_op jit(solution)/shard_map/ppermute | solution.py:41
  115.9 2.1 %collective-permute-start.4 = (bf16[2304,128]{1,0:T(8,128)(2,1)S(1)}, bf16[2304,128]{1,0:T(8,128)(2,1)S(1)}, u32[]{:S(2)}, u32[]{:S(2)}) collective-permute-start(bf16[2304,128]{1,0:T(8,128)(2,1)S(1)} %collective-permute-done.3.refs_0_), channel_id=1, source_target_pairs={{0,1},{1,0},{2,3},{3,2},{4,5},{5,4},{6,7},{7,6},{8,9},{9,8},{10,11... | collective-permute-start | bytes 1769480 | tf_op jit(solution)/shard_map/ppermute | solution.py:41
  118.0 5.2 %near.3 = (f32[192,1024]{1,0:T(8,128)S(1)}, f32[8,1024]{1,0:T(8,128)S(1)}) custom-call(bf16[4,192,256]{2,1,0:T(8,128)(2,1)} %get-tuple-element.71.q_ref, bf16[2304,128]{1,0:T(8,128)(2,1)S(1)} %collective-permute-done.3.refs_0_, f32[192,1024]{1,0:T(8,128)S(1)} %get-tuple-element.78.refs_1_, f32[8,1024]{1,0:T(8,128)} %get-tuple-element.79.refs_2_), custom_call_target="tpu_custom_call" | custom-call | tf_op jit(solution)/shard_map/near/pallas_call | solution.py:282
  123.2 0.0 collective-permute-done.4.refs_0_
  123.3 5.1 %last.1 = bf16[4,192,256]{2,1,0:T(8,128)(2,1)S(1)} custom-call(bf16[4,192,256]{2,1,0:T(8,128)(2,1)} %get-tuple-element.71.q_ref, bf16[2304,128]{1,0:T(8,128)(2,1)S(1)} %collective-permute-done.4.refs_0_, f32[192,1024]{1,0:T(8,128)S(1)} %get-tuple-element.80.refs_1_, f32[8,1024]{1,0:T(8,128)S(1)} %get-tuple-element.81.refs_2_, ...), custom_call_target="tpu_custom_call" | custom-call | tf_op jit(solution)/shard_map/last/pallas_call | solution.py:282
  128.4 11.4 %all_to_all.23 = bf16[4,192,256]{2,1,0:T(8,128)(2,1)S(1)} all-to-all(bf16[4,192,256]{2,1,0:T(8,128)(2,1)S(1)} %last.1), channel_id=1, replica_groups=mesh['zl'=8,'x'=4,'y'=4,'zh'=2,'core'=2] {'y'}, dimensions={0} | all-to-all | bytes 786432 | tf_op jit(solution)/shard_map/all_to_all | solution.py:436
  139.8 0.9 turn.1
Async XLA Ops:
  29.9 28.8 %collective-permute-start.2 = (bf16[768,128]{1,0:T(8,128)(2,1)S(1)}, bf16[768,128]{1,0:T(8,128)(2,1)S(1)}, u32[]{:S(2)}, u32[]{:S(2)}) collective-permute-start(bf16[768,128]{1,0:T(8,128)(2,1)S(1)} %get-tuple-element.69), channel_id=1, source_target_pairs={{0,2},{1,3},{2,0},{3,1},{4,6},{5,7},{6,4},{7,5},{8,10},{9,11},{10,... | collective-permute-start | bytes 589832 | tf_op jit(solution)/shard_map/ppermute | solution.py:41
  34.9 16.1 %all-to-all-start = ((bf16[4,768,128]{2,1,0:T(8,128)(2,1)}), bf16[4,768,128]{2,1,0:T(8,128)(2,1)}, u32[]{:S(2)}, u32[]{:S(2)}) async-start(bf16[4,768,128]{2,1,0:T(8,128)(2,1)} %get-tuple-element.21), calls=%async_computation | async-start | bytes 1572864 | tf_op jit(solution)/shard_map/cond/branch_1_fun/all_to_all | solution.py:398
  58.7 0.7 copy-start.1
  59.4 56.5 %collective-permute-start.3 = (bf16[2304,128]{1,0:T(8,128)(2,1)S(1)}, bf16[2304,128]{1,0:T(8,128)(2,1)S(1)}, u32[]{:S(2)}, u32[]{:S(2)}) collective-permute-start(bf16[2304,128]{1,0:T(8,128)(2,1)S(1)} %get-tuple-element.72), channel_id=1, source_target_pairs={{0,2},{1,3},{2,0},{3,1},{4,6},{5,7},{6,4},{7,5},{8,10},{9,11},{10,... | collective-permute-start | bytes 1769480 | tf_op jit(solution)/shard_map/ppermute | solution.py:41
  65.0 12.0 %copy-start = (bf16[32,96,128]{2,1,0:T(8,128)(2,1)}, bf16[32,96,128]{2,1,0:T(8,128)(2,1)S(1)}, u32[]{:S(2)}) copy-start(bf16[32,96,128]{2,1,0:T(8,128)(2,1)S(1)} %get-tuple-element.25) | copy-start | bytes 2359300 | tf_op jit(solution)/shard_map/cond
  65.0 12.0 %all-to-all-start.1 = ((bf16[4,192,256]{2,1,0:T(8,128)(2,1)}), bf16[4,192,256]{2,1,0:T(8,128)(2,1)}, u32[]{:S(2)}, u32[]{:S(2)}) async-start(bf16[4,192,256]{2,1,0:T(8,128)(2,1)} %get-tuple-element.24), calls=%async_computation.1 | async-start | bytes 786432 | tf_op jit(solution)/shard_map/cond/branch_1_fun/all_to_all | solution.py:404
  69.5 16.6 %collective-permute-start = (bf16[3072,128]{1,0:T(8,128)(2,1)}, bf16[3072,128]{1,0:T(8,128)(2,1)S(1)}, u32[]{:S(2)}, u32[]{:S(2)}) collective-permute-start(bf16[3072,128]{1,0:T(8,128)(2,1)} %get-tuple-element.26.refs_0_), channel_id=1, source_target_pairs={{0,1},{1,0},{2,3},{3,2},{4,5},{5,4},{6,7},{7,6},{8,9},{9,8},{10,11... | collective-permute-start | bytes 2359304 | tf_op jit(solution)/shard_map/cond/branch_1_fun/ppermute | solution.py:41
  77.0 5.7 %copy-start.2 = (bf16[768,128]{1,0:T(8,128)(2,1)S(1)}, bf16[768,128]{1,0:T(8,128)(2,1)}, u32[]{:S(2)}) copy-start(bf16[768,128]{1,0:T(8,128)(2,1)} %get-tuple-element.27.refs_2_) | copy-start | bytes 589828 | tf_op jit(solution)/shard_map/cond
  77.0 22.7 %all-to-all-start.2 = ((bf16[32,96,128]{2,1,0:T(8,128)(2,1)}), bf16[32,96,128]{2,1,0:T(8,128)(2,1)S(1)}, u32[]{:S(2)}, u32[]{:S(2)}) async-start(bf16[32,96,128]{2,1,0:T(8,128)(2,1)} %copy-done), calls=%async_computation.2 | async-start | bytes 1572864 | tf_op jit(solution)/shard_map/cond/branch_1_fun/all_to_all | solution.py:403
  82.7 3.3 %collective-permute-start.1 = (bf16[768,128]{1,0:T(8,128)(2,1)S(1)}, bf16[768,128]{1,0:T(8,128)(2,1)S(1)}, u32[]{:S(2)}, u32[]{:S(2)}) collective-permute-start(bf16[768,128]{1,0:T(8,128)(2,1)S(1)} %copy-done.2), channel_id=1, source_target_pairs={{0,1},{1,0},{2,3},{3,2},{4,5},{5,4},{6,7},{7,6},{8,9},{9,8},{10,11... | collective-permute-start | bytes 589832 | tf_op jit(solution)/shard_map/cond/branch_1_fun/ppermute | solution.py:41
  115.9 7.3 %collective-permute-start.4 = (bf16[2304,128]{1,0:T(8,128)(2,1)S(1)}, bf16[2304,128]{1,0:T(8,128)(2,1)S(1)}, u32[]{:S(2)}, u32[]{:S(2)}) collective-permute-start(bf16[2304,128]{1,0:T(8,128)(2,1)S(1)} %collective-permute-done.3.refs_0_), channel_id=1, source_target_pairs={{0,1},{1,0},{2,3},{3,2},{4,5},{5,4},{6,7},{7,6},{8,9},{9,8},{10,11... | collective-permute-start | bytes 1769480 | tf_op jit(solution)/shard_map/ppermute | solution.py:41

commit v7 on v5

--- a/solution.py
+++ b/solution.py
@@ -64,7 +64,7 @@
 
 
 def prep_kernel(
-    y_ref, q_hbm, k_hbm, v_hbm, far_out, own_kv, staged, q_out, q_ref, k_ref, v_ref, sems
+    q_hbm, k_hbm, v_hbm, far_out, staged, q_out, q_ref, k_ref, v_ref, sems
 ):
     copies = [
         pltpu.make_async_copy(source, target, sems.at[i])
@@ -106,42 +106,21 @@
                 jnp.concatenate([first[:, 128:192], second[:, 128:192]], axis=1),
             ]
         packed += far_rows + [jnp.zeros((2, 128), F32)]
-    packed = jnp.concatenate(packed, axis=0).astype(BF16)
-    for i in range(16):
-        far_out[i] = packed
-    own_kv[...] = staged[y_ref[0]]
-
-
-def prep(y, queries, keys, values):
-    shapes = [(16, 32, 128), (KV, 128), (4, KV, 128), (4, SPAN, 256)]
+    far_out[...] = jnp.concatenate(packed, axis=0).astype(BF16)
+
+
+def prep(queries, keys, values):
+    shapes = [(32, 128), (4, KV, 128), (4, SPAN, 256)]
     return pl.pallas_call(
         prep_kernel,
         grid=(1,),
         out_shape=[shape(*dims) for dims in shapes],
-        in_specs=[SMEM] + [pl.BlockSpec(memory_space=pltpu.HBM)] * 3,
+        in_specs=[pl.BlockSpec(memory_space=pltpu.HBM)] * 3,
         out_specs=[whole(*dims) for dims in shapes],
         scratch_shapes=[pltpu.VMEM((256, 768), BF16)] * 3 + [pltpu.SemaphoreType.DMA((3,))],
         compiler_params=params(),
         name="prep",
-    )(y, queries, keys, values)
-
-
-def sort_kernel(y_ref, got, away):
-    for i in range(3):
-        away[i * KV : (i + 1) * KV, :] = got[lax.rem(y_ref[0] + 1 + i, 4)]
-
-
-def sort(y, got):
-    return pl.pallas_call(
-        sort_kernel,
-        grid=(1,),
-        out_shape=shape(3 * KV, 128),
-        in_specs=[SMEM, whole(4, KV, 128)],
-        out_specs=whole(3 * KV, 128),
-        compiler_params=params(),
-        cost_estimate=FREE,
-        name="sort",
-    )(y, got)
+    )(queries, keys, values)
 
 
 def spread_kernel(rows_ref, out):
@@ -163,7 +142,7 @@
         spread_kernel,
         grid=(1,),
         out_shape=shape(32, 96, 128),
-        in_specs=[whole(16, 32, 128)],
+        in_specs=[whole(512, 128)],
         out_specs=whole(32, 96, 128),
         compiler_params=params(),
         cost_estimate=FREE,
@@ -393,18 +372,22 @@
     )(array)
 
 
-def exchange(y, staged, far_rows):
-    far_rows = spread(far_rows)
+def double(rows, dz):
+    return jnp.concatenate([rows, move(rows, dz=dz)], axis=0)
+
+
+def exchange(staged, far_rows):
     got = lax.all_to_all(staged, "y", 0, 0, tiled=True)
-    return got.reshape(4 * KV, 128), sort(y, got), far_rows
-
-
-def beside(y, q, all_kv, crossed_own, far_rows):
-    far_rows = lax.all_to_all(far_rows, ("x", "y", "core"), 0, 0, tiled=True)
+    for dz in (1, -2, 4, 8):
+        far_rows = double(far_rows, dz)
+    return got.reshape(4 * KV, 128), far_rows
+
+
+def beside(y, q, all_kv, far_rows):
+    far_rows = lax.all_to_all(spread(far_rows), ("x", "y", "core"), 0, 0, tiled=True)
     q = lax.all_to_all(q, "y", 0, 0, tiled=True)
     partner_kv = move(all_kv, flip=1)
-    partner_own = move(crossed_own, flip=1)
-    state = near(q, [all_kv, partner_kv, crossed_own, partner_own])
+    state = near(q, [all_kv, partner_kv])
     far_rows, *state = lax.optimization_barrier((far_rows, *state))
     return q, tuple(state), tuple(far(y, q, far_rows))
 
@@ -421,13 +404,10 @@
     queries, keys, values = (
         pltpu.with_memory_space_constraint(a, pltpu.HBM) for a in (queries, keys, values)
     )
-    far_rows, own_kv, staged, q = prep(y, queries, keys, values)
-    far_rows = lax.all_to_all(far_rows, ("zl", "zh"), 0, 0, tiled=True)
-    crossed_own = move(own_kv, dz=8)
-    all_kv, away, far_rows = branch(y, exchange, y, staged, far_rows)
-    away, crossed_own = lax.optimization_barrier((away, crossed_own))
-    crossed = move(away, dz=8)
-    q, state, far_state = branch(y, beside, y, q, all_kv, crossed_own, far_rows)
+    far_rows, staged, q = prep(queries, keys, values)
+    all_kv, far_rows = branch(y, exchange, staged, far_rows)
+    crossed = move(all_kv, dz=8)
+    q, state, far_state = branch(y, beside, y, q, all_kv, far_rows)
     crossed, state, far_state = lax.optimization_barrier((crossed, state, far_state))
     partner_crossed = move(crossed, flip=1)
     state = near(q, [crossed], state)

time: 137 us -> 151 us (1.10)
  the two profiles are of different devices: /device:TPU:1 before, /device:TPU:226 now
where the time goes in v7:
time: 151 us; the launch traced here: 150 us
  waiting for transfers between devices  63.9 us (42%)
  starting transfers between devices  40 us (26%)
  Pallas kernels  30.8 us (20%)
  blocking collectives  12.5 us (8%)
  local copies, waits for them, and re-layouts  3.03 us (2%)
    ppermute x7, waiting for transfers between devices, move(): return lax.ppermute(array, AXES, route(**step))  58.8 us
    ppermute x7, starting transfers between devices, move(): return lax.ppermute(array, AXES, route(**step))  25.1 us
    pallas_call x3, Pallas kernels, near(): pl.pallas_call(functools.partial(near_kernel, counts, state is not None,...  22.6 us
    all_to_all x1, blocking collectives, body(): back = lax.all_to_all(result, 'y', 0, 0, tiled=True)  12.5 us
    all_to_all x1, starting transfers between devices, beside(): lax.all_to_all(spread(far_rows), ('x', 'y', 'core'), 0, 0, tiled=True)  5.6 us
    all_to_all x1, starting transfers between devices, beside(): q = lax.all_to_all(q, 'y', 0, 0, tiled=True)  4.81 us
    all_to_all x1, starting transfers between devices, exchange(): got = lax.all_to_all(staged, 'y', 0, 0, tiled=True)  4.48 us
    all_to_all x1, waiting for transfers between devices, beside(): q = lax.all_to_all(q, 'y', 0, 0, tiled=True)  3.71 us
  transfers between devices with their start and end apart: 10, of which 6 were waited for; matrix products, arithmetic and copies ran while one was open for 2% of the time, Pallas kernels for 14%

profile of v7, /device:TPU:226, one launch (start us, length us, event | category | flops | bytes accessed | tf_op | source)
XLA Modules:
  0.0 150.3 jit_solution(18202752616882601439)
XLA Ops:
  0.0 2.5 %prep.1 = (bf16[32,128]{1,0:T(8,128)(2,1)S(1)}, bf16[4,768,128]{2,1,0:T(8,128)(2,1)}, bf16[4,192,256]{2,1,0:T(8,128)(2,1)}) custom-call(bf16[256,768]{1,0:T(8,128)(2,1)} %q_hbm.1, bf16[256,768]{1,0:T(8,128)(2,1)} %k_hbm.1, bf16[256,768]{1,0:T(8,128)(2,1)} %v_hbm.1), custom_call_target="tpu_custom_call" | custom-call | tf_op jit(solution)/shard_map/prep/pallas_call | solution.py:114
  2.6 44.8 %conditional.2 = (bf16[3072,128]{1,0:T(8,128)(2,1)}, bf16[512,128]{1,0:T(8,128)(2,1)}) conditional(s32[]{:T(128)} %convert_element_type.4, () %tuple.24, (bf16[4,768,128]{2,1,0:T(8,128)(2,1)}, bf16[32,128]{1,0:T(8,128)(2,1)S(1)}) %tuple.25), branch_computations={%region_0.0_spmd, %region_1.0_spmd} | conditional | flops 393216 | bytes 3342544 | solution.py:399
  2.6 5.0 %collective-permute-start.1 = (bf16[32,128]{1,0:T(8,128)(2,1)S(1)}, bf16[32,128]{1,0:T(8,128)(2,1)S(1)}, u32[]{:S(2)}, u32[]{:S(2)}) collective-permute-start(bf16[32,128]{1,0:T(8,128)(2,1)S(1)} %get-tuple-element.19), channel_id=1, source_target_pairs={{0,64},{1,65},{2,66},{3,67},{4,68},{5,69},{6,70},{7,71},{8,72},{9,... | collective-permute-start | bytes 24584 | tf_op jit(solution)/shard_map/cond/branch_1_fun/ppermute | solution.py:41
  7.6 4.5 %all-to-all-start.2 = ((bf16[4,768,128]{2,1,0:T(8,128)(2,1)}), bf16[4,768,128]{2,1,0:T(8,128)(2,1)}, u32[]{:S(2)}, u32[]{:S(2)}) async-start(bf16[4,768,128]{2,1,0:T(8,128)(2,1)} %get-tuple-element.18), calls=%async_computation.2 | async-start | bytes 1572864 | tf_op jit(solution)/shard_map/cond/branch_1_fun/all_to_all | solution.py:380
  12.1 0.6 constant_dynamic-update-slice_fusion.4
  12.7 0.0 collective-permute-done.1
  12.7 1.9 %collective-permute-start.2 = (bf16[64,128]{1,0:T(8,128)(2,1)S(1)}, bf16[64,128]{1,0:T(8,128)(2,1)S(1)}, u32[]{:S(2)}, u32[]{:S(2)}) collective-permute-start(bf16[64,128]{1,0:T(8,128)(2,1)S(1)} %pad_maximum_fusion.2), channel_id=1, source_target_pairs={{0,386},{1,387},{2,384},{3,385},{4,390},{5,391},{6,388},{7,389},{8... | collective-permute-start | bytes 49160 | tf_op jit(solution)/shard_map/cond/branch_1_fun/ppermute | solution.py:41
  14.6 0.6 constant_dynamic-update-slice_fusion.3
  15.2 5.2 %collective-permute-done.2 = bf16[64,128]{1,0:T(8,128)(2,1)S(1)} collective-permute-done((bf16[64,128]{1,0:T(8,128)(2,1)S(1)}, bf16[64,128]{1,0:T(8,128)(2,1)S(1)}, u32[]{:S(2)}, u32[]{:S(2)}) %collective-permute-start.2) | collective-permute-done | bytes 16416 | tf_op jit(solution)/shard_map/cond/branch_1_fun/ppermute | solution.py:41
  20.4 4.3 %collective-permute-start.3 = (bf16[128,128]{1,0:T(8,128)(2,1)S(1)}, bf16[128,128]{1,0:T(8,128)(2,1)S(1)}, u32[]{:S(2)}, u32[]{:S(2)}) collective-permute-start(bf16[128,128]{1,0:T(8,128)(2,1)S(1)} %pad_maximum_fusion.1), channel_id=1, source_target_pairs={{0,256},{1,257},{2,258},{3,259},{4,260},{5,261},{6,262},{7,263},{8... | collective-permute-start | bytes 98312 | tf_op jit(solution)/shard_map/cond/branch_1_fun/ppermute | solution.py:41
  24.7 0.6 constant_dynamic-update-slice_fusion.2
  25.3 4.8 %collective-permute-done.3 = bf16[128,128]{1,0:T(8,128)(2,1)S(1)} collective-permute-done((bf16[128,128]{1,0:T(8,128)(2,1)S(1)}, bf16[128,128]{1,0:T(8,128)(2,1)S(1)}, u32[]{:S(2)}, u32[]{:S(2)}) %collective-permute-start.3) | collective-permute-done | bytes 32800 | tf_op jit(solution)/shard_map/cond/branch_1_fun/ppermute | solution.py:41
  30.1 5.1 %collective-permute-start.4 = (bf16[256,128]{1,0:T(8,128)(2,1)S(1)}, bf16[256,128]{1,0:T(8,128)(2,1)S(1)}, u32[]{:S(2)}, u32[]{:S(2)}) collective-permute-start(bf16[256,128]{1,0:T(8,128)(2,1)S(1)} %pad_maximum_fusion), channel_id=1, source_target_pairs={{0,2},{1,3},{2,0},{3,1},{4,6},{5,7},{6,4},{7,5},{8,10},{9,11},{10,... | collective-permute-start | bytes 196616 | tf_op jit(solution)/shard_map/cond/branch_1_fun/ppermute | solution.py:41
  35.2 0.6 constant_dynamic-update-slice_fusion.1
  35.8 10.9 %collective-permute-done.4 = bf16[256,128]{1,0:T(8,128)(2,1)S(1)} collective-permute-done((bf16[256,128]{1,0:T(8,128)(2,1)S(1)}, bf16[256,128]{1,0:T(8,128)(2,1)S(1)}, u32[]{:S(2)}, u32[]{:S(2)}) %collective-permute-start.4) | collective-permute-done | bytes 65568 | tf_op jit(solution)/shard_map/cond/branch_1_fun/ppermute | solution.py:41
  46.7 0.6 constant_dynamic-update-slice_fusion
  47.3 0.0 all-to-all-done.2
  47.3 4.8 %collective-permute-start.5 = (bf16[3072,128]{1,0:T(8,128)(2,1)}, bf16[3072,128]{1,0:T(8,128)(2,1)S(1)}, u32[]{:S(2)}, u32[]{:S(2)}) collective-permute-start(bf16[3072,128]{1,0:T(8,128)(2,1)} %get-tuple-element.52), channel_id=1, source_target_pairs={{0,2},{1,3},{2,0},{3,1},{4,6},{5,7},{6,4},{7,5},{8,10},{9,11},{10,... | collective-permute-start | bytes 2359304 | tf_op jit(solution)/shard_map/ppermute | solution.py:41
  52.1 32.7 %conditional.3 = (bf16[4,192,256]{2,1,0:T(8,128)(2,1)}, f32[192,1024]{1,0:T(8,128)S(1)}, f32[8,1024]{1,0:T(8,128)S(1)}, f32[192,1024]{1,0:T(8,128)S(1)}, f32[16,1024]{1,0:T(8,128)S(1)}) conditional(s32[]{:T(128)} %convert_element_type.4, () %tuple.23, (bf16[4,192,256]{2,1,0:T(8,128)(2,1)}, bf16[512,128]{1,0:T(8,128)(2,1)}, ...), branch_computations={%region_2.0_spmd, %region_3.0_spmd} | conditional | flops 1 | bytes 6684817 | solution.py:399
  52.1 4.8 %all-to-all-start = ((bf16[4,192,256]{2,1,0:T(8,128)(2,1)}), bf16[4,192,256]{2,1,0:T(8,128)(2,1)}, u32[]{:S(2)}, u32[]{:S(2)}) async-start(bf16[4,192,256]{2,1,0:T(8,128)(2,1)} %get-tuple-element.20), calls=%async_computation | async-start | bytes 786432 | tf_op jit(solution)/shard_map/cond/branch_1_fun/all_to_all | solution.py:388
  56.9 1.9 %collective-permute-start = (bf16[3072,128]{1,0:T(8,128)(2,1)}, bf16[3072,128]{1,0:T(8,128)(2,1)S(1)}, u32[]{:S(2)}, u32[]{:S(2)}) collective-permute-start(bf16[3072,128]{1,0:T(8,128)(2,1)} %get-tuple-element.22.refs_0_), channel_id=1, source_target_pairs={{0,1},{1,0},{2,3},{3,2},{4,5},{5,4},{6,7},{7,6},{8,9},{9,8},{10,11... | collective-permute-start | bytes 2359304 | tf_op jit(solution)/shard_map/cond/branch_1_fun/ppermute | solution.py:41
  58.8 1.9 %spread.1 = bf16[32,96,128]{2,1,0:T(8,128)(2,1)} custom-call(bf16[512,128]{1,0:T(8,128)(2,1)} %get-tuple-element.21.rows_ref), custom_call_target="tpu_custom_call" | custom-call | flops 1 | bytes 1 | tf_op jit(solution)/shard_map/cond/branch_1_fun/spread/pallas_call | solution.py:141
  60.7 3.7 %all-to-all-done.q_ref = bf16[4,192,256]{2,1,0:T(8,128)(2,1)} async-done(((bf16[4,192,256]{2,1,0:T(8,128)(2,1)}), bf16[4,192,256]{2,1,0:T(8,128)(2,1)}, u32[]{:S(2)}, u32[]{:S(2)}) %all-to-all-start) | async-done | bytes 393248 | tf_op jit(solution)/shard_map/cond/branch_1_fun/all_to_all | solution.py:388
  64.4 5.6 %all-to-all-start.1 = ((bf16[32,96,128]{2,1,0:T(8,128)(2,1)}), bf16[32,96,128]{2,1,0:T(8,128)(2,1)S(1)}, u32[]{:S(2)}, u32[]{:S(2)}) async-start(bf16[32,96,128]{2,1,0:T(8,128)(2,1)} %spread.1), calls=%async_computation.1 | async-start | bytes 1572864 | tf_op jit(solution)/shard_map/cond/branch_1_fun/all_to_all | solution.py:387
  70.0 0.0 collective-permute-done.refs_1_
  70.0 10.6 %near.2 = (f32[192,1024]{1,0:T(8,128)S(1)}, f32[8,1024]{1,0:T(8,128)S(1)}) custom-call(bf16[4,192,256]{2,1,0:T(8,128)(2,1)} %all-to-all-done.q_ref, bf16[3072,128]{1,0:T(8,128)(2,1)} %get-tuple-element.22.refs_0_, bf16[3072,128]{1,0:T(8,128)(2,1)S(1)} %collective-permute-done.refs_1_), custom_call_target="tpu_custom_call" | custom-call | tf_op jit(solution)/shard_map/cond/branch_1_fun/near/pallas_call | solution.py:261
  80.6 1.4 all-to-all-done.1.rows_ref
  82.0 2.8 %far.1 = (f32[192,1024]{1,0:T(8,128)S(1)}, f32[16,1024]{1,0:T(8,128)S(1)}) custom-call(s32[1]{0:T(128)} %bitcast.1.y_ref, bf16[4,192,256]{2,1,0:T(8,128)(2,1)} %all-to-all-done.q_ref, bf16[32,96,128]{2,1,0:T(8,128)(2,1)S(1)} %all-to-all-done.1.rows_ref), custom_call_target="tpu_custom_call" | custom-call | tf_op jit(solution)/shard_map/cond/branch_1_fun/far/pallas_call | solution.py:348
  84.9 37.9 %collective-permute-done.5.refs_0_ = bf16[3072,128]{1,0:T(8,128)(2,1)S(1)} collective-permute-done((bf16[3072,128]{1,0:T(8,128)(2,1)}, bf16[3072,128]{1,0:T(8,128)(2,1)S(1)}, u32[]{:S(2)}, u32[]{:S(2)}) %collective-permute-start.5) | collective-permute-done | bytes 786464 | tf_op jit(solution)/shard_map/ppermute | solution.py:41
  122.7 2.1 %collective-permute-start.6 = (bf16[3072,128]{1,0:T(8,128)(2,1)S(1)}, bf16[3072,128]{1,0:T(8,128)(2,1)S(1)}, u32[]{:S(2)}, u32[]{:S(2)}) collective-permute-start(bf16[3072,128]{1,0:T(8,128)(2,1)S(1)} %collective-permute-done.5.refs_0_), channel_id=1, source_target_pairs={{0,1},{1,0},{2,3},{3,2},{4,5},{5,4},{6,7},{7,6},{8,9},{9,8},{10,11... | collective-permute-start | bytes 2359304 | tf_op jit(solution)/shard_map/ppermute | solution.py:41
  124.8 6.2 %near.3 = (f32[192,1024]{1,0:T(8,128)S(1)}, f32[8,1024]{1,0:T(8,128)S(1)}) custom-call(bf16[4,192,256]{2,1,0:T(8,128)(2,1)} %get-tuple-element.53.q_ref, bf16[3072,128]{1,0:T(8,128)(2,1)S(1)} %collective-permute-done.5.refs_0_, f32[192,1024]{1,0:T(8,128)S(1)} %get-tuple-element.59.refs_1_, f32[8,1024]{1,0:T(8,128)S(1)} %get-tuple-element.60.refs_2_), custom_call_target="tpu_custom_call" | custom-call | tf_op jit(solution)/shard_map/near/pallas_call | solution.py:261
  131.0 0.0 collective-permute-done.6.refs_0_
  131.0 5.9 %last.1 = bf16[4,192,256]{2,1,0:T(8,128)(2,1)S(1)} custom-call(bf16[4,192,256]{2,1,0:T(8,128)(2,1)} %get-tuple-element.53.q_ref, bf16[3072,128]{1,0:T(8,128)(2,1)S(1)} %collective-permute-done.6.refs_0_, f32[192,1024]{1,0:T(8,128)S(1)} %get-tuple-element.61.refs_1_, f32[8,1024]{1,0:T(8,128)S(1)} %get-tuple-element.62.refs_2_, ...), custom_call_target="tpu_custom_call" | custom-call | tf_op jit(solution)/shard_map/last/pallas_call | solution.py:261
  136.9 12.5 %all_to_all.17 = bf16[4,192,256]{2,1,0:T(8,128)(2,1)S(1)} all-to-all(bf16[4,192,256]{2,1,0:T(8,128)(2,1)S(1)} %last.1), channel_id=1, replica_groups=mesh['zl'=8,'x'=4,'y'=4,'zh'=2,'core'=2] {'y'}, dimensions={0} | all-to-all | bytes 786432 | tf_op jit(solution)/shard_map/all_to_all | solution.py:415
  149.4 0.9 turn.1
  (3 shorter events, 0.0 us)
Async XLA Ops:
  2.6 10.1 %collective-permute-start.1 = (bf16[32,128]{1,0:T(8,128)(2,1)S(1)}, bf16[32,128]{1,0:T(8,128)(2,1)S(1)}, u32[]{:S(2)}, u32[]{:S(2)}) collective-permute-start(bf16[32,128]{1,0:T(8,128)(2,1)S(1)} %get-tuple-element.19), channel_id=1, source_target_pairs={{0,64},{1,65},{2,66},{3,67},{4,68},{5,69},{6,70},{7,71},{8,72},{9,... | collective-permute-start | bytes 24584 | tf_op jit(solution)/shard_map/cond/branch_1_fun/ppermute | solution.py:41
  7.6 39.7 %all-to-all-start.2 = ((bf16[4,768,128]{2,1,0:T(8,128)(2,1)}), bf16[4,768,128]{2,1,0:T(8,128)(2,1)}, u32[]{:S(2)}, u32[]{:S(2)}) async-start(bf16[4,768,128]{2,1,0:T(8,128)(2,1)} %get-tuple-element.18), calls=%async_computation.2 | async-start | bytes 1572864 | tf_op jit(solution)/shard_map/cond/branch_1_fun/all_to_all | solution.py:380
  12.7 7.7 %collective-permute-start.2 = (bf16[64,128]{1,0:T(8,128)(2,1)S(1)}, bf16[64,128]{1,0:T(8,128)(2,1)S(1)}, u32[]{:S(2)}, u32[]{:S(2)}) collective-permute-start(bf16[64,128]{1,0:T(8,128)(2,1)S(1)} %pad_maximum_fusion.2), channel_id=1, source_target_pairs={{0,386},{1,387},{2,384},{3,385},{4,390},{5,391},{6,388},{7,389},{8... | collective-permute-start | bytes 49160 | tf_op jit(solution)/shard_map/cond/branch_1_fun/ppermute | solution.py:41
  20.4 9.7 %collective-permute-start.3 = (bf16[128,128]{1,0:T(8,128)(2,1)S(1)}, bf16[128,128]{1,0:T(8,128)(2,1)S(1)}, u32[]{:S(2)}, u32[]{:S(2)}) collective-permute-start(bf16[128,128]{1,0:T(8,128)(2,1)S(1)} %pad_maximum_fusion.1), channel_id=1, source_target_pairs={{0,256},{1,257},{2,258},{3,259},{4,260},{5,261},{6,262},{7,263},{8... | collective-permute-start | bytes 98312 | tf_op jit(solution)/shard_map/cond/branch_1_fun/ppermute | solution.py:41
  30.1 16.6 %collective-permute-start.4 = (bf16[256,128]{1,0:T(8,128)(2,1)S(1)}, bf16[256,128]{1,0:T(8,128)(2,1)S(1)}, u32[]{:S(2)}, u32[]{:S(2)}) collective-permute-start(bf16[256,128]{1,0:T(8,128)(2,1)S(1)} %pad_maximum_fusion), channel_id=1, source_target_pairs={{0,2},{1,3},{2,0},{3,1},{4,6},{5,7},{6,4},{7,5},{8,10},{9,11},{10,... | collective-permute-start | bytes 196616 | tf_op jit(solution)/shard_map/cond/branch_1_fun/ppermute | solution.py:41
  47.3 75.4 %collective-permute-start.5 = (bf16[3072,128]{1,0:T(8,128)(2,1)}, bf16[3072,128]{1,0:T(8,128)(2,1)S(1)}, u32[]{:S(2)}, u32[]{:S(2)}) collective-permute-start(bf16[3072,128]{1,0:T(8,128)(2,1)} %get-tuple-element.52), channel_id=1, source_target_pairs={{0,2},{1,3},{2,0},{3,1},{4,6},{5,7},{6,4},{7,5},{8,10},{9,11},{10,... | collective-permute-start | bytes 2359304 | tf_op jit(solution)/shard_map/ppermute | solution.py:41
  52.1 12.3 %all-to-all-start = ((bf16[4,192,256]{2,1,0:T(8,128)(2,1)}), bf16[4,192,256]{2,1,0:T(8,128)(2,1)}, u32[]{:S(2)}, u32[]{:S(2)}) async-start(bf16[4,192,256]{2,1,0:T(8,128)(2,1)} %get-tuple-element.20), calls=%async_computation | async-start | bytes 786432 | tf_op jit(solution)/shard_map/cond/branch_1_fun/all_to_all | solution.py:388
  56.9 13.1 %collective-permute-start = (bf16[3072,128]{1,0:T(8,128)(2,1)}, bf16[3072,128]{1,0:T(8,128)(2,1)S(1)}, u32[]{:S(2)}, u32[]{:S(2)}) collective-permute-start(bf16[3072,128]{1,0:T(8,128)(2,1)} %get-tuple-element.22.refs_0_), channel_id=1, source_target_pairs={{0,1},{1,0},{2,3},{3,2},{4,5},{5,4},{6,7},{7,6},{8,9},{9,8},{10,11... | collective-permute-start | bytes 2359304 | tf_op jit(solution)/shard_map/cond/branch_1_fun/ppermute | solution.py:41
  64.4 17.6 %all-to-all-start.1 = ((bf16[32,96,128]{2,1,0:T(8,128)(2,1)}), bf16[32,96,128]{2,1,0:T(8,128)(2,1)S(1)}, u32[]{:S(2)}, u32[]{:S(2)}) async-start(bf16[32,96,128]{2,1,0:T(8,128)(2,1)} %spread.1), calls=%async_computation.1 | async-start | bytes 1572864 | tf_op jit(solution)/shard_map/cond/branch_1_fun/all_to_all | solution.py:387
  122.7 8.3 %collective-permute-start.6 = (bf16[3072,128]{1,0:T(8,128)(2,1)S(1)}, bf16[3072,128]{1,0:T(8,128)(2,1)S(1)}, u32[]{:S(2)}, u32[]{:S(2)}) collective-permute-start(bf16[3072,128]{1,0:T(8,128)(2,1)S(1)} %collective-permute-done.5.refs_0_), channel_id=1, source_target_pairs={{0,1},{1,0},{2,3},{3,2},{4,5},{5,4},{6,7},{7,6},{8,9},{9,8},{10,11... | collective-permute-start | bytes 2359304 | tf_op jit(solution)/shard_map/ppermute | solution.py:41

commit v8 on v4

--- a/solution.py
+++ b/solution.py
@@ -418,6 +418,9 @@
 
 def body(queries, keys, values):
     y = lax.axis_index("y").astype(jnp.int32).reshape(1)
+    queries, keys, values = (
+        pltpu.with_memory_space_constraint(a, pltpu.HBM) for a in (queries, keys, values)
+    )
     far_rows, own_kv, staged, q = prep(y, queries, keys, values)
     crossed_own = move(own_kv, dz=8)
     all_kv, away, far_rows = branch(y, exchange, y, staged, far_rows)

time: 136 us -> 133 us (0.978)
  the two profiles are of different devices: /device:TPU:38 before, /device:TPU:34 now
where the time goes in v8:
time: 133 us; the launch traced here: 132 us
  starting transfers between devices  39.6 us (30%)
  Pallas kernels  33.9 us (25%)
  waiting for transfers between devices  30.3 us (23%)
  blocking collectives  27.8 us (21%)
    pallas_call x3, Pallas kernels, near(): pl.pallas_call(functools.partial(near_kernel, counts, state is not None,...  24 us
    ppermute x5, starting transfers between devices, move(): return lax.ppermute(array, AXES, route(**step))  23.8 us
    all_to_all x1, blocking collectives, exchange(): got = lax.all_to_all(staged, 'y', 0, 0, tiled=True)  16.4 us
    ppermute x5, waiting for transfers between devices, move(): return lax.ppermute(array, AXES, route(**step))  13.9 us
    all_to_all x1, waiting for transfers between devices, exchange(): far_rows = lax.all_to_all(far_rows, ('zl', 'zh'), 0, 0, tiled=True)  12.8 us
    all_to_all x1, blocking collectives, body(): back = lax.all_to_all(result, 'y', 0, 0, tiled=True)  11.4 us
    all_to_all x1, starting transfers between devices, exchange(): far_rows = lax.all_to_all(far_rows, ('zl', 'zh'), 0, 0, tiled=True)  6.04 us
    all_to_all x1, starting transfers between devices, beside(): lax.all_to_all(spread(far_rows), ('x', 'y', 'core'), 0, 0, tiled=True)  5.6 us
  transfers between devices with their start and end apart: 8, of which 4 were waited for; matrix products, arithmetic and copies ran while one was open for 0% of the time, Pallas kernels for 19%

profile of v8, /device:TPU:34, one launch (start us, length us, event | category | flops | bytes accessed | tf_op | source)
XLA Modules:
  0.0 132.4 jit_solution(6894676487185991398)
XLA Ops:
  0.0 2.3 %prep.1 = (bf16[16,32,128]{2,1,0:T(8,128)(2,1)}, bf16[768,128]{1,0:T(8,128)(2,1)S(1)}, bf16[4,768,128]{2,1,0:T(8,128)(2,1)S(1)}, bf16[4,192,256]{2,1,0:T(8,128)(2,1)}) custom-call(s32[1]{0:T(128)} %bitcast.1.y_ref, bf16[256,768]{1,0:T(8,128)(2,1)} %q_hbm.1, bf16[256,768]{1,0:T(8,128)(2,1)} %k_hbm.1, bf16[256,768]{1,0:T(8,128)(2,1)} %v_hbm.1), custom_call_target="tpu_custom_call" | custom-call | tf_op jit(solution)/shard_map/prep/pallas_call | solution.py:117
  2.3 14.8 %collective-permute-start.2 = (bf16[768,128]{1,0:T(8,128)(2,1)S(1)}, bf16[768,128]{1,0:T(8,128)(2,1)S(1)}, u32[]{:S(2)}, u32[]{:S(2)}) collective-permute-start(bf16[768,128]{1,0:T(8,128)(2,1)S(1)} %get-tuple-element.63), channel_id=1, source_target_pairs={{0,2},{1,3},{2,0},{3,1},{4,6},{5,7},{6,4},{7,5},{8,10},{9,11},{10,... | collective-permute-start | bytes 589832 | tf_op jit(solution)/shard_map/ppermute | solution.py:41
  17.2 36.4 %conditional.2 = (bf16[3072,128]{1,0:T(8,128)(2,1)}, bf16[2304,128]{1,0:T(8,128)(2,1)S(1)}, bf16[16,32,128]{2,1,0:T(8,128)(2,1)}) conditional(s32[]{:T(128)} %convert_element_type.4, () %tuple.25, (bf16[4,768,128]{2,1,0:T(8,128)(2,1)S(1)}, s32[1]{0:T(128)}, bf16[16,32,128]{2,1,0:T(8,128)(2,1)}) %tuple.26), branch_computations={%region_0.0_spmd, %region_1.0_spmd} | conditional | flops 1 | bytes 1966137 | solution.py:416
  17.2 16.4 %all_to_all.21.got = bf16[4,768,128]{2,1,0:T(8,128)(2,1)} all-to-all(bf16[4,768,128]{2,1,0:T(8,128)(2,1)S(1)} %get-tuple-element.21), channel_id=1, replica_groups=mesh['zl'=8,'x'=4,'y'=4,'zh'=2,'core'=2] {'y'}, dimensions={0} | all-to-all | bytes 1572864 | tf_op jit(solution)/shard_map/cond/branch_1_fun/all_to_all | solution.py:398
  33.6 6.0 %all-to-all-start.1 = ((bf16[16,32,128]{2,1,0:T(8,128)(2,1)}), bf16[16,32,128]{2,1,0:T(8,128)(2,1)}, u32[]{:S(2)}, u32[]{:S(2)}) async-start(bf16[16,32,128]{2,1,0:T(8,128)(2,1)} %get-tuple-element.23), calls=%async_computation.1 | async-start | bytes 262144 | tf_op jit(solution)/shard_map/cond/branch_1_fun/all_to_all | solution.py:397
  39.6 1.2 sort.1
  40.8 12.8 %all-to-all-done.1 = bf16[16,32,128]{2,1,0:T(8,128)(2,1)} async-done(((bf16[16,32,128]{2,1,0:T(8,128)(2,1)}), bf16[16,32,128]{2,1,0:T(8,128)(2,1)}, u32[]{:S(2)}, u32[]{:S(2)}) %all-to-all-start.1) | async-done | bytes 131104 | tf_op jit(solution)/shard_map/cond/branch_1_fun/all_to_all | solution.py:397
  53.5 0.0 collective-permute-done.2
  53.5 2.9 %collective-permute-start.3 = (bf16[2304,128]{1,0:T(8,128)(2,1)S(1)}, bf16[2304,128]{1,0:T(8,128)(2,1)S(1)}, u32[]{:S(2)}, u32[]{:S(2)}) collective-permute-start(bf16[2304,128]{1,0:T(8,128)(2,1)S(1)} %get-tuple-element.66), channel_id=1, source_target_pairs={{0,2},{1,3},{2,0},{3,1},{4,6},{5,7},{6,4},{7,5},{8,10},{9,11},{10,... | collective-permute-start | bytes 1769480 | tf_op jit(solution)/shard_map/ppermute | solution.py:41
  56.5 38.5 %conditional.3 = (bf16[4,192,256]{2,1,0:T(8,128)(2,1)}, f32[192,1024]{1,0:T(8,128)S(1)}, f32[8,1024]{1,0:T(8,128)}, f32[192,1024]{1,0:T(8,128)}, f32[16,1024]{1,0:T(8,128)}) conditional(s32[]{:T(128)} %convert_element_type.4, () %tuple.24, (bf16[4,192,256]{2,1,0:T(8,128)(2,1)}, bf16[16,32,128]{2,1,0:T(8,128)(2,1)}, bf16[3072,128]{1,0:T(8,128)(2,1)}, ...), branch_computations={%region_2.0_spmd, %region_3.0_spmd} | conditional | flops 1 | bytes 9044209 | solution.py:416
  56.5 0.0 copy-start
  56.5 0.7 copy-done
  57.1 4.1 %all-to-all-start.2 = ((bf16[4,192,256]{2,1,0:T(8,128)(2,1)}), bf16[4,192,256]{2,1,0:T(8,128)(2,1)}, u32[]{:S(2)}, u32[]{:S(2)}) async-start(bf16[4,192,256]{2,1,0:T(8,128)(2,1)} %get-tuple-element.24), calls=%async_computation.2 | async-start | bytes 786432 | tf_op jit(solution)/shard_map/cond/branch_1_fun/all_to_all | solution.py:404
  61.3 1.9 %collective-permute-start = (bf16[3072,128]{1,0:T(8,128)(2,1)}, bf16[3072,128]{1,0:T(8,128)(2,1)S(1)}, u32[]{:S(2)}, u32[]{:S(2)}) collective-permute-start(bf16[3072,128]{1,0:T(8,128)(2,1)} %get-tuple-element.26.refs_0_), channel_id=1, source_target_pairs={{0,1},{1,0},{2,3},{3,2},{4,5},{5,4},{6,7},{7,6},{8,9},{9,8},{10,11... | collective-permute-start | bytes 2359304 | tf_op jit(solution)/shard_map/cond/branch_1_fun/ppermute | solution.py:41
  63.2 1.9 %spread.1 = bf16[32,96,128]{2,1,0:T(8,128)(2,1)} custom-call(bf16[16,32,128]{2,1,0:T(8,128)(2,1)} %get-tuple-element.25.rows_ref), custom_call_target="tpu_custom_call" | custom-call | flops 1 | bytes 1 | tf_op jit(solution)/shard_map/cond/branch_1_fun/spread/pallas_call | solution.py:162
  65.0 0.0 copy-start.1
  65.0 3.7 %all-to-all-done.2.q_ref = bf16[4,192,256]{2,1,0:T(8,128)(2,1)} async-done(((bf16[4,192,256]{2,1,0:T(8,128)(2,1)}), bf16[4,192,256]{2,1,0:T(8,128)(2,1)}, u32[]{:S(2)}, u32[]{:S(2)}) %all-to-all-start.2) | async-done | bytes 393248 | tf_op jit(solution)/shard_map/cond/branch_1_fun/all_to_all | solution.py:404
  68.7 5.6 %all-to-all-start.3 = ((bf16[32,96,128]{2,1,0:T(8,128)(2,1)}), bf16[32,96,128]{2,1,0:T(8,128)(2,1)S(1)}, u32[]{:S(2)}, u32[]{:S(2)}) async-start(bf16[32,96,128]{2,1,0:T(8,128)(2,1)} %spread.1), calls=%async_computation.3 | async-start | bytes 1572864 | tf_op jit(solution)/shard_map/cond/branch_1_fun/all_to_all | solution.py:403
  74.3 0.0 copy-done.1
  74.3 2.1 %collective-permute-start.1 = (bf16[768,128]{1,0:T(8,128)(2,1)S(1)}, bf16[768,128]{1,0:T(8,128)(2,1)S(1)}, u32[]{:S(2)}, u32[]{:S(2)}) collective-permute-start(bf16[768,128]{1,0:T(8,128)(2,1)S(1)} %copy-done.1), channel_id=1, source_target_pairs={{0,1},{1,0},{2,3},{3,2},{4,5},{5,4},{6,7},{7,6},{8,9},{9,8},{10,11... | collective-permute-start | bytes 589832 | tf_op jit(solution)/shard_map/cond/branch_1_fun/ppermute | solution.py:41
  76.4 1.3 collective-permute-done.1.refs_3_
  77.7 0.0 collective-permute-done.refs_1_
  77.7 13.6 %near.2 = (f32[192,1024]{1,0:T(8,128)S(1)}, f32[8,1024]{1,0:T(8,128)}) custom-call(bf16[4,192,256]{2,1,0:T(8,128)(2,1)} %all-to-all-done.2.q_ref, bf16[3072,128]{1,0:T(8,128)(2,1)} %get-tuple-element.26.refs_0_, bf16[3072,128]{1,0:T(8,128)(2,1)S(1)} %collective-permute-done.refs_1_, bf16[768,128]{1,0:T(8,128)(2,1)} %copy-done, ...), custom_call_target="tpu_custom_call" | custom-call | tf_op jit(solution)/shard_map/cond/branch_1_fun/near/pallas_call | solution.py:282
  91.3 0.0 all-to-all-done.3.rows_ref
  91.3 3.7 %far.1 = (f32[192,1024]{1,0:T(8,128)}, f32[16,1024]{1,0:T(8,128)}) custom-call(s32[1]{0:T(128)} %get-tuple-element.32.y_ref, bf16[4,192,256]{2,1,0:T(8,128)(2,1)} %all-to-all-done.2.q_ref, bf16[32,96,128]{2,1,0:T(8,128)(2,1)S(1)} %all-to-all-done.3.rows_ref), custom_call_target="tpu_custom_call" | custom-call | tf_op jit(solution)/shard_map/cond/branch_1_fun/far/pallas_call | solution.py:369
  95.0 12.7 %collective-permute-done.3.refs_0_ = bf16[2304,128]{1,0:T(8,128)(2,1)S(1)} collective-permute-done((bf16[2304,128]{1,0:T(8,128)(2,1)S(1)}, bf16[2304,128]{1,0:T(8,128)(2,1)S(1)}, u32[]{:S(2)}, u32[]{:S(2)}) %collective-permute-start.3) | collective-permute-done | bytes 589856 | tf_op jit(solution)/shard_map/ppermute | solution.py:41
  107.6 2.1 %collective-permute-start.4 = (bf16[2304,128]{1,0:T(8,128)(2,1)S(1)}, bf16[2304,128]{1,0:T(8,128)(2,1)S(1)}, u32[]{:S(2)}, u32[]{:S(2)}) collective-permute-start(bf16[2304,128]{1,0:T(8,128)(2,1)S(1)} %collective-permute-done.3.refs_0_), channel_id=1, source_target_pairs={{0,1},{1,0},{2,3},{3,2},{4,5},{5,4},{6,7},{7,6},{8,9},{9,8},{10,11... | collective-permute-start | bytes 1769480 | tf_op jit(solution)/shard_map/ppermute | solution.py:41
  109.7 5.2 %near.3 = (f32[192,1024]{1,0:T(8,128)S(1)}, f32[8,1024]{1,0:T(8,128)S(1)}) custom-call(bf16[4,192,256]{2,1,0:T(8,128)(2,1)} %get-tuple-element.65.q_ref, bf16[2304,128]{1,0:T(8,128)(2,1)S(1)} %collective-permute-done.3.refs_0_, f32[192,1024]{1,0:T(8,128)S(1)} %get-tuple-element.72.refs_1_, f32[8,1024]{1,0:T(8,128)} %get-tuple-element.73.refs_2_), custom_call_target="tpu_custom_call" | custom-call | tf_op jit(solution)/shard_map/near/pallas_call | solution.py:282
  114.9 0.0 collective-permute-done.4.refs_0_
  114.9 5.1 %last.1 = bf16[4,192,256]{2,1,0:T(8,128)(2,1)S(1)} custom-call(bf16[4,192,256]{2,1,0:T(8,128)(2,1)} %get-tuple-element.65.q_ref, bf16[2304,128]{1,0:T(8,128)(2,1)S(1)} %collective-permute-done.4.refs_0_, f32[192,1024]{1,0:T(8,128)S(1)} %get-tuple-element.74.refs_1_, f32[8,1024]{1,0:T(8,128)S(1)} %get-tuple-element.75.refs_2_, ...), custom_call_target="tpu_custom_call" | custom-call | tf_op jit(solution)/shard_map/last/pallas_call | solution.py:282
  120.1 11.4 %all_to_all.22 = bf16[4,192,256]{2,1,0:T(8,128)(2,1)S(1)} all-to-all(bf16[4,192,256]{2,1,0:T(8,128)(2,1)S(1)} %last.1), channel_id=1, replica_groups=mesh['zl'=8,'x'=4,'y'=4,'zh'=2,'core'=2] {'y'}, dimensions={0} | all-to-all | bytes 786432 | tf_op jit(solution)/shard_map/all_to_all | solution.py:434
  131.5 0.9 turn.1
Async XLA Ops:
  2.3 51.2 %collective-permute-start.2 = (bf16[768,128]{1,0:T(8,128)(2,1)S(1)}, bf16[768,128]{1,0:T(8,128)(2,1)S(1)}, u32[]{:S(2)}, u32[]{:S(2)}) collective-permute-start(bf16[768,128]{1,0:T(8,128)(2,1)S(1)} %get-tuple-element.63), channel_id=1, source_target_pairs={{0,2},{1,3},{2,0},{3,1},{4,6},{5,7},{6,4},{7,5},{8,10},{9,11},{10,... | collective-permute-start | bytes 589832 | tf_op jit(solution)/shard_map/ppermute | solution.py:41
  33.6 20.0 %all-to-all-start.1 = ((bf16[16,32,128]{2,1,0:T(8,128)(2,1)}), bf16[16,32,128]{2,1,0:T(8,128)(2,1)}, u32[]{:S(2)}, u32[]{:S(2)}) async-start(bf16[16,32,128]{2,1,0:T(8,128)(2,1)} %get-tuple-element.23), calls=%async_computation.1 | async-start | bytes 262144 | tf_op jit(solution)/shard_map/cond/branch_1_fun/all_to_all | solution.py:397
  53.5 54.1 %collective-permute-start.3 = (bf16[2304,128]{1,0:T(8,128)(2,1)S(1)}, bf16[2304,128]{1,0:T(8,128)(2,1)S(1)}, u32[]{:S(2)}, u32[]{:S(2)}) collective-permute-start(bf16[2304,128]{1,0:T(8,128)(2,1)S(1)} %get-tuple-element.66), channel_id=1, source_target_pairs={{0,2},{1,3},{2,0},{3,1},{4,6},{5,7},{6,4},{7,5},{8,10},{9,11},{10,... | collective-permute-start | bytes 1769480 | tf_op jit(solution)/shard_map/ppermute | solution.py:41
  56.5 0.7 copy-start
  57.1 11.6 %all-to-all-start.2 = ((bf16[4,192,256]{2,1,0:T(8,128)(2,1)}), bf16[4,192,256]{2,1,0:T(8,128)(2,1)}, u32[]{:S(2)}, u32[]{:S(2)}) async-start(bf16[4,192,256]{2,1,0:T(8,128)(2,1)} %get-tuple-element.24), calls=%async_computation.2 | async-start | bytes 786432 | tf_op jit(solution)/shard_map/cond/branch_1_fun/all_to_all | solution.py:404
  61.3 16.4 %collective-permute-start = (bf16[3072,128]{1,0:T(8,128)(2,1)}, bf16[3072,128]{1,0:T(8,128)(2,1)S(1)}, u32[]{:S(2)}, u32[]{:S(2)}) collective-permute-start(bf16[3072,128]{1,0:T(8,128)(2,1)} %get-tuple-element.26.refs_0_), channel_id=1, source_target_pairs={{0,1},{1,0},{2,3},{3,2},{4,5},{5,4},{6,7},{7,6},{8,9},{9,8},{10,11... | collective-permute-start | bytes 2359304 | tf_op jit(solution)/shard_map/cond/branch_1_fun/ppermute | solution.py:41
  65.0 9.3 %copy-start.1 = (bf16[768,128]{1,0:T(8,128)(2,1)S(1)}, bf16[768,128]{1,0:T(8,128)(2,1)}, u32[]{:S(2)}) copy-start(bf16[768,128]{1,0:T(8,128)(2,1)} %copy-done) | copy-start | bytes 589828 | tf_op jit(solution)/shard_map/cond
  68.7 22.6 %all-to-all-start.3 = ((bf16[32,96,128]{2,1,0:T(8,128)(2,1)}), bf16[32,96,128]{2,1,0:T(8,128)(2,1)S(1)}, u32[]{:S(2)}, u32[]{:S(2)}) async-start(bf16[32,96,128]{2,1,0:T(8,128)(2,1)} %spread.1), calls=%async_computation.3 | async-start | bytes 1572864 | tf_op jit(solution)/shard_map/cond/branch_1_fun/all_to_all | solution.py:403
  74.3 3.3 %collective-permute-start.1 = (bf16[768,128]{1,0:T(8,128)(2,1)S(1)}, bf16[768,128]{1,0:T(8,128)(2,1)S(1)}, u32[]{:S(2)}, u32[]{:S(2)}) collective-permute-start(bf16[768,128]{1,0:T(8,128)(2,1)S(1)} %copy-done.1), channel_id=1, source_target_pairs={{0,1},{1,0},{2,3},{3,2},{4,5},{5,4},{6,7},{7,6},{8,9},{9,8},{10,11... | collective-permute-start | bytes 589832 | tf_op jit(solution)/shard_map/cond/branch_1_fun/ppermute | solution.py:41
  107.6 7.3 %collective-permute-start.4 = (bf16[2304,128]{1,0:T(8,128)(2,1)S(1)}, bf16[2304,128]{1,0:T(8,128)(2,1)S(1)}, u32[]{:S(2)}, u32[]{:S(2)}) collective-permute-start(bf16[2304,128]{1,0:T(8,128)(2,1)S(1)} %collective-permute-done.3.refs_0_), channel_id=1, source_target_pairs={{0,1},{1,0},{2,3},{3,2},{4,5},{5,4},{6,7},{7,6},{8,9},{9,8},{10,11... | collective-permute-start | bytes 1769480 | tf_op jit(solution)/shard_map/ppermute | solution.py:41

commit v9 on v8

--- a/solution.py
+++ b/solution.py
@@ -393,19 +393,20 @@
     )(array)
 
 
-def exchange(y, staged, far_rows):
+def exchange(y, staged):
+    got = lax.all_to_all(staged, "y", 0, 0, tiled=True)
+    return got.reshape(4 * KV, 128), sort(y, got)
+
+
+def beside(y, q, all_kv, crossed_own, far_rows):
+    q = lax.all_to_all(q, "y", 0, 0, tiled=True)
+    q, far_rows = lax.optimization_barrier((q, far_rows))
     far_rows = lax.all_to_all(far_rows, ("zl", "zh"), 0, 0, tiled=True)
-    got = lax.all_to_all(staged, "y", 0, 0, tiled=True)
-    return got.reshape(4 * KV, 128), sort(y, got), far_rows
-
-
-def beside(y, q, all_kv, crossed_own, far_rows):
-    far_rows = lax.all_to_all(spread(far_rows), ("x", "y", "core"), 0, 0, tiled=True)
-    q = lax.all_to_all(q, "y", 0, 0, tiled=True)
     partner_kv = move(all_kv, flip=1)
     partner_own = move(crossed_own, flip=1)
     state = near(q, [all_kv, partner_kv, crossed_own, partner_own])
     far_rows, *state = lax.optimization_barrier((far_rows, *state))
+    far_rows = lax.all_to_all(spread(far_rows), ("x", "y", "core"), 0, 0, tiled=True)
     return q, tuple(state), tuple(far(y, q, far_rows))
 
 
@@ -423,7 +424,7 @@
     )
     far_rows, own_kv, staged, q = prep(y, queries, keys, values)
     crossed_own = move(own_kv, dz=8)
-    all_kv, away, far_rows = branch(y, exchange, y, staged, far_rows)
+    all_kv, away = branch(y, exchange, y, staged)
     away, crossed_own = lax.optimization_barrier((away, crossed_own))
     crossed = move(away, dz=8)
     q, state, far_state = branch(y, beside, y, q, all_kv, crossed_own, far_rows)

time: 133 us -> 152 us (1.14)
  the two profiles are of different devices: /device:TPU:34 before, /device:TPU:1 now
where the time goes in v9:
time: 152 us; the launch traced here: 151 us
  starting transfers between devices  49.2 us (32%)
  blocking collectives  45.7 us (30%)
  Pallas kernels  31.3 us (21%)
  waiting for transfers between devices  24.9 us (16%)
    ppermute x5, starting transfers between devices, move(): return lax.ppermute(array, AXES, route(**step))  30.2 us
    pallas_call x3, Pallas kernels, near(): pl.pallas_call(functools.partial(near_kernel, counts, state is not None,...  23.2 us
    all_to_all x1, waiting for transfers between devices, beside(): far_rows = lax.all_to_all(far_rows, ('zl', 'zh'), 0, 0, tiled=True)  22.2 us
    all_to_all x1, blocking collectives, beside(): lax.all_to_all(spread(far_rows), ('x', 'y', 'core'), 0, 0, tiled=True)  20.4 us
    all_to_all x1, blocking collectives, exchange(): got = lax.all_to_all(staged, 'y', 0, 0, tiled=True)  14.9 us
    all_to_all x1, starting transfers between devices, beside(): far_rows = lax.all_to_all(far_rows, ('zl', 'zh'), 0, 0, tiled=True)  14.8 us
    all_to_all x1, blocking collectives, body(): back = lax.all_to_all(result, 'y', 0, 0, tiled=True)  10.3 us
    all_to_all x1, starting transfers between devices, beside(): q = lax.all_to_all(q, 'y', 0, 0, tiled=True)  4.12 us
  transfers between devices with their start and end apart: 7, of which 3 were waited for; matrix products, arithmetic and copies ran while one was open for 0% of the time, Pallas kernels for 15%

profile of v9, /device:TPU:1, one launch (start us, length us, event | category | flops | bytes accessed | tf_op | source)
XLA Modules:
  0.0 151.2 jit_solution(12766593013282504926)
XLA Ops:
  0.0 2.3 %prep.1 = (bf16[16,32,128]{2,1,0:T(8,128)(2,1)}, bf16[768,128]{1,0:T(8,128)(2,1)S(1)}, bf16[4,768,128]{2,1,0:T(8,128)(2,1)S(1)}, bf16[4,192,256]{2,1,0:T(8,128)(2,1)}) custom-call(s32[1]{0:T(128)} %bitcast.1.y_ref, bf16[256,768]{1,0:T(8,128)(2,1)} %q_hbm.1, bf16[256,768]{1,0:T(8,128)(2,1)} %k_hbm.1, bf16[256,768]{1,0:T(8,128)(2,1)} %v_hbm.1), custom_call_target="tpu_custom_call" | custom-call | tf_op jit(solution)/shard_map/prep/pallas_call | solution.py:117
  2.4 16.3 %collective-permute-start.2 = (bf16[768,128]{1,0:T(8,128)(2,1)S(1)}, bf16[768,128]{1,0:T(8,128)(2,1)S(1)}, u32[]{:S(2)}, u32[]{:S(2)}) collective-permute-start(bf16[768,128]{1,0:T(8,128)(2,1)S(1)} %get-tuple-element.60), channel_id=1, source_target_pairs={{0,2},{1,3},{2,0},{3,1},{4,6},{5,7},{6,4},{7,5},{8,10},{9,11},{10,... | collective-permute-start | bytes 589832 | tf_op jit(solution)/shard_map/ppermute | solution.py:41
  18.6 16.9 %conditional.2 = (bf16[3072,128]{1,0:T(8,128)(2,1)}, bf16[2304,128]{1,0:T(8,128)(2,1)}) conditional(s32[]{:T(128)} %convert_element_type.4, () %tuple.26, (bf16[4,768,128]{2,1,0:T(8,128)(2,1)S(1)}, s32[1]{0:T(128)}) %tuple.27), branch_computations={%region_0.0_spmd, %region_1.0_spmd} | conditional | flops 1 | bytes 1572881 | solution.py:417
  18.6 14.9 %all_to_all.21.got = bf16[4,768,128]{2,1,0:T(8,128)(2,1)} all-to-all(bf16[4,768,128]{2,1,0:T(8,128)(2,1)S(1)} %get-tuple-element.19), channel_id=1, replica_groups=mesh['zl'=8,'x'=4,'y'=4,'zh'=2,'core'=2] {'y'}, dimensions={0} | all-to-all | bytes 1572864 | tf_op jit(solution)/shard_map/cond/branch_1_fun/all_to_all | solution.py:397
  33.5 2.0 %sort.1 = bf16[2304,128]{1,0:T(8,128)(2,1)} custom-call(s32[1]{0:T(128)} %get-tuple-element.20.y_ref, bf16[4,768,128]{2,1,0:T(8,128)(2,1)} %all_to_all.21.got), custom_call_target="tpu_custom_call" | custom-call | flops 1 | bytes 1 | tf_op jit(solution)/shard_map/cond/branch_1_fun/sort/pallas_call | solution.py:135
  35.5 0.0 collective-permute-done.2
  35.5 1.9 %collective-permute-start.3 = (bf16[2304,128]{1,0:T(8,128)(2,1)}, bf16[2304,128]{1,0:T(8,128)(2,1)S(1)}, u32[]{:S(2)}, u32[]{:S(2)}) collective-permute-start(bf16[2304,128]{1,0:T(8,128)(2,1)} %get-tuple-element.63), channel_id=1, source_target_pairs={{0,2},{1,3},{2,0},{3,1},{4,6},{5,7},{6,4},{7,5},{8,10},{9,11},{10,... | collective-permute-start | bytes 1769480 | tf_op jit(solution)/shard_map/ppermute | solution.py:41
  37.4 90.2 %conditional.3 = (bf16[4,192,256]{2,1,0:T(8,128)(2,1)}, f32[192,1024]{1,0:T(8,128)S(1)}, f32[8,1024]{1,0:T(8,128)S(1)}, f32[192,1024]{1,0:T(8,128)S(1)}, f32[16,1024]{1,0:T(8,128)S(1)}) conditional(s32[]{:T(128)} %convert_element_type.4, () %tuple.25, (bf16[4,192,256]{2,1,0:T(8,128)(2,1)}, bf16[16,32,128]{2,1,0:T(8,128)(2,1)}, ...), branch_computations={%region_2.0_spmd, %region_3.0_spmd} | conditional | flops 1 | bytes 7078073 | solution.py:417
  37.5 4.1 %all-to-all-start.1 = ((bf16[4,192,256]{2,1,0:T(8,128)(2,1)}), bf16[4,192,256]{2,1,0:T(8,128)(2,1)}, u32[]{:S(2)}, u32[]{:S(2)}) async-start(bf16[4,192,256]{2,1,0:T(8,128)(2,1)} %get-tuple-element.21), calls=%async_computation.1 | async-start | bytes 786432 | tf_op jit(solution)/shard_map/cond/branch_1_fun/all_to_all | solution.py:402
  41.6 4.6 %collective-permute-start = (bf16[3072,128]{1,0:T(8,128)(2,1)}, bf16[3072,128]{1,0:T(8,128)(2,1)S(1)}, u32[]{:S(2)}, u32[]{:S(2)}) collective-permute-start(bf16[3072,128]{1,0:T(8,128)(2,1)} %get-tuple-element.25.refs_0_), channel_id=1, source_target_pairs={{0,1},{1,0},{2,3},{3,2},{4,5},{5,4},{6,7},{7,6},{8,9},{9,8},{10,11... | collective-permute-start | bytes 2359304 | tf_op jit(solution)/shard_map/cond/branch_1_fun/ppermute | solution.py:41
  46.2 1.6 %all-to-all-done.1.q_ref = bf16[4,192,256]{2,1,0:T(8,128)(2,1)} async-done(((bf16[4,192,256]{2,1,0:T(8,128)(2,1)}), bf16[4,192,256]{2,1,0:T(8,128)(2,1)}, u32[]{:S(2)}, u32[]{:S(2)}) %all-to-all-start.1) | async-done | bytes 393248 | tf_op jit(solution)/shard_map/cond/branch_1_fun/all_to_all | solution.py:402
  47.9 14.8 %all-to-all-start.2 = ((bf16[16,32,128]{2,1,0:T(8,128)(2,1)}), bf16[16,32,128]{2,1,0:T(8,128)(2,1)S(1)}, u32[]{:S(2)}, u32[]{:S(2)}) async-start(bf16[16,32,128]{2,1,0:T(8,128)(2,1)} %get-tuple-element.24), calls=%async_computation.2 | async-start | bytes 262144 | tf_op jit(solution)/shard_map/cond/branch_1_fun/all_to_all | solution.py:404
  62.7 5.3 %collective-permute-start.1 = (bf16[768,128]{1,0:T(8,128)(2,1)S(1)}, bf16[768,128]{1,0:T(8,128)(2,1)S(1)}, u32[]{:S(2)}, u32[]{:S(2)}) collective-permute-start(bf16[768,128]{1,0:T(8,128)(2,1)S(1)} %get-tuple-element.26.refs_2_), channel_id=1, source_target_pairs={{0,1},{1,0},{2,3},{3,2},{4,5},{5,4},{6,7},{7,6},{8,9},{9,8},{10,11... | collective-permute-start | bytes 589832 | tf_op jit(solution)/shard_map/cond/branch_1_fun/ppermute | solution.py:41
  68.0 1.0 collective-permute-done.1.refs_3_
  69.1 0.0 collective-permute-done.refs_1_
  69.1 13.0 %near.2 = (f32[192,1024]{1,0:T(8,128)S(1)}, f32[8,1024]{1,0:T(8,128)S(1)}) custom-call(bf16[4,192,256]{2,1,0:T(8,128)(2,1)} %all-to-all-done.1.q_ref, bf16[3072,128]{1,0:T(8,128)(2,1)} %get-tuple-element.25.refs_0_, bf16[3072,128]{1,0:T(8,128)(2,1)S(1)} %collective-permute-done.refs_1_, bf16[768,128]{1,0:T(8,128)(2,1)S(1)} %get-tuple-element.26.refs_2_, ...), custom_call_target="tpu_custom_call" | custom-call | tf_op jit(solution)/shard_map/cond/branch_1_fun/near/pallas_call | solution.py:282
  82.1 22.2 %all-to-all-done.2.rows_ref = bf16[16,32,128]{2,1,0:T(8,128)(2,1)S(1)} async-done(((bf16[16,32,128]{2,1,0:T(8,128)(2,1)}), bf16[16,32,128]{2,1,0:T(8,128)(2,1)S(1)}, u32[]{:S(2)}, u32[]{:S(2)}) %all-to-all-start.2) | async-done | bytes 131104 | tf_op jit(solution)/shard_map/cond/branch_1_fun/all_to_all | solution.py:404
  104.3 0.1 spread.1
  104.4 20.4 %all_to_all.22.rows_ref = bf16[32,96,128]{2,1,0:T(8,128)(2,1)S(1)} all-to-all(bf16[32,96,128]{2,1,0:T(8,128)(2,1)S(1)} %spread.1), channel_id=1, replica_groups=mesh['zl'=8,'x'=4,'y'=4,'zh'=2,'core'=2] {'x','y','core'}, dimensions={0} | all-to-all | bytes 1572864 | tf_op jit(solution)/shard_map/cond/branch_1_fun/all_to_all | solution.py:409
  124.8 2.8 %far.1 = (f32[192,1024]{1,0:T(8,128)S(1)}, f32[16,1024]{1,0:T(8,128)S(1)}) custom-call(s32[1]{0:T(128)} %get-tuple-element.31.y_ref, bf16[4,192,256]{2,1,0:T(8,128)(2,1)} %all-to-all-done.1.q_ref, bf16[32,96,128]{2,1,0:T(8,128)(2,1)S(1)} %all_to_all.22.rows_ref), custom_call_target="tpu_custom_call" | custom-call | tf_op jit(solution)/shard_map/cond/branch_1_fun/far/pallas_call | solution.py:369
  127.6 0.0 collective-permute-done.3.refs_0_
  127.6 2.1 %collective-permute-start.4 = (bf16[2304,128]{1,0:T(8,128)(2,1)S(1)}, bf16[2304,128]{1,0:T(8,128)(2,1)S(1)}, u32[]{:S(2)}, u32[]{:S(2)}) collective-permute-start(bf16[2304,128]{1,0:T(8,128)(2,1)S(1)} %collective-permute-done.3.refs_0_), channel_id=1, source_target_pairs={{0,1},{1,0},{2,3},{3,2},{4,5},{5,4},{6,7},{7,6},{8,9},{9,8},{10,11... | collective-permute-start | bytes 1769480 | tf_op jit(solution)/shard_map/ppermute | solution.py:41
  129.7 5.2 %near.3 = (f32[192,1024]{1,0:T(8,128)S(1)}, f32[8,1024]{1,0:T(8,128)S(1)}) custom-call(bf16[4,192,256]{2,1,0:T(8,128)(2,1)} %get-tuple-element.62.q_ref, bf16[2304,128]{1,0:T(8,128)(2,1)S(1)} %collective-permute-done.3.refs_0_, f32[192,1024]{1,0:T(8,128)S(1)} %get-tuple-element.69.refs_1_, f32[8,1024]{1,0:T(8,128)S(1)} %get-tuple-element.70.refs_2_), custom_call_target="tpu_custom_call" | custom-call | tf_op jit(solution)/shard_map/near/pallas_call | solution.py:282
  134.9 0.0 collective-permute-done.4.refs_0_
  135.0 4.9 %last.1 = bf16[4,192,256]{2,1,0:T(8,128)(2,1)S(1)} custom-call(bf16[4,192,256]{2,1,0:T(8,128)(2,1)} %get-tuple-element.62.q_ref, bf16[2304,128]{1,0:T(8,128)(2,1)S(1)} %collective-permute-done.4.refs_0_, f32[192,1024]{1,0:T(8,128)S(1)} %get-tuple-element.71.refs_1_, f32[8,1024]{1,0:T(8,128)S(1)} %get-tuple-element.72.refs_2_, ...), custom_call_target="tpu_custom_call" | custom-call | tf_op jit(solution)/shard_map/last/pallas_call | solution.py:282
  139.9 10.3 %all_to_all.23 = bf16[4,192,256]{2,1,0:T(8,128)(2,1)S(1)} all-to-all(bf16[4,192,256]{2,1,0:T(8,128)(2,1)S(1)} %last.1), channel_id=1, replica_groups=mesh['zl'=8,'x'=4,'y'=4,'zh'=2,'core'=2] {'y'}, dimensions={0} | all-to-all | bytes 786432 | tf_op jit(solution)/shard_map/all_to_all | solution.py:435
  150.3 0.9 turn.1
Async XLA Ops:
  2.4 33.2 %collective-permute-start.2 = (bf16[768,128]{1,0:T(8,128)(2,1)S(1)}, bf16[768,128]{1,0:T(8,128)(2,1)S(1)}, u32[]{:S(2)}, u32[]{:S(2)}) collective-permute-start(bf16[768,128]{1,0:T(8,128)(2,1)S(1)} %get-tuple-element.60), channel_id=1, source_target_pairs={{0,2},{1,3},{2,0},{3,1},{4,6},{5,7},{6,4},{7,5},{8,10},{9,11},{10,... | collective-permute-start | bytes 589832 | tf_op jit(solution)/shard_map/ppermute | solution.py:41
  35.5 92.1 %collective-permute-start.3 = (bf16[2304,128]{1,0:T(8,128)(2,1)}, bf16[2304,128]{1,0:T(8,128)(2,1)S(1)}, u32[]{:S(2)}, u32[]{:S(2)}) collective-permute-start(bf16[2304,128]{1,0:T(8,128)(2,1)} %get-tuple-element.63), channel_id=1, source_target_pairs={{0,2},{1,3},{2,0},{3,1},{4,6},{5,7},{6,4},{7,5},{8,10},{9,11},{10,... | collective-permute-start | bytes 1769480 | tf_op jit(solution)/shard_map/ppermute | solution.py:41
  37.5 10.4 %all-to-all-start.1 = ((bf16[4,192,256]{2,1,0:T(8,128)(2,1)}), bf16[4,192,256]{2,1,0:T(8,128)(2,1)}, u32[]{:S(2)}, u32[]{:S(2)}) async-start(bf16[4,192,256]{2,1,0:T(8,128)(2,1)} %get-tuple-element.21), calls=%async_computation.1 | async-start | bytes 786432 | tf_op jit(solution)/shard_map/cond/branch_1_fun/all_to_all | solution.py:402
  41.6 27.5 %collective-permute-start = (bf16[3072,128]{1,0:T(8,128)(2,1)}, bf16[3072,128]{1,0:T(8,128)(2,1)S(1)}, u32[]{:S(2)}, u32[]{:S(2)}) collective-permute-start(bf16[3072,128]{1,0:T(8,128)(2,1)} %get-tuple-element.25.refs_0_), channel_id=1, source_target_pairs={{0,1},{1,0},{2,3},{3,2},{4,5},{5,4},{6,7},{7,6},{8,9},{9,8},{10,11... | collective-permute-start | bytes 2359304 | tf_op jit(solution)/shard_map/cond/branch_1_fun/ppermute | solution.py:41
  47.9 56.4 %all-to-all-start.2 = ((bf16[16,32,128]{2,1,0:T(8,128)(2,1)}), bf16[16,32,128]{2,1,0:T(8,128)(2,1)S(1)}, u32[]{:S(2)}, u32[]{:S(2)}) async-start(bf16[16,32,128]{2,1,0:T(8,128)(2,1)} %get-tuple-element.24), calls=%async_computation.2 | async-start | bytes 262144 | tf_op jit(solution)/shard_map/cond/branch_1_fun/all_to_all | solution.py:404
  62.7 6.4 %collective-permute-start.1 = (bf16[768,128]{1,0:T(8,128)(2,1)S(1)}, bf16[768,128]{1,0:T(8,128)(2,1)S(1)}, u32[]{:S(2)}, u32[]{:S(2)}) collective-permute-start(bf16[768,128]{1,0:T(8,128)(2,1)S(1)} %get-tuple-element.26.refs_2_), channel_id=1, source_target_pairs={{0,1},{1,0},{2,3},{3,2},{4,5},{5,4},{6,7},{7,6},{8,9},{9,8},{10,11... | collective-permute-start | bytes 589832 | tf_op jit(solution)/shard_map/cond/branch_1_fun/ppermute | solution.py:41
  127.6 7.3 %collective-permute-start.4 = (bf16[2304,128]{1,0:T(8,128)(2,1)S(1)}, bf16[2304,128]{1,0:T(8,128)(2,1)S(1)}, u32[]{:S(2)}, u32[]{:S(2)}) collective-permute-start(bf16[2304,128]{1,0:T(8,128)(2,1)S(1)} %collective-permute-done.3.refs_0_), channel_id=1, source_target_pairs={{0,1},{1,0},{2,3},{3,2},{4,5},{5,4},{6,7},{7,6},{8,9},{9,8},{10,11... | collective-permute-start | bytes 1769480 | tf_op jit(solution)/shard_map/ppermute | solution.py:41
